TPU v7x, 32 devices: a whole 2x2x4 slice. The times are simulated.
32 devices in a mesh: dp: 2 (over y), owner: 4 (over z), context: 4 (over x, core).
Axes of the slice: x: 2, y: 2, z: 4, core: 2. Of those that a mesh axis runs over, the one named last changes fastest.
Arguments:
- grad_partials: bfloat16 [8, 1536, 32, 192], P(('dp', 'context'), None, 'owner')
- assignment: int32 [32, 1], replicated, may hold values from 0 to 3; in each aligned block of 8 rows (0 to 7, 8 to 15, ...) at most 2 rows name the same one
- momentum: float32 [32, 1536, 192], P('owner', ('dp', 'context')), may hold values from -6 to 6
- q_weight: float32 [32, 1536, 192], P('owner', ('dp', 'context')), may hold values from -1.2 to 1.2
- k_weight: float32 [32, 512, 128], P('owner', ('dp', 'context')), may hold values from -6 to 6
- max_logits: float32 [4, 32], P('context'), may hold values from 20 to 400
Outputs:
- momentum_out: float32 [32, 1536, 192], P('owner', ('dp', 'context'))
- q_weight_out: float32 [32, 1536, 192], P('owner', ('dp', 'context'))
- k_weight_out: float32 [32, 512, 128], P('owner', ('dp', 'context'))
Inputs may be any that keep to these rules, and one draw needn't show every extreme that they name: `assignment`: in each aligned block of 8 heads no owner index is named more than 2 times, and some owner index exactly 2 times.
All inputs are finite; a program needn't handle non-finite values.
Results may differ from a plain program's by a relative error of at most 0.0007.
Values may be sent and summed in bfloat16 or wider, within the bound.
No kernel may reach another device: no remote copies, remote signals or barrier semaphores. Data moves between devices by JAX's collectives and lax.ppermute only.
A program may use at most 128 MiB of HBM per device.

v0:
```python
import math

import jax
import jax.numpy as jnp
from jax import lax
from jax.sharding import PartitionSpec as P

QR = 1536
QK = 192
ITERS = 2


MOMENTUM_RATE = 0.95
WEIGHT_KEEP = 0.98
LOGIT_CAP = 100.0
QUINTIC_A = 3.4445
QUINTIC_B = -4.775
QUINTIC_C = 2.0315


def routing(assignment, heads_own, per_source):
    target = assignment[:, 0]
    head_index = jnp.arange(target.shape[0], dtype=jnp.int32)
    source_block = head_index // heads_own
    earlier = (
        (source_block[None, :] == source_block[:, None])
        & (head_index[None, :] < head_index[:, None])
        & (target[None, :] == target[:, None])
    )
    position = jnp.sum(earlier.astype(jnp.int32), axis=1)
    return (target, position, source_block * per_source + position)


def refresh(weight, orthogonal, gamma, kn_count):
    step_size = 0.04 * math.sqrt(max(QR, QK))
    column_index = jnp.arange(weight.shape[2])
    column_scale = jnp.where(
        column_index[None, :] < kn_count, jnp.sqrt(gamma)[:, None], gamma[:, None]
    )
    return (WEIGHT_KEEP * weight - step_size * orthogonal.astype(jnp.float32)) * column_scale[
        :, None, :
    ]


def quintic(whole):
    for step in range(ITERS):
        gram_matrix = jnp.einsum("nrk,nrl->nkl", whole, whole, preferred_element_type=jnp.float32)
        polynomial = (
            QUINTIC_B * gram_matrix
            + QUINTIC_C
            * jnp.einsum("nkl,nlm->nkm", gram_matrix, gram_matrix, precision=lax.Precision.HIGHEST)
        ).astype(jnp.bfloat16)
        whole = (
            QUINTIC_A * whole.astype(jnp.float32)
            + jnp.einsum("nrk,nkl->nrl", whole, polynomial, preferred_element_type=jnp.float32)
        ).astype(jnp.bfloat16)
    return whole


def orthogonalize(matrix):
    square_sum = lax.psum(jnp.sum(matrix * matrix, axis=(1, 2)), ("dp", "context"))
    iterate = (matrix / (jnp.sqrt(square_sum) + 1e-07)[:, None, None]).astype(jnp.bfloat16)
    row_count = matrix.shape[1]
    gathered = lax.all_gather(iterate, ("dp", "context"), axis=1, tiled=True)
    gathered = quintic(gathered)
    return lax.dynamic_slice_in_dim(
        gathered, lax.axis_index(("dp", "context")) * row_count, row_count, 1
    )


def body(grad_partials, assignment, momentum, q_weight, k_weight, max_logits):
    heads_own = grad_partials.shape[2]
    slots_own = momentum.shape[0]
    kn_count = k_weight.shape[2]
    per_source = slots_own // lax.axis_size("owner")
    my_owner = lax.axis_index("owner")
    target, position, local_slot = routing(assignment, heads_own, per_source)
    peak_logit = lax.pmax(max_logits[0], "context")
    gamma = jnp.minimum(1.0, LOGIT_CAP / peak_logit)
    partial_value = grad_partials[0]
    grad_rows = lax.psum_scatter(
        partial_value.astype(jnp.float32), ("dp", "context"), scatter_dimension=0, tiled=True
    )
    home_target = lax.dynamic_slice_in_dim(target, my_owner * heads_own, heads_own)
    home_position = lax.dynamic_slice_in_dim(position, my_owner * heads_own, heads_own)
    send_index = home_target * per_source + home_position
    slot_index = jnp.arange(slots_own, dtype=jnp.int32)
    sender = (slot_index[:, None] == send_index[None, :]).astype(jnp.float32)
    owned_mask = (
        (target[None, :] == my_owner) & (local_slot[None, :] == slot_index[:, None])
    ).astype(jnp.float32)
    occupied = (jnp.sum(owned_mask, axis=1) > 0.5)[:, None, None]
    home_gamma = lax.dynamic_slice_in_dim(gamma, my_owner * heads_own, heads_own)
    outgoing = jnp.einsum("qi,rik->qrk", sender, grad_rows, precision=lax.Precision.HIGHEST)
    arrived = lax.all_to_all(outgoing, "owner", split_axis=0, concat_axis=0, tiled=True)
    refreshed = jnp.where(occupied, MOMENTUM_RATE * momentum + arrived, momentum)
    orthogonal = orthogonalize(refreshed)
    slot_gamma = jnp.sum(owned_mask * gamma[None, :], axis=1)
    slot_gamma = jnp.where(occupied[:, 0, 0], slot_gamma, 1.0)
    q_weight_out = jnp.where(
        occupied, refresh(q_weight, orthogonal, slot_gamma, kn_count), q_weight
    )
    k_weight_out = k_weight * jnp.sqrt(home_gamma)[:, None, None]
    return (refreshed, q_weight_out, k_weight_out)


def solution(mesh):
    placed = (
        P(("dp", "context"), None, "owner", None),
        P(),
        P("owner", ("dp", "context"), None),
        P("owner", ("dp", "context"), None),
        P("owner", ("dp", "context"), None),
        P("context", None),
    )
    return jax.shard_map(
        body,
        mesh=mesh,
        in_specs=placed,
        out_specs=(
            P("owner", ("dp", "context"), None),
            P("owner", ("dp", "context"), None),
            P("owner", ("dp", "context"), None),
        ),
        check_vma=False,
    )
```

profile of v0, /device:TPU:0, one launch (start us, length us, event | category | flops | bytes accessed | tf_op | source)
XLA Modules:
  0.0 242.7 jit_solution(5322479201671485981)
XLA Ops:
  7.2 0.0 reduce-scatter.4.cloned.1.call-start
  7.2 7.3 %bitcast_convert_fusion = f32[1536,1536]{0,1:T(8,128)} fusion(bf16[1,1536,8,192]{1,3,2,0:T(8,128)(2,1)} %param.6), kind=kLoop, calls=%fused_computation.1 | loop fusion | flops 2359296 | bytes 14155776
  14.5 9.6 %copy.61 = f32[1536,1536]{1,0:T(8,128)} copy(f32[1536,1536]{0,1:T(8,128)} %bitcast_convert_fusion) | data formatting | bytes 18874368
  24.2 0.0 copy-start.2
  24.2 0.0 reduce-scatter.4.cloned.1.call-update
  24.2 0.6 copy-done.2
  24.8 0.2 convert_reduce_fusion
  25.0 0.1 fusion.10
  25.1 78.4 %reduce-scatter.4.cloned.1.call-done = f32[192,1536]{1,0:T(8,128)} async-done(((f32[1536,1536]{1,0:T(8,128)}), f32[192,1536]{1,0:T(8,128)}) %reduce-scatter.4.cloned.1.call-update) | async-done | bytes 1179664
  103.5 1.7 copy.62
  105.3 0.8 copy.42
  106.1 0.8 fusion.5
  106.9 1.6 copy.43
  108.5 4.6 %all-to-all-start = ((f32[8,192,192]{2,1,0:T(8,128)}), f32[8,192,192]{2,1,0:T(8,128)S(1)}, u32[]{:S(2)}, u32[]{:S(2)}) async-start(f32[8,192,192]{2,1,0:T(8,128)} %copy.43), calls=%async_computation | async-start | bytes 3145728 | tf_op jit(solution)/shard_map/all_to_all | solution.py:95
  113.1 0.0 copy-start.3
  113.1 0.0 all-gather.2.cloned.1.call-start
  113.1 2.0 copy.41
  115.1 0.0 copy-done.3
  115.2 6.5 %pmax.7 = f32[32]{0:T(128)S(1)} all-reduce(f32[32]{0:T(128)S(1)} %bitcast.33), channel_id=1, replica_groups=mesh['dp'=2,'owner'=4,'context'=4] {'context'}, use_global_device_ids=true, to_apply=%region_5.6 | all-reduce | flops 32 | bytes 256 | tf_op jit(solution)/shard_map/pmax | solution.py:78
  121.6 0.1 select_reduce_fusion
  121.8 28.3 %all-to-all-done = f32[8,192,192]{2,1,0:T(8,128)S(1)} async-done(((f32[8,192,192]{2,1,0:T(8,128)}), f32[8,192,192]{2,1,0:T(8,128)S(1)}, u32[]{:S(2)}, u32[]{:S(2)}) %all-to-all-start) | async-done | bytes 1179680 | tf_op jit(solution)/shard_map/all_to_all | solution.py:95
  150.1 1.7 copy.44
  151.8 1.8 multiply_reduce_fusion
  153.7 12.1 %psum.7 = f32[8]{0:T(128)S(1)} all-reduce(f32[8]{0:T(128)S(1)} %get-tuple-element.16), channel_id=1, replica_groups=mesh['dp'=2,'owner'=4,'context'=4] {'dp','context'}, use_global_device_ids=true, to_apply=%region_4.5 | all-reduce | flops 8 | bytes 64 | tf_op jit(solution)/shard_map/psum | solution.py:61
  165.8 0.2 divide_convert_fusion
  166.0 1.5 copy.47
  167.5 0.0 all-gather.2.cloned.1.call-update
  167.5 0.0 copy-start.1
  167.5 2.0 copy.46
  169.6 0.1 dynamic-slice_sqrt_fusion
  169.7 0.1 broadcast_select_fusion
  169.8 0.0 copy-done.1
  169.8 0.8 broadcast_multiply_fusion
  170.6 1.7 copy.55
  172.3 38.8 %all-gather.2.cloned.1.call-done = bf16[8,1536,192]{2,0,1:T(8,128)(2,1)} async-done(((bf16[8,192,192]{2,0,1:T(8,128)(2,1)}), bf16[8,1536,192]{2,0,1:T(8,128)(2,1)}) %all-gather.2.cloned.1.call-update) | async-done | bytes 4718608 | tf_op jit(solution)/shard_map/all_gather | solution.py:64
  211.1 8.7 %copy.48 = bf16[8,1536,192]{1,2,0:T(8,128)(2,1)} copy(bf16[8,1536,192]{2,0,1:T(8,128)(2,1)} %all-gather.2.cloned.1.call-done) | data formatting | bytes 9437184 | tf_op jit(solution)/shard_map/all_gather | solution.py:64
  219.8 0.0 copy-start
  219.8 5.3 %fusion.12 = f32[8,192,192]{2,1,0:T(8,128)S(1)} fusion(bf16[8,1536,192]{1,2,0:T(8,128)(2,1)} %copy.48), kind=kOutput, calls=%fused_computation.41 | convolution fusion | flops 905969664 | bytes 5898240 | tf_op jit(solution)/shard_map/nrk,nrl->nkl/dot_general | solution.py:47
  225.1 1.8 add_convert_fusion.2
  226.9 0.0 copy-done
  226.9 1.6 add_convert_fusion
  228.5 1.4 fusion.13
  229.9 1.8 add_convert_fusion.1
  231.7 1.4 fusion.14
  233.1 1.0 multiply_select_fusion
  234.1 1.7 copy.56
  (8 shorter events, 0.0 us)
Async XLA Ops:
  7.2 96.3 %reduce-scatter.4.cloned.1.call-start = ((), (), s32[]{:S(2)}) async-start(), calls=%async_computation.3 | async-start | bytes 10616832
  24.2 0.7 copy-start.2
  108.5 41.6 %all-to-all-start = ((f32[8,192,192]{2,1,0:T(8,128)}), f32[8,192,192]{2,1,0:T(8,128)S(1)}, u32[]{:S(2)}, u32[]{:S(2)}) async-start(f32[8,192,192]{2,1,0:T(8,128)} %copy.43), calls=%async_computation | async-start | bytes 3145728 | tf_op jit(solution)/shard_map/all_to_all | solution.py:95
  113.1 2.0 copy-start.3
  113.1 98.0 %all-gather.2.cloned.1.call-start = ((), (), s32[]{:S(2)}) async-start(), calls=%async_computation.2 | async-start | bytes 7077888 | tf_op jit(solution)/shard_map/all_gather | solution.py:64
  167.5 2.2 copy-start.1
  219.8 7.1 %copy-start = (bf16[8,1536,192]{1,2,0:T(8,128)(2,1)S(1)}, bf16[8,1536,192]{1,2,0:T(8,128)(2,1)}, u32[]{:S(2)}) copy-start(bf16[8,1536,192]{1,2,0:T(8,128)(2,1)} %copy.48) | copy-start | bytes 14155780
Sparse Core Ops, SparseCore 0:
  24.3 79.1 reduce-scatter.3
  167.6 43.4 all-gather.1
where the time goes:
time: 243 us
  waiting for transfers between devices  146 us (60%)
  local copies, waits for them, and re-layouts  34 us (14%)
  blocking collectives  18.5 us (8%)
  between operations  14.2 us (6%)
  matrix products  14.1 us (6%)
  other arithmetic  11.7 us (5%)
  starting transfers between devices  4.65 us (2%)
    unnamed x3, waiting for transfers between devices  78.5 us
    all_gather x1, waiting for transfers between devices, orthogonalize(): gathered = lax.all_gather(iterate, ('dp', 'context'), axis=1, tiled=True)  38.8 us
    all_to_all x1, waiting for transfers between devices, body(): lax.all_to_all(outgoing, 'owner', split_axis=0, concat_axis=0, tiled=True)  28.3 us
    unnamed x14, local copies, waits for them, and re-layouts  19.5 us
    psum x1, blocking collectives, orthogonalize(): lax.psum(jnp.sum(matrix * matrix, axis=(1, 2)), ('dp', 'context'))  12.1 us
    all_gather x1, local copies, waits for them, and re-layouts, orthogonalize(): gathered = lax.all_gather(iterate, ('dp', 'context'), axis=1, tiled=True)  8.7 us
    unnamed x1, other arithmetic  7.32 us
    dot_general x2, matrix products, quintic(): jnp.einsum('nrk,nrl->nkl', whole, whole, preferred_element_type=jnp.float32)  6.69 us
  transfers between devices with their start and end apart: 3, of which 3 were waited for; matrix products, arithmetic and copies ran while one was open for 3% of the time, Pallas kernels for 0%

commit v1 on v0

v1 whole, which is shorter than its diff:
```python
import functools
import math

import jax
import jax.numpy as jnp
from jax import lax
from jax.experimental import pallas as pl
from jax.experimental.pallas import tpu as pltpu
from jax.sharding import PartitionSpec as P

ITERS = 2
MOMENTUM_RATE = 0.95
WEIGHT_KEEP = 0.98
LOGIT_CAP = 100.0
QUINTIC_A = 3.4445
QUINTIC_B = -4.775
QUINTIC_C = 2.0315

CORES = 2
PLANE = ("dp", "context")
SCALE_ROWS = 16
LEVELS = 14.99
STEPS = 8.0
CHUNKS = 2

SMEM = pl.BlockSpec(memory_space=pltpu.SMEM)
VMEM = pl.BlockSpec(memory_space=pltpu.VMEM)
PARAMS = pltpu.CompilerParams(vmem_limit_bytes=48 * 1024 * 1024)


def encode(values, out):
    top = jnp.max(jnp.abs(values), axis=0, keepdims=True)
    level = jnp.clip(jnp.ceil(STEPS * jnp.log2(top)), -100.0 * STEPS, 128.0 * STEPS)
    scaled = values * jnp.exp2(LEVELS - level * (1.0 / STEPS))
    count = values.shape[0]
    out[:count] = jnp.round(scaled).astype(jnp.int32).astype(jnp.int16)
    rows = jnp.broadcast_to(level, (SCALE_ROWS, values.shape[1]))
    out[count:] = rows.astype(jnp.int32).astype(jnp.int16)


def decode(block):
    count = block.shape[0] - SCALE_ROWS
    level = block[count : count + SCALE_ROWS].astype(jnp.int32).astype(jnp.float32)[0:1]
    return block[:count].astype(jnp.int32).astype(jnp.float32) * jnp.exp2(
        level * (1.0 / STEPS) - LEVELS
    )


def pair_kernel(chips, aligned, index, own, sibling, here, *away):
    width = here.shape[-1]
    for k in range(chips):
        chip = index[0] ^ k
        if aligned:
            rows = pl.ds(pl.multiple_of(chip * width, 128), width)
            first, second = own[0, :, rows], sibling[0, :, rows]
        else:
            first, second = own[0, chip], sibling[0, chip]
        total = first.astype(jnp.float32) + second.astype(jnp.float32)
        if k == 0:
            here[0] = total
        else:
            encode(total, away[k - 1].at[0])


def pair_sums(g, sibling, heads, chip, chips):
    count, cols = sibling.shape[0], sibling.shape[1 if sibling.ndim == 3 else 2]
    aligned = sibling.ndim == 3
    width = sibling.shape[2] // chips if aligned else sibling.shape[3]
    block = (1,) + sibling.shape[1:]
    zeros = (0,) * (sibling.ndim - 1)
    coded = jax.ShapeDtypeStruct((count, cols + SCALE_ROWS, width), jnp.int16)
    return pl.pallas_call(
        functools.partial(pair_kernel, chips, aligned),
        grid_spec=pltpu.PrefetchScalarGridSpec(
            num_scalar_prefetch=1,
            grid=(count,),
            in_specs=[
                pl.BlockSpec(block, lambda i, index: (index[i + 1],) + zeros),
                pl.BlockSpec(block, lambda i, index: (i,) + zeros),
            ],
            out_specs=[pl.BlockSpec((1, cols, width), lambda i, index: (i, 0, 0))]
            + [pl.BlockSpec((1, cols + SCALE_ROWS, width), lambda i, index: (i, 0, 0))]
            * (chips - 1),
        ),
        out_shape=[jax.ShapeDtypeStruct((count, cols, width), jnp.float32)] + [coded] * (chips - 1),
        compiler_params=PARAMS,
        name="pair_sum",
    )(jnp.concatenate([chip[None], heads]).astype(jnp.int32), g, sibling)


def plane_kernel(plain, here, *refs):
    count = here.shape[0]
    away, outs = refs[: len(refs) - count], refs[len(refs) - count :]
    for i in range(count):
        total = here[i]
        for block in away:
            total = total + decode(block[i])
        if plain[i]:
            outs[i][...] = total
        else:
            encode(total, outs[i])


def plane_sums(here, away, plain):
    count, cols, width = here.shape
    coded = jax.ShapeDtypeStruct((cols + SCALE_ROWS, width), jnp.int16)
    whole = jax.ShapeDtypeStruct((cols, width), jnp.float32)
    return pl.pallas_call(
        functools.partial(plane_kernel, plain),
        in_specs=[VMEM] * (1 + len(away)),
        out_specs=[VMEM] * count,
        out_shape=[whole if p else coded for p in plain],
        compiler_params=PARAMS,
        name="plane_sum",
    )(here, *away)


def turn_kernel(index, own, sibling, out, both):
    core = index[0]
    rows = own.shape[1]
    for s in range(sibling.shape[0]):
        both[pl.ds(pl.multiple_of(core * rows, 16), rows)] = own[s * CORES + core]
        both[pl.ds(pl.multiple_of((1 - core) * rows, 16), rows)] = sibling[s]
        out[s] = both[...].T


def turn(index, own, sibling):
    sources, rows, cols = sibling.shape
    return pl.pallas_call(
        turn_kernel,
        in_specs=[SMEM, VMEM, VMEM],
        out_specs=VMEM,
        out_shape=jax.ShapeDtypeStruct((sources, cols, CORES * rows), jnp.float32),
        scratch_shapes=[pltpu.VMEM((CORES * rows, cols), jnp.float32)],
        compiler_params=PARAMS,
        name="turn_momentum",
    )(index, own, sibling)


def refresh_kernel(chips, index, occupied, old, near, *refs):
    sources = old.shape[0]
    arrived, (new, here), away = refs[: sources - 1], refs[sources - 1 : sources + 1], refs[sources + 1 :]
    core, chip, owner = index[0], index[1], index[2]
    for k in range(sources):
        source = owner ^ k
        grad = near[...] if k == 0 else decode(arrived[k - 1])
        kept = old[source]
        mask = occupied[source * CORES + core] > 0
        new[source] = jnp.where(mask, MOMENTUM_RATE * kept + grad, kept)
    for k in range(chips):
        value = new[lax.rem(chip ^ k, sources)]
        if k == 0:
            here[...] = value
        else:
            encode(value, away[k - 1])


def refreshed_rows(index, occupied, old, near, arrived, chips):
    _, cols, width = old.shape
    coded = jax.ShapeDtypeStruct((cols + SCALE_ROWS, width), jnp.int16)
    return pl.pallas_call(
        functools.partial(refresh_kernel, chips),
        in_specs=[SMEM, SMEM] + [VMEM] * (2 + len(arrived)),
        out_specs=[VMEM] * (1 + chips),
        out_shape=[
            jax.ShapeDtypeStruct(old.shape, jnp.float32),
            jax.ShapeDtypeStruct((cols, width), jnp.float32),
        ]
        + [coded] * (chips - 1),
        compiler_params=PARAMS,
        name="refresh_momentum",
    )(index, occupied, old, near, *arrived)


def back_kernel(index, new, own, sibling, both):
    core = index[0]
    rows = own.shape[1]
    for s in range(own.shape[0]):
        both[...] = new[s].T
        own[s] = both[pl.ds(pl.multiple_of(core * rows, 16), rows)]
        sibling[s] = both[pl.ds(pl.multiple_of((1 - core) * rows, 16), rows)]


def turn_back(index, new):
    sources, cols, width = new.shape
    half = jax.ShapeDtypeStruct((sources, width // CORES, cols), jnp.float32)
    return pl.pallas_call(
        back_kernel,
        in_specs=[SMEM, VMEM],
        out_specs=[VMEM, VMEM],
        out_shape=[half, half],
        scratch_shapes=[pltpu.VMEM((width, cols), jnp.float32)],
        compiler_params=PARAMS,
        name="turn_back",
    )(index, new)


def merge_kernel(index, own, sibling, out):
    core = index[0]
    for s in range(own.shape[0]):
        out[s * CORES + core] = own[s]
        out[s * CORES + 1 - core] = sibling[s]


def merge(index, own, sibling):
    sources, rows, cols = own.shape
    return pl.pallas_call(
        merge_kernel,
        in_specs=[SMEM, VMEM, VMEM],
        out_specs=VMEM,
        out_shape=jax.ShapeDtypeStruct((sources * CORES, rows, cols), jnp.float32),
        compiler_params=PARAMS,
        name="merge_momentum",
    )(index, own, sibling)


def fold_rows(rows):
    return 2 if rows % 32 == 0 else 1


def newton_kernel(chips, index, here, *refs):
    away, outs, (matrix, turned) = refs[: chips - 1], refs[chips - 1 : -2], refs[-2:]
    cols, width = here.shape
    matrix[:, :width] = here[...]
    for k in range(1, chips):
        matrix[:, k * width : (k + 1) * width] = decode(away[k - 1])
    value = matrix[...]
    norm = jnp.sqrt(jnp.sum(value * value)) + 1e-07
    iterate = (value / norm).astype(jnp.bfloat16)
    for _ in range(ITERS):
        gram = lax.dot_general(
            iterate, iterate, (((1,), (1,)), ((), ())), preferred_element_type=jnp.float32
        )
        square = lax.dot_general(
            gram, gram, (((1,), (0,)), ((), ())), precision=lax.Precision.HIGHEST,
            preferred_element_type=jnp.float32,
        )
        polynomial = (QUINTIC_B * gram + QUINTIC_C * square).T.astype(jnp.bfloat16)
        product = lax.dot_general(
            polynomial, iterate, (((1,), (0,)), ((), ())), preferred_element_type=jnp.float32
        )
        iterate = (QUINTIC_A * iterate.astype(jnp.float32) + product).astype(jnp.bfloat16)
    matrix[...] = iterate.astype(jnp.float32)
    core = index[0]
    rows = width // CORES
    fold = fold_rows(rows)
    for k in range(chips):
        turned[...] = matrix[:, k * width : (k + 1) * width].T
        for c in range(CORES):
            out = outs[k * CORES + c]
            for f in range(fold):
                first = (core ^ c) * rows + f * (rows // fold)
                part = turned[pl.ds(pl.multiple_of(first, 8), rows // fold)]
                out[:, f * cols : (f + 1) * cols] = part.astype(jnp.bfloat16)


def newton(index, here, away):
    cols, width = here.shape
    chips = len(away) + 1
    rows = width // CORES
    fold = fold_rows(rows)
    block = jax.ShapeDtypeStruct((rows // fold, fold * cols), jnp.bfloat16)
    return pl.pallas_call(
        functools.partial(newton_kernel, chips),
        in_specs=[SMEM] + [VMEM] * chips,
        out_specs=[VMEM] * (chips * CORES),
        out_shape=[block] * (chips * CORES),
        scratch_shapes=[
            pltpu.VMEM((cols, chips * width), jnp.float32),
            pltpu.VMEM((width, cols), jnp.float32),
        ],
        compiler_params=PARAMS,
        name="newton_schulz",
    )(index, here, *away)


def weight_kernel(chips, sources, kn_count, index, occupied, gamma, root, weight, *refs):
    blocks, out = refs[:-1], refs[-1]
    _, rows, cols = weight.shape
    fold = blocks[0].shape[1] // cols
    step_size = 0.04 * math.sqrt(max(rows * chips * CORES, cols))
    core, chip = index[0], index[1]
    column = lax.broadcasted_iota(jnp.int32, (1, cols), 1)

    def update(k, c):
        slot = (chip ^ k) * CORES + (core ^ c)
        scale = jnp.where(column < kn_count, root[slot], gamma[slot])
        mask = occupied[slot] > 0
        part = rows // fold
        for f in range(fold):
            old = weight[slot, f * part : (f + 1) * part]
            value = blocks[k * CORES + c][:, f * cols : (f + 1) * cols].astype(jnp.float32)
            new = (WEIGHT_KEEP * old - step_size * value) * scale
            out[slot, f * part : (f + 1) * part] = jnp.where(mask, new, old)

    for k in range(chips):
        for c in range(CORES):
            if sources == chips:
                update(k, c)
            else:
                pl.when((chip ^ k) < sources)(functools.partial(update, k, c))


def weights(index, occupied, gamma, weight, blocks, kn_count):
    chips = len(blocks) // CORES
    sources = weight.shape[0] // CORES
    return pl.pallas_call(
        functools.partial(weight_kernel, chips, sources, kn_count),
        in_specs=[SMEM] * 4 + [VMEM] * (1 + len(blocks)),
        out_specs=VMEM,
        out_shape=jax.ShapeDtypeStruct(weight.shape, jnp.float32),
        compiler_params=PARAMS,
        name="update_weight",
    )(index, occupied, gamma, jnp.sqrt(gamma), weight, *blocks)


def body(grad_partials, assignment, momentum, q_weight, k_weight, max_logits):
    heads_own = grad_partials.shape[2]
    kn_count = k_weight.shape[2]
    sources = lax.axis_size("owner")
    devices = lax.axis_size("dp") * lax.axis_size("context")
    chips = devices // CORES
    owner = lax.axis_index("owner")
    device = lax.axis_index(PLANE)
    core, chip = device % CORES, device // CORES
    index = jnp.stack([core, chip, owner]).astype(jnp.int32)

    def swap(value, bits):
        return lax.ppermute(value, PLANE, [(i, i ^ bits) for i in range(devices)])

    target = assignment[:, 0]
    blocks = target.reshape(sources, heads_own)
    number = jnp.arange(heads_own, dtype=jnp.int32)
    earlier = (blocks[:, None, :] == blocks[:, :, None]) & (number[None, :] < number[:, None])[None]
    position = jnp.sum(earlier.astype(jnp.int32), axis=2)
    mine, my_position = (lax.dynamic_index_in_dim(a, owner, 0, False) for a in (blocks, position))
    to = owner ^ jnp.arange(sources, dtype=jnp.int32)
    places = jnp.arange(CORES, dtype=jnp.int32)
    chosen = (mine == to[None, :, None]) & (my_position == places[:, None, None])
    heads = jnp.sum(jnp.where(chosen, number, 0), axis=2)
    own_heads = lax.dynamic_index_in_dim(heads, core, 0, False)
    other_heads = lax.dynamic_index_in_dim(heads, 1 - core, 0, False)
    held = (blocks[:, None, :] == owner) & (position[:, None, :] == places[None, :, None])
    occupied = jnp.any(held, axis=2).reshape(-1)

    old = momentum.reshape((sources, CORES) + momentum.shape[1:])
    sibling_old = swap(lax.dynamic_index_in_dim(old, 1 - core, 1, False), 1)

    g = jnp.transpose(grad_partials[0], (1, 2, 0))
    width = g.shape[2] // chips
    if width % 128:
        g = jnp.transpose(g.reshape(g.shape[:2] + (chips, width)), (0, 2, 1, 3))
    order = list(range(sources))[::-1]
    size = sources // CHUNKS
    near, arrived = None, {}
    for at in range(0, sources, size):
        ks = order[at : at + size]
        outgoing = jnp.stack([lax.dynamic_index_in_dim(g, other_heads[k], 0, False) for k in ks])
        sibling = swap(outgoing, 1)
        here, *away = pair_sums(g, sibling, jnp.stack([own_heads[k] for k in ks]), chip, chips)
        away = [swap(value, CORES * (k + 1)) for k, value in enumerate(away)]
        totals = plane_sums(here, away, [k == 0 for k in ks])
        for k, total in zip(ks, totals):
            if k == 0:
                near = total
            else:
                arrived[k] = lax.ppermute(total, "owner", [(i, i ^ k) for i in range(sources)])

    peak = max_logits
    parts = lax.axis_size("context")
    bit = 1
    while bit < parts:
        peak = jnp.maximum(peak, lax.ppermute(peak, "context", [(i, i ^ bit) for i in range(parts)]))
        bit *= 2
    gamma = jnp.minimum(1.0, LOGIT_CAP / peak[0]).reshape(sources, heads_own)
    home_gamma = lax.dynamic_index_in_dim(gamma, owner, 0, False)
    slot_gamma = jnp.sum(jnp.where(held, gamma[:, None, :], 0.0), axis=2).reshape(-1)
    k_weight_out = k_weight * jnp.sqrt(home_gamma)[:, None, None]

    occupied = occupied.astype(jnp.int32)
    turned = turn(index, momentum, sibling_old)
    new, here, *away = refreshed_rows(
        index, occupied, turned, near, [arrived[k] for k in range(1, sources)], chips
    )
    away = [swap(value, CORES * (k + 1)) for k, value in enumerate(away)]
    own_new, sibling_new = turn_back(index, new)
    momentum_out = merge(index, own_new, swap(sibling_new, 1))

    results = newton(index, here, away)
    results = [value if bits == 0 else swap(value, bits) for bits, value in enumerate(results)]
    q_weight_out = weights(index, occupied, slot_gamma, q_weight, results, kn_count)
    return (momentum_out, q_weight_out, k_weight_out)


def solution(mesh):
    rows = P("owner", ("dp", "context"), None)
    return jax.shard_map(
        body,
        mesh=mesh,
        in_specs=(
            P(("dp", "context"), None, "owner", None),
            P(),
            rows,
            rows,
            rows,
            P("context", None),
        ),
        out_specs=(rows, rows, rows),
        check_vma=False,
    )
```

time: 243 us -> 101 us (0.42)
  waiting for transfers between devices: 146 us -> 27.2 us
  local copies, waits for them, and re-layouts: 34 us -> 7.34 us
  starting transfers between devices: 4.65 us -> 29.2 us
  Pallas kernels: 0 us -> 20.4 us
  blocking collectives: 18.5 us -> 0 us
  matrix products: 14.1 us -> 0 us
  between operations: 14.2 us -> 8.5 us
  other arithmetic: 11.7 us -> 7.83 us
    unnamed x3 -> x0, waiting for transfers between devices: 78.5 us -> none
    all_gather x1 -> x0, waiting for transfers between devices: 38.8 us -> none  [orthogonalize(): gathered = lax.all_gather(iterate, ('dp', 'context'), axis=1, tiled=True)]
    ppermute x0 -> x25, starting transfers between devices: none -> 29.2 us  [the longest x20 19.7 us: swap(): return lax.ppermute(value, PLANE, [(i, i ^ bits) for i in range(devices)])]
    all_to_all x1 -> x0, waiting for transfers between devices: 28.3 us -> none  [body(): lax.all_to_all(outgoing, 'owner', split_axis=0, concat_axis=0, tiled=True)]
    ppermute x0 -> x25, waiting for transfers between devices: none -> 27.2 us  [the longest x20 22.6 us: swap(): return lax.ppermute(value, PLANE, [(i, i ^ bits) for i in range(devices)])]
    pallas_call x0 -> x10, Pallas kernels: none -> 20.4 us  [the longest x1 4.95 us: newton(): pl.pallas_call(functools.partial(newton_kernel, chips), in_specs=[SMEM] +...]
    unnamed x14 -> x11, local copies, waits for them, and re-layouts: 19.5 us -> 2.81 us
    dot_general x7 -> x0, matrix products: 14.1 us -> none  [the longest x2 6.69 us: quintic(): jnp.einsum('nrk,nrl->nkl', whole, whole, preferred_element_type=jnp.float32)]
  transfers between devices with their start and end apart: 3 -> 25, of which waited for: 3 -> 12; matrix products, arithmetic and copies ran while one was open for 3% -> 8% of each run, Pallas kernels for 0% -> 15%
where the time goes in v1:
time: 101 us; the launch traced here: 100 us
  starting transfers between devices  29.2 us (29%)
  waiting for transfers between devices  27.2 us (27%)
  Pallas kernels  20.4 us (20%)
  between operations  8.5 us (8%)
  other arithmetic  7.83 us (8%)
  local copies, waits for them, and re-layouts  7.34 us (7%)
    ppermute x20, waiting for transfers between devices, swap(): return lax.ppermute(value, PLANE, [(i, i ^ bits) for i in range(devices)])  22.6 us
    ppermute x20, starting transfers between devices, swap(): return lax.ppermute(value, PLANE, [(i, i ^ bits) for i in range(devices)])  19.7 us
    ppermute x3, starting transfers between devices, body(): lax.ppermute(total, 'owner', [(i, i ^ k) for i in range(sources)])  8.32 us
    pallas_call x1, Pallas kernels, newton(): pl.pallas_call(functools.partial(newton_kernel, chips), in_specs=[SMEM] +...  4.95 us
    pallas_call x2, Pallas kernels, pair_sums(): pl.pallas_call(functools.partial(pair_kernel, chips, aligned), grid_spec=...  4.38 us
    ppermute x3, waiting for transfers between devices, body(): lax.ppermute(total, 'owner', [(i, i ^ k) for i in range(sources)])  3.16 us
    unnamed x11, local copies, waits for them, and re-layouts  2.81 us
    concatenate x2, other arithmetic, pair_sums(): jnp.concatenate([chip[None], heads]).astype(jnp.int32)  2.75 us
  transfers between devices with their start and end apart: 25, of which 12 were waited for; matrix products, arithmetic and copies ran while one was open for 8% of the time, Pallas kernels for 15%

profile of v1, /device:TPU:0, one launch (start us, length us, event | category | flops | bytes accessed | tf_op | source)
XLA Modules:
  0.0 100.5 jit_solution(13322916315837860320)
XLA Ops:
  0.7 0.5 broadcast.73
  1.2 1.3 %reduce.7 = s32[32]{0:T(128)S(1)} reduce(s32[32,1]{0,1:T(1,128)} %param.7, s32[]{:T(128)} %broadcast.73), dimensions={1}, to_apply=%param.7.reduce_sub_computation.3 | reduce | bytes 260 | tf_op args[1]
  2.5 0.1 broadcast_in_dim_reshape_squeeze.2
  2.6 0.2 convert_reduce_fusion
  2.9 0.1 select_reduce_fusion.1
  3.1 0.6 fusion.6
  11.4 1.8 %dynamic-slice_bitcast_fusion.2 = (bf16[1,192,1536]{2,1,0:T(8,128)(2,1)S(1)}, bf16[1,192,1536]{2,1,0:T(8,128)(2,1)S(1)}, bf16[1,192,1536]{2,1,0:T(8,128)(2,1)S(1)}, bf16[1,192,1536]{2,1,0:T(8,128)(2,1)S(1)}) fusion(bf16[1,1536,8,192]{1,3,2,0:T(8,128)(2,1)} %param.6, s32[]{:T(128)S(6)} %select_n.56, s32[]{:T(128)S(6)} %select_n.55, s32[]{:T(128)S(6)} %select_n.54, ...), kind=kLoop, calls=%fused_computation.4 | loop fusion | bytes 4718608 | tf_op jit(solution)/shard_map/jit(dynamic_index_in_dim)/dynamic_slice | solution.py:358
  13.2 0.1 pad_maximum_fusion.1
  13.3 0.5 collective-permute-start.6
  13.8 1.1 %pad_maximum_fusion = bf16[2,192,1536]{2,1,0:T(8,128)(2,1)} fusion(bf16[1,192,1536]{2,1,0:T(8,128)(2,1)S(1)} %get-tuple-element.58, bf16[1,192,1536]{2,1,0:T(8,128)(2,1)S(1)} %get-tuple-element.59), kind=kLoop, calls=%fused_computation | loop fusion | flops 589824 | bytes 2359296 | tf_op jit(solution)/shard_map/stack | solution.py:358
  15.0 0.7 fusion.7
  15.6 1.4 %pad_add_fusion.2.index = s32[3]{0:T(128)S(1)} fusion(s32[1]{0:T(128)} %bitcast.18, s32[1]{0:T(128)} %bitcast.17, s32[1]{0:T(128)} %bitcast.1), kind=kLoop, calls=%fused_computation.29 | loop fusion | flops 6 | bytes 24 | tf_op jit(solution)/shard_map/concatenate | solution.py:88
  17.0 1.0 %copy-done.2 = bf16[2,192,1536]{2,1,0:T(8,128)(2,1)} copy-done((bf16[2,192,1536]{2,1,0:T(8,128)(2,1)}, bf16[2,192,1536]{2,1,0:T(8,128)(2,1)S(1)}, u32[]{:S(2)}) %copy-start.2) | copy-done | bytes 1179672
  18.0 1.3 %copy-done.3 = bf16[2,192,1536]{2,1,0:T(8,128)(2,1)S(1)} copy-done((bf16[2,192,1536]{2,1,0:T(8,128)(2,1)S(1)}, bf16[2,192,1536]{2,1,0:T(8,128)(2,1)}, u32[]{:S(2)}) %copy-start.3) | copy-done | bytes 1179672
  19.3 2.2 %pair_sum.3 = (f32[2,192,384]{2,1,0:T(8,128)S(1)}, s16[2,208,384]{2,1,0:T(8,128)(2,1)S(1)}, s16[2,208,384]{2,1,0:T(8,128)(2,1)S(1)}, s16[2,208,384]{2,1,0:T(8,128)(2,1)S(1)}) custom-call(s32[3]{0:T(128)S(1)} %pad_add_fusion.2.index, bf16[8,192,1536]{2,1,0:T(8,128)(2,1)} %bitcast.43, bf16[2,192,1536]{2,1,0:T(8,128)(2,1)S(1)} %copy-done.3), custom_call_target="tpu_custom_call" | custom-call | tf_op jit(solution)/shard_map/pair_sum/pallas_call | solution.py:72
  21.5 3.0 %collective-permute-start.7 = (s16[2,208,384]{2,1,0:T(8,128)(2,1)S(1)}, s16[2,208,384]{2,1,0:T(8,128)(2,1)S(1)}, u32[]{:S(2)}, u32[]{:S(2)}) collective-permute-start(s16[2,208,384]{2,1,0:T(8,128)(2,1)S(1)} %get-tuple-element.37), channel_id=1, source_target_pairs={{0,2},{1,3},{2,0},{3,1},{16,18},{17,19},{18,16},{19,17},{4,6},{5,7... | collective-permute-start | bytes 958472 | tf_op jit(solution)/shard_map/ppermute | solution.py:329
  24.5 1.5 %collective-permute-start.8 = (s16[2,208,384]{2,1,0:T(8,128)(2,1)S(1)}, s16[2,208,384]{2,1,0:T(8,128)(2,1)S(1)}, u32[]{:S(2)}, u32[]{:S(2)}) collective-permute-start(s16[2,208,384]{2,1,0:T(8,128)(2,1)S(1)} %get-tuple-element.38), channel_id=1, source_target_pairs={{0,16},{1,17},{2,18},{3,19},{16,0},{17,1},{18,2},{19,3},{4,20},{5,... | collective-permute-start | bytes 958472 | tf_op jit(solution)/shard_map/ppermute | solution.py:329
  26.0 0.9 dynamic-slice_bitcast_fusion
  27.0 1.4 %pad_add_fusion.1.index = s32[3]{0:T(128)S(1)} fusion(s32[1]{0:T(128)} %bitcast.8, s32[1]{0:T(128)} %bitcast.7, s32[1]{0:T(128)} %bitcast.1), kind=kLoop, calls=%fused_computation.28 | loop fusion | flops 6 | bytes 24 | tf_op jit(solution)/shard_map/concatenate | solution.py:88
  28.4 2.2 %pair_sum.2 = (f32[2,192,384]{2,1,0:T(8,128)S(1)}, s16[2,208,384]{2,1,0:T(8,128)(2,1)S(1)}, s16[2,208,384]{2,1,0:T(8,128)(2,1)S(1)}, s16[2,208,384]{2,1,0:T(8,128)(2,1)S(1)}) custom-call(s32[3]{0:T(128)S(1)} %pad_add_fusion.1.index, bf16[8,192,1536]{2,1,0:T(8,128)(2,1)} %bitcast.44, bf16[2,192,1536]{2,1,0:T(8,128)(2,1)S(1)} %collective-permute-done.1.sibling), custom_call_target="tpu_custom_call" | custom-call | tf_op jit(solution)/shard_map/pair_sum/pallas_call | solution.py:72
  30.6 2.0 %collective-permute-start.2 = (s16[2,208,384]{2,1,0:T(8,128)(2,1)S(1)}, s16[2,208,384]{2,1,0:T(8,128)(2,1)S(1)}, u32[]{:S(2)}, u32[]{:S(2)}) collective-permute-start(s16[2,208,384]{2,1,0:T(8,128)(2,1)S(1)} %get-tuple-element.31), channel_id=1, source_target_pairs={{0,2},{1,3},{2,0},{3,1},{16,18},{17,19},{18,16},{19,17},{4,6},{5,7... | collective-permute-start | bytes 958472 | tf_op jit(solution)/shard_map/ppermute | solution.py:329
  32.6 0.2 collective-permute-done.7.refs_0_
  32.9 2.1 %collective-permute-start.3 = (s16[2,208,384]{2,1,0:T(8,128)(2,1)S(1)}, s16[2,208,384]{2,1,0:T(8,128)(2,1)S(1)}, u32[]{:S(2)}, u32[]{:S(2)}) collective-permute-start(s16[2,208,384]{2,1,0:T(8,128)(2,1)S(1)} %get-tuple-element.32), channel_id=1, source_target_pairs={{0,16},{1,17},{2,18},{3,19},{16,0},{17,1},{18,2},{19,3},{4,20},{5,... | collective-permute-start | bytes 958472 | tf_op jit(solution)/shard_map/ppermute | solution.py:329
  34.9 5.9 %collective-permute-done.8.refs_1_ = s16[2,208,384]{2,1,0:T(8,128)(2,1)S(1)} collective-permute-done((s16[2,208,384]{2,1,0:T(8,128)(2,1)S(1)}, s16[2,208,384]{2,1,0:T(8,128)(2,1)S(1)}, u32[]{:S(2)}, u32[]{:S(2)}) %collective-permute-start.8) | collective-permute-done | bytes 319520 | tf_op jit(solution)/shard_map/ppermute | solution.py:329
  40.8 0.7 collective-permute-start.4
  41.6 1.0 %plane_sum.3 = (s16[208,384]{1,0:T(8,128)(2,1)}, s16[208,384]{1,0:T(8,128)(2,1)}) custom-call(f32[2,192,384]{2,1,0:T(8,128)S(1)} %get-tuple-element.36.here, s16[2,208,384]{2,1,0:T(8,128)(2,1)S(1)} %collective-permute-done.7.refs_0_, s16[2,208,384]{2,1,0:T(8,128)(2,1)S(1)} %collective-permute-done.8.refs_1_, ...), custom_call_target="tpu_custom_call" | custom-call | tf_op jit(solution)/shard_map/plane_sum/pallas_call | solution.py:108
  42.6 2.6 %collective-permute-start.10 = (s16[208,384]{1,0:T(8,128)(2,1)}, s16[208,384]{1,0:T(8,128)(2,1)S(1)}, u32[]{:S(2)}, u32[]{:S(2)}) collective-permute-start(s16[208,384]{1,0:T(8,128)(2,1)} %get-tuple-element.40), channel_id=1, source_target_pairs={{0,8},{4,12},{8,0},{12,4},{1,9},{5,13},{9,1},{13,5},{2,10},{6,14},... | collective-permute-start | bytes 479240 | tf_op jit(solution)/shard_map/ppermute | solution.py:367
  45.2 1.4 %collective-permute-done.2.refs_0_ = s16[2,208,384]{2,1,0:T(8,128)(2,1)S(1)} collective-permute-done((s16[2,208,384]{2,1,0:T(8,128)(2,1)S(1)}, s16[2,208,384]{2,1,0:T(8,128)(2,1)S(1)}, u32[]{:S(2)}, u32[]{:S(2)}) %collective-permute-start.2) | collective-permute-done | bytes 319520 | tf_op jit(solution)/shard_map/ppermute | solution.py:329
  46.6 4.2 %collective-permute-start.11 = (s16[208,384]{1,0:T(8,128)(2,1)}, s16[208,384]{1,0:T(8,128)(2,1)S(1)}, u32[]{:S(2)}, u32[]{:S(2)}) collective-permute-start(s16[208,384]{1,0:T(8,128)(2,1)} %get-tuple-element.41), channel_id=1, source_target_pairs={{0,12},{4,8},{8,4},{12,0},{1,13},{5,9},{9,5},{13,1},{2,14},{6,10},... | collective-permute-start | bytes 479240 | tf_op jit(solution)/shard_map/ppermute | solution.py:367
  50.8 3.5 %collective-permute-done.3.refs_1_ = s16[2,208,384]{2,1,0:T(8,128)(2,1)S(1)} collective-permute-done((s16[2,208,384]{2,1,0:T(8,128)(2,1)S(1)}, s16[2,208,384]{2,1,0:T(8,128)(2,1)S(1)}, u32[]{:S(2)}, u32[]{:S(2)}) %collective-permute-start.3) | collective-permute-done | bytes 319520 | tf_op jit(solution)/shard_map/ppermute | solution.py:329
  54.2 1.0 plane_sum.2
  55.2 1.6 %collective-permute-start.5 = (s16[208,384]{1,0:T(8,128)(2,1)}, s16[208,384]{1,0:T(8,128)(2,1)S(1)}, u32[]{:S(2)}, u32[]{:S(2)}) collective-permute-start(s16[208,384]{1,0:T(8,128)(2,1)} %get-tuple-element.35), channel_id=1, source_target_pairs={{0,4},{4,0},{8,12},{12,8},{1,5},{5,1},{9,13},{13,9},{2,6},{6,2},{1... | collective-permute-start | bytes 479240 | tf_op jit(solution)/shard_map/ppermute | solution.py:367
  56.8 0.1 fusion.1
  56.9 0.1 copy.11
  57.0 0.1 reshape.149.occupied
  57.2 1.1 %turn_momentum.1.old = f32[4,192,384]{2,1,0:T(8,128)S(1)} custom-call(s32[3]{0:T(128)S(1)} %pad_add_fusion.index, f32[8,192,192]{2,1,0:T(8,128)S(1)} %copy-done, f32[4,192,192]{2,1,0:T(8,128)S(1)} %collective-permute-done.sibling), custom_call_target="tpu_custom_call" | custom-call | tf_op jit(solution)/shard_map/turn_momentum/pallas_call | solution.py:129
  58.3 3.2 %collective-permute-done.5.refs_0_ = s16[208,384]{1,0:T(8,128)(2,1)S(1)} collective-permute-done((s16[208,384]{1,0:T(8,128)(2,1)}, s16[208,384]{1,0:T(8,128)(2,1)S(1)}, u32[]{:S(2)}, u32[]{:S(2)}) %collective-permute-start.5) | collective-permute-done | bytes 159776 | tf_op jit(solution)/shard_map/ppermute | solution.py:367
  61.4 1.8 %refresh_momentum.1 = (f32[4,192,384]{2,1,0:T(8,128)S(1)}, f32[192,384]{1,0:T(8,128)S(1)}, s16[208,384]{1,0:T(8,128)(2,1)}, s16[208,384]{1,0:T(8,128)(2,1)}, s16[208,384]{1,0:T(8,128)(2,1)}) custom-call(s32[3]{0:T(128)S(1)} %pad_add_fusion.index, s32[8]{0:T(128)S(1)} %reshape.149.occupied, f32[4,192,384]{2,1,0:T(8,128)S(1)} %turn_momentum.1.old, ...), custom_call_target="tpu_custom_call" | custom-call | tf_op jit(solution)/shard_map/refresh_momentum/pallas_call | solution.py:161
  63.2 1.9 %turn_back.1 = (f32[4,192,192]{2,1,0:T(8,128)S(1)}, f32[4,192,192]{2,1,0:T(8,128)}) custom-call(s32[3]{0:T(128)S(1)} %pad_add_fusion.index, f32[4,192,384]{2,1,0:T(8,128)S(1)} %get-tuple-element.42.new), custom_call_target="tpu_custom_call" | custom-call | tf_op jit(solution)/shard_map/turn_back/pallas_call | solution.py:187
  65.2 0.5 collective-permute-start.13
  65.7 1.4 %collective-permute-done.13 = f32[1,32]{1,0:T(1,128)S(1)} collective-permute-done((f32[1,32]{1,0:T(1,128)S(1)}, f32[1,32]{1,0:T(1,128)S(1)}, u32[]{:S(2)}, u32[]{:S(2)}) %collective-permute-start.13) | collective-permute-done | bytes 160 | tf_op jit(solution)/shard_map/ppermute | solution.py:373
  67.1 0.6 collective-permute-start.14
  67.7 1.4 %collective-permute-start.15 = (s16[208,384]{1,0:T(8,128)(2,1)}, s16[208,384]{1,0:T(8,128)(2,1)}, u32[]{:S(2)}, u32[]{:S(2)}) collective-permute-start(s16[208,384]{1,0:T(8,128)(2,1)} %get-tuple-element.46), channel_id=1, source_target_pairs={{0,2},{1,3},{2,0},{3,1},{16,18},{17,19},{18,16},{19,17},{4,6},{5,7... | collective-permute-start | bytes 479240 | tf_op jit(solution)/shard_map/ppermute | solution.py:329
  69.1 0.8 collective-permute-start.16
  69.9 1.3 %collective-permute-start.17 = (s16[208,384]{1,0:T(8,128)(2,1)}, s16[208,384]{1,0:T(8,128)(2,1)}, u32[]{:S(2)}, u32[]{:S(2)}) collective-permute-start(s16[208,384]{1,0:T(8,128)(2,1)} %get-tuple-element.48), channel_id=1, source_target_pairs={{0,18},{1,19},{2,16},{3,17},{16,2},{17,3},{18,0},{19,1},{4,22},{5,... | collective-permute-start | bytes 479240 | tf_op jit(solution)/shard_map/ppermute | solution.py:329
  71.3 0.1 min.16
  71.3 3.7 %collective-permute-done.15.refs_0_ = s16[208,384]{1,0:T(8,128)(2,1)} collective-permute-done((s16[208,384]{1,0:T(8,128)(2,1)}, s16[208,384]{1,0:T(8,128)(2,1)}, u32[]{:S(2)}, u32[]{:S(2)}) %collective-permute-start.15) | collective-permute-done | bytes 159776 | tf_op jit(solution)/shard_map/ppermute | solution.py:329
  75.0 3.6 %collective-permute-done.16.refs_1_ = s16[208,384]{1,0:T(8,128)(2,1)} collective-permute-done((s16[208,384]{1,0:T(8,128)(2,1)}, s16[208,384]{1,0:T(8,128)(2,1)}, u32[]{:S(2)}, u32[]{:S(2)}) %collective-permute-start.16) | collective-permute-done | bytes 159776 | tf_op jit(solution)/shard_map/ppermute | solution.py:329
  78.7 5.0 %newton_schulz.1 = (bf16[96,384]{1,0:T(8,128)(2,1)S(1)}, bf16[96,384]{1,0:T(8,128)(2,1)S(1)}, bf16[96,384]{1,0:T(8,128)(2,1)S(1)}, bf16[96,384]{1,0:T(8,128)(2,1...) custom-call(s32[3]{0:T(128)S(1)} %pad_add_fusion.index, ...), custom_call_target="tpu_custom_call" | custom-call | tf_op jit(solution)/shard_map/newton_schulz/pallas_call | solution.py:263
  83.6 0.7 collective-permute-start.19
  84.3 1.2 %collective-permute-start.20 = (bf16[96,384]{1,0:T(8,128)(2,1)S(1)}, bf16[96,384]{1,0:T(8,128)(2,1)S(1)}, u32[]{:S(2)}, u32[]{:S(2)}) collective-permute-start(bf16[96,384]{1,0:T(8,128)(2,1)S(1)} %get-tuple-element.52), channel_id=1, source_target_pairs={{0,3},{1,2},{2,1},{3,0},{16,19},{17,18},{18,17},{19,16},{4,7},{5,6... | collective-permute-start | bytes 221192 | tf_op jit(solution)/shard_map/ppermute | solution.py:329
  85.5 1.7 %broadcast_multiply_fusion = f32[8,64,128]{2,1,0:T(8,128)} fusion(f32[8,64,128]{2,1,0:T(8,128)} %param.10, f32[8]{0:T(128)S(1)} %fusion.5), kind=kLoop, calls=%fused_computation.7 | loop fusion | flops 65536 | bytes 524320 | tf_op jit(solution)/shard_map/mul | solution.py:378
  87.2 0.8 collective-permute-start.21
  88.0 0.9 collective-permute-start.22
  88.9 1.5 %collective-permute-start.23 = (bf16[96,384]{1,0:T(8,128)(2,1)}, bf16[96,384]{1,0:T(8,128)(2,1)}, u32[]{:S(2)}, u32[]{:S(2)}) collective-permute-start(bf16[96,384]{1,0:T(8,128)(2,1)} %get-tuple-element.55), channel_id=1, source_target_pairs={{0,18},{1,19},{2,16},{3,17},{16,2},{17,3},{18,0},{19,1},{4,22},{5,... | collective-permute-start | bytes 221192 | tf_op jit(solution)/shard_map/ppermute | solution.py:329
  90.3 1.3 %collective-permute-start.24 = (bf16[96,384]{1,0:T(8,128)(2,1)}, bf16[96,384]{1,0:T(8,128)(2,1)}, u32[]{:S(2)}, u32[]{:S(2)}) collective-permute-start(bf16[96,384]{1,0:T(8,128)(2,1)} %get-tuple-element.56), channel_id=1, source_target_pairs={{0,19},{1,18},{2,17},{3,16},{16,3},{17,2},{18,1},{19,0},{4,23},{5,... | collective-permute-start | bytes 221192 | tf_op jit(solution)/shard_map/ppermute | solution.py:329
  91.6 0.1 select_reduce_fusion
  91.7 0.1 copy.13
  91.8 0.1 reshape.148.gamma
  91.9 0.6 collective-permute-done.21.refs_4_
  92.5 2.6 %collective-permute-done.22.refs_5_ = bf16[96,384]{1,0:T(8,128)(2,1)} collective-permute-done((bf16[96,384]{1,0:T(8,128)(2,1)}, bf16[96,384]{1,0:T(8,128)(2,1)}, u32[]{:S(2)}, u32[]{:S(2)}) %collective-permute-start.22) | collective-permute-done | bytes 73760 | tf_op jit(solution)/shard_map/ppermute | solution.py:329
  95.1 1.0 %collective-permute-done.24.refs_7_ = bf16[96,384]{1,0:T(8,128)(2,1)} collective-permute-done((bf16[96,384]{1,0:T(8,128)(2,1)}, bf16[96,384]{1,0:T(8,128)(2,1)}, u32[]{:S(2)}, u32[]{:S(2)}) %collective-permute-start.24) | collective-permute-done | bytes 73760 | tf_op jit(solution)/shard_map/ppermute | solution.py:329
  96.1 2.5 %update_weight.1 = f32[8,192,192]{2,1,0:T(8,128)} custom-call(s32[3]{0:T(128)S(1)} %pad_add_fusion.index, s32[8]{0:T(128)S(1)} %reshape.149.occupied, f32[8]{0:T(128)S(1)} %reshape.148.gamma, f32[8]{0:T(128)S(1)} %sqrt.13.root, f32[8,192,192]{2,1,0:T(8,128)S(1)} %copy-done.1, bf16[96,384]{1,0:T(8,128)(2,1)S(1)} %get-tuple-element.49.refs_0_, ...), custom_call_target="tpu_custom_call" | custom-call | tf_op jit(solution)/shard_map/update_weight/pallas_call | solution.py:307
  98.7 1.8 %merge_momentum.1 = f32[8,192,192]{2,1,0:T(8,128)} custom-call(s32[3]{0:T(128)S(1)} %pad_add_fusion.index, f32[4,192,192]{2,1,0:T(8,128)S(1)} %get-tuple-element.43.own, f32[4,192,192]{2,1,0:T(8,128)S(1)} %collective-permute-done.12.sibling), custom_call_target="tpu_custom_call" | custom-call | tf_op jit(solution)/shard_map/merge_momentum/pallas_call | solution.py:207
  (40 shorter events, 0.4 us)
Async XLA Ops:
  13.3 3.7 %collective-permute-start.6 = (bf16[2,192,1536]{2,1,0:T(8,128)(2,1)S(1)}, bf16[2,192,1536]{2,1,0:T(8,128)(2,1)S(1)}, u32[]{:S(2)}, u32[]{:S(2)}) collective-permute-start(bf16[2,192,1536]{2,1,0:T(8,128)(2,1)S(1)} %pad_maximum_fusion.1), channel_id=1, source_target_pairs={{0,1},{1,0},{2,3},{3,2},{16,17},{17,16},{18,19},{19,18},{4,5},{5,4... | collective-permute-start | bytes 3538952 | tf_op jit(solution)/shard_map/ppermute | solution.py:329
  14.9 13.5 %collective-permute-start.1 = (bf16[2,192,1536]{2,1,0:T(8,128)(2,1)}, bf16[2,192,1536]{2,1,0:T(8,128)(2,1)S(1)}, u32[]{:S(2)}, u32[]{:S(2)}) collective-permute-start(bf16[2,192,1536]{2,1,0:T(8,128)(2,1)} %pad_maximum_fusion), channel_id=1, source_target_pairs={{0,1},{1,0},{2,3},{3,2},{16,17},{17,16},{18,19},{19,18},{4,5},{5,4... | collective-permute-start | bytes 3538952 | tf_op jit(solution)/shard_map/ppermute | solution.py:329
  17.0 1.0 %copy-start.2 = (bf16[2,192,1536]{2,1,0:T(8,128)(2,1)}, bf16[2,192,1536]{2,1,0:T(8,128)(2,1)S(1)}, u32[]{:S(2)}) copy-start(bf16[2,192,1536]{2,1,0:T(8,128)(2,1)S(1)} %collective-permute-done.6.sibling) | copy-start | bytes 3538948
  18.0 1.3 %copy-start.3 = (bf16[2,192,1536]{2,1,0:T(8,128)(2,1)S(1)}, bf16[2,192,1536]{2,1,0:T(8,128)(2,1)}, u32[]{:S(2)}) copy-start(bf16[2,192,1536]{2,1,0:T(8,128)(2,1)} %copy-done.2) | copy-start | bytes 3538948
  19.3 6.7 %copy-start = (f32[8,192,192]{2,1,0:T(8,128)S(1)}, f32[8,192,192]{2,1,0:T(8,128)}, u32[]{:S(2)}) copy-start(f32[8,192,192]{2,1,0:T(8,128)} %own.1) | copy-start | bytes 3538948
  21.5 11.4 %collective-permute-start.7 = (s16[2,208,384]{2,1,0:T(8,128)(2,1)S(1)}, s16[2,208,384]{2,1,0:T(8,128)(2,1)S(1)}, u32[]{:S(2)}, u32[]{:S(2)}) collective-permute-start(s16[2,208,384]{2,1,0:T(8,128)(2,1)S(1)} %get-tuple-element.37), channel_id=1, source_target_pairs={{0,2},{1,3},{2,0},{3,1},{16,18},{17,19},{18,16},{19,17},{4,6},{5,7... | collective-permute-start | bytes 958472 | tf_op jit(solution)/shard_map/ppermute | solution.py:329
  24.5 16.3 %collective-permute-start.8 = (s16[2,208,384]{2,1,0:T(8,128)(2,1)S(1)}, s16[2,208,384]{2,1,0:T(8,128)(2,1)S(1)}, u32[]{:S(2)}, u32[]{:S(2)}) collective-permute-start(s16[2,208,384]{2,1,0:T(8,128)(2,1)S(1)} %get-tuple-element.38), channel_id=1, source_target_pairs={{0,16},{1,17},{2,18},{3,19},{16,0},{17,1},{18,2},{19,3},{4,20},{5,... | collective-permute-start | bytes 958472 | tf_op jit(solution)/shard_map/ppermute | solution.py:329
  27.0 30.2 %collective-permute-start = (f32[4,192,192]{2,1,0:T(8,128)}, f32[4,192,192]{2,1,0:T(8,128)S(1)}, u32[]{:S(2)}, u32[]{:S(2)}) collective-permute-start(f32[4,192,192]{2,1,0:T(8,128)} %dynamic-slice_bitcast_fusion), channel_id=1, source_target_pairs={{0,1},{1,0},{2,3},{3,2},{16,17},{17,16},{18,19},{19,18},{4,5},{5,4... | collective-permute-start | bytes 1769480 | tf_op jit(solution)/shard_map/ppermute | solution.py:329
  28.4 13.2 %collective-permute-start.9 = (s16[2,208,384]{2,1,0:T(8,128)(2,1)S(1)}, s16[2,208,384]{2,1,0:T(8,128)(2,1)S(1)}, u32[]{:S(2)}, u32[]{:S(2)}) collective-permute-start(s16[2,208,384]{2,1,0:T(8,128)(2,1)S(1)} %get-tuple-element.39), channel_id=1, source_target_pairs={{0,18},{1,19},{2,16},{3,17},{16,2},{17,3},{18,0},{19,1},{4,22},{5,... | collective-permute-start | bytes 958472 | tf_op jit(solution)/shard_map/ppermute | solution.py:329
  30.6 16.0 %collective-permute-start.2 = (s16[2,208,384]{2,1,0:T(8,128)(2,1)S(1)}, s16[2,208,384]{2,1,0:T(8,128)(2,1)S(1)}, u32[]{:S(2)}, u32[]{:S(2)}) collective-permute-start(s16[2,208,384]{2,1,0:T(8,128)(2,1)S(1)} %get-tuple-element.31), channel_id=1, source_target_pairs={{0,2},{1,3},{2,0},{3,1},{16,18},{17,19},{18,16},{19,17},{4,6},{5,7... | collective-permute-start | bytes 958472 | tf_op jit(solution)/shard_map/ppermute | solution.py:329
  32.9 21.4 %collective-permute-start.3 = (s16[2,208,384]{2,1,0:T(8,128)(2,1)S(1)}, s16[2,208,384]{2,1,0:T(8,128)(2,1)S(1)}, u32[]{:S(2)}, u32[]{:S(2)}) collective-permute-start(s16[2,208,384]{2,1,0:T(8,128)(2,1)S(1)} %get-tuple-element.32), channel_id=1, source_target_pairs={{0,16},{1,17},{2,18},{3,19},{16,0},{17,1},{18,2},{19,3},{4,20},{5,... | collective-permute-start | bytes 958472 | tf_op jit(solution)/shard_map/ppermute | solution.py:329
  40.8 13.4 %collective-permute-start.4 = (s16[2,208,384]{2,1,0:T(8,128)(2,1)S(1)}, s16[2,208,384]{2,1,0:T(8,128)(2,1)S(1)}, u32[]{:S(2)}, u32[]{:S(2)}) collective-permute-start(s16[2,208,384]{2,1,0:T(8,128)(2,1)S(1)} %get-tuple-element.33), channel_id=1, source_target_pairs={{0,18},{1,19},{2,16},{3,17},{16,2},{17,3},{18,0},{19,1},{4,22},{5,... | collective-permute-start | bytes 958472 | tf_op jit(solution)/shard_map/ppermute | solution.py:329
  42.6 15.7 %collective-permute-start.10 = (s16[208,384]{1,0:T(8,128)(2,1)}, s16[208,384]{1,0:T(8,128)(2,1)S(1)}, u32[]{:S(2)}, u32[]{:S(2)}) collective-permute-start(s16[208,384]{1,0:T(8,128)(2,1)} %get-tuple-element.40), channel_id=1, source_target_pairs={{0,8},{4,12},{8,0},{12,4},{1,9},{5,13},{9,1},{13,5},{2,10},{6,14},... | collective-permute-start | bytes 479240 | tf_op jit(solution)/shard_map/ppermute | solution.py:367
  46.6 11.7 %collective-permute-start.11 = (s16[208,384]{1,0:T(8,128)(2,1)}, s16[208,384]{1,0:T(8,128)(2,1)S(1)}, u32[]{:S(2)}, u32[]{:S(2)}) collective-permute-start(s16[208,384]{1,0:T(8,128)(2,1)} %get-tuple-element.41), channel_id=1, source_target_pairs={{0,12},{4,8},{8,4},{12,0},{1,13},{5,9},{9,5},{13,1},{2,14},{6,10},... | collective-permute-start | bytes 479240 | tf_op jit(solution)/shard_map/ppermute | solution.py:367
  55.2 6.2 %collective-permute-start.5 = (s16[208,384]{1,0:T(8,128)(2,1)}, s16[208,384]{1,0:T(8,128)(2,1)S(1)}, u32[]{:S(2)}, u32[]{:S(2)}) collective-permute-start(s16[208,384]{1,0:T(8,128)(2,1)} %get-tuple-element.35), channel_id=1, source_target_pairs={{0,4},{4,0},{8,12},{12,8},{1,5},{5,1},{9,13},{13,9},{2,6},{6,2},{1... | collective-permute-start | bytes 479240 | tf_op jit(solution)/shard_map/ppermute | solution.py:367
  61.4 3.7 %copy-start.4 = (f32[1,32]{1,0:T(1,128)S(1)}, f32[1,32]{1,0:T(1,128)}, u32[]{:S(2)}) copy-start(f32[1,32]{1,0:T(1,128)} %param.11) | copy-start | bytes 388
  63.2 32.9 %copy-start.1 = (f32[8,192,192]{2,1,0:T(8,128)S(1)}, f32[8,192,192]{2,1,0:T(8,128)}, u32[]{:S(2)}) copy-start(f32[8,192,192]{2,1,0:T(8,128)} %weight.1) | copy-start | bytes 3538948
  65.2 33.5 %collective-permute-start.12 = (f32[4,192,192]{2,1,0:T(8,128)}, f32[4,192,192]{2,1,0:T(8,128)S(1)}, u32[]{:S(2)}, u32[]{:S(2)}) collective-permute-start(f32[4,192,192]{2,1,0:T(8,128)} %get-tuple-element.44), channel_id=1, source_target_pairs={{0,1},{1,0},{2,3},{3,2},{16,17},{17,16},{18,19},{19,18},{4,5},{5,4... | collective-permute-start | bytes 1769480 | tf_op jit(solution)/shard_map/ppermute | solution.py:329
  65.2 1.9 %collective-permute-start.13 = (f32[1,32]{1,0:T(1,128)S(1)}, f32[1,32]{1,0:T(1,128)S(1)}, u32[]{:S(2)}, u32[]{:S(2)}) collective-permute-start(f32[1,32]{1,0:T(1,128)S(1)} %copy-done.4), channel_id=1, source_target_pairs={{0,1},{1,0},{2,3},{3,2},{4,5},{5,4},{6,7},{7,6},{8,9},{9,8},{10,11... | collective-permute-start | bytes 392 | tf_op jit(solution)/shard_map/ppermute | solution.py:373
  67.1 4.1 %collective-permute-start.14 = (f32[1,32]{1,0:T(1,128)S(1)}, f32[1,32]{1,0:T(1,128)S(1)}, u32[]{:S(2)}, u32[]{:S(2)}) collective-permute-start(f32[1,32]{1,0:T(1,128)S(1)} %max.6), channel_id=1, source_target_pairs={{0,2},{1,3},{2,0},{3,1},{4,6},{5,7},{6,4},{7,5},{8,10},{9,11},{10,... | collective-permute-start | bytes 392 | tf_op jit(solution)/shard_map/ppermute | solution.py:373
  67.7 7.3 %collective-permute-start.15 = (s16[208,384]{1,0:T(8,128)(2,1)}, s16[208,384]{1,0:T(8,128)(2,1)}, u32[]{:S(2)}, u32[]{:S(2)}) collective-permute-start(s16[208,384]{1,0:T(8,128)(2,1)} %get-tuple-element.46), channel_id=1, source_target_pairs={{0,2},{1,3},{2,0},{3,1},{16,18},{17,19},{18,16},{19,17},{4,6},{5,7... | collective-permute-start | bytes 479240 | tf_op jit(solution)/shard_map/ppermute | solution.py:329
  69.1 9.5 %collective-permute-start.16 = (s16[208,384]{1,0:T(8,128)(2,1)}, s16[208,384]{1,0:T(8,128)(2,1)}, u32[]{:S(2)}, u32[]{:S(2)}) collective-permute-start(s16[208,384]{1,0:T(8,128)(2,1)} %get-tuple-element.47), channel_id=1, source_target_pairs={{0,16},{1,17},{2,18},{3,19},{16,0},{17,1},{18,2},{19,3},{4,20},{5,... | collective-permute-start | bytes 479240 | tf_op jit(solution)/shard_map/ppermute | solution.py:329
  69.9 8.8 %collective-permute-start.17 = (s16[208,384]{1,0:T(8,128)(2,1)}, s16[208,384]{1,0:T(8,128)(2,1)}, u32[]{:S(2)}, u32[]{:S(2)}) collective-permute-start(s16[208,384]{1,0:T(8,128)(2,1)} %get-tuple-element.48), channel_id=1, source_target_pairs={{0,18},{1,19},{2,16},{3,17},{16,2},{17,3},{18,0},{19,1},{4,22},{5,... | collective-permute-start | bytes 479240 | tf_op jit(solution)/shard_map/ppermute | solution.py:329
  83.6 4.4 %collective-permute-start.18 = (bf16[96,384]{1,0:T(8,128)(2,1)S(1)}, bf16[96,384]{1,0:T(8,128)(2,1)S(1)}, u32[]{:S(2)}, u32[]{:S(2)}) collective-permute-start(bf16[96,384]{1,0:T(8,128)(2,1)S(1)} %get-tuple-element.50), channel_id=1, source_target_pairs={{0,1},{1,0},{2,3},{3,2},{16,17},{17,16},{18,19},{19,18},{4,5},{5,4... | collective-permute-start | bytes 221192 | tf_op jit(solution)/shard_map/ppermute | solution.py:329
  83.6 5.2 %collective-permute-start.19 = (bf16[96,384]{1,0:T(8,128)(2,1)S(1)}, bf16[96,384]{1,0:T(8,128)(2,1)S(1)}, u32[]{:S(2)}, u32[]{:S(2)}) collective-permute-start(bf16[96,384]{1,0:T(8,128)(2,1)S(1)} %get-tuple-element.51), channel_id=1, source_target_pairs={{0,2},{1,3},{2,0},{3,1},{16,18},{17,19},{18,16},{19,17},{4,6},{5,7... | collective-permute-start | bytes 221192 | tf_op jit(solution)/shard_map/ppermute | solution.py:329
  84.3 6.1 %collective-permute-start.20 = (bf16[96,384]{1,0:T(8,128)(2,1)S(1)}, bf16[96,384]{1,0:T(8,128)(2,1)S(1)}, u32[]{:S(2)}, u32[]{:S(2)}) collective-permute-start(bf16[96,384]{1,0:T(8,128)(2,1)S(1)} %get-tuple-element.52), channel_id=1, source_target_pairs={{0,3},{1,2},{2,1},{3,0},{16,19},{17,18},{18,17},{19,16},{4,7},{5,6... | collective-permute-start | bytes 221192 | tf_op jit(solution)/shard_map/ppermute | solution.py:329
  87.2 5.3 %collective-permute-start.21 = (bf16[96,384]{1,0:T(8,128)(2,1)}, bf16[96,384]{1,0:T(8,128)(2,1)S(1)}, u32[]{:S(2)}, u32[]{:S(2)}) collective-permute-start(bf16[96,384]{1,0:T(8,128)(2,1)} %get-tuple-element.53), channel_id=1, source_target_pairs={{0,16},{1,17},{2,18},{3,19},{16,0},{17,1},{18,2},{19,3},{4,20},{5,... | collective-permute-start | bytes 221192 | tf_op jit(solution)/shard_map/ppermute | solution.py:329
  88.0 7.1 %collective-permute-start.22 = (bf16[96,384]{1,0:T(8,128)(2,1)}, bf16[96,384]{1,0:T(8,128)(2,1)}, u32[]{:S(2)}, u32[]{:S(2)}) collective-permute-start(bf16[96,384]{1,0:T(8,128)(2,1)} %get-tuple-element.54), channel_id=1, source_target_pairs={{0,17},{1,16},{2,19},{3,18},{16,1},{17,0},{18,3},{19,2},{4,21},{5,... | collective-permute-start | bytes 221192 | tf_op jit(solution)/shard_map/ppermute | solution.py:329
  88.9 6.3 %collective-permute-start.23 = (bf16[96,384]{1,0:T(8,128)(2,1)}, bf16[96,384]{1,0:T(8,128)(2,1)}, u32[]{:S(2)}, u32[]{:S(2)}) collective-permute-start(bf16[96,384]{1,0:T(8,128)(2,1)} %get-tuple-element.55), channel_id=1, source_target_pairs={{0,18},{1,19},{2,16},{3,17},{16,2},{17,3},{18,0},{19,1},{4,22},{5,... | collective-permute-start | bytes 221192 | tf_op jit(solution)/shard_map/ppermute | solution.py:329
  90.3 5.8 %collective-permute-start.24 = (bf16[96,384]{1,0:T(8,128)(2,1)}, bf16[96,384]{1,0:T(8,128)(2,1)}, u32[]{:S(2)}, u32[]{:S(2)}) collective-permute-start(bf16[96,384]{1,0:T(8,128)(2,1)} %get-tuple-element.56), channel_id=1, source_target_pairs={{0,19},{1,18},{2,17},{3,16},{16,3},{17,2},{18,1},{19,0},{4,23},{5,... | collective-permute-start | bytes 221192 | tf_op jit(solution)/shard_map/ppermute | solution.py:329

commit v2 on v0

v2 whole, which is shorter than its diff:
```python
import functools
import math

import jax
import jax.numpy as jnp
from jax import lax
from jax.experimental import pallas as pl
from jax.experimental.pallas import tpu as pltpu
from jax.sharding import PartitionSpec as P

ITERS = 2
MOMENTUM_RATE = 0.95
WEIGHT_KEEP = 0.98
LOGIT_CAP = 100.0
QUINTIC_A = 3.4445
QUINTIC_B = -4.775
QUINTIC_C = 2.0315

CORES = 2
PLANE = ("dp", "context")
SCALE_ROWS = 16
LEVELS = 14.99
STEPS = 8.0
LEFT = 128

SMEM = pl.BlockSpec(memory_space=pltpu.SMEM)
VMEM = pl.BlockSpec(memory_space=pltpu.VMEM)
ANY = pl.BlockSpec(memory_space=pl.ANY)
PARAMS = pltpu.CompilerParams(vmem_limit_bytes=48 * 1024 * 1024)


def whereabouts():
    device = lax.axis_index("dp") * lax.axis_size("context") + lax.axis_index("context")
    return lax.axis_index("owner"), device // CORES, device % CORES


def head_of(assignment, block, who, place, heads_own):
    found, seen = 0, 0
    for i in range(heads_own):
        hit = (assignment[0, block * heads_own + i] == who).astype(jnp.int32)
        found = jnp.where((hit == 1) & (seen == place), i, found)
        seen = seen + hit
    return found, seen


def encode(parts, out):
    top = functools.reduce(jnp.maximum, [jnp.max(jnp.abs(p), axis=0, keepdims=True) for p in parts])
    level = jnp.clip(jnp.ceil(STEPS * jnp.log2(top)), -100.0 * STEPS, 128.0 * STEPS)
    factor = jnp.exp2(LEVELS - level * (1.0 / STEPS))
    at = 0
    for p in parts:
        out[at : at + p.shape[0]] = jnp.round(p * factor).astype(jnp.int32).astype(jnp.int16)
        at += p.shape[0]
    rows = jnp.broadcast_to(level, (SCALE_ROWS, level.shape[1]))
    out[at:] = rows.astype(jnp.int32).astype(jnp.int16)


def decode(block, count):
    size = (block.shape[0] - SCALE_ROWS) // count
    level = block[size * count :].astype(jnp.int32).astype(jnp.float32)[0:1]
    factor = jnp.exp2(level * (1.0 / STEPS) - LEVELS)
    return [
        block[i * size : (i + 1) * size].astype(jnp.int32).astype(jnp.float32) * factor
        for i in range(count)
    ]


def fetch_kernel(heads_own, wanted, with_momentum, assignment, g, momentum, *refs):
    owner, _, core = whereabouts()
    outs, sem = refs[:-1], refs[-1]
    copies = []
    for group, out in zip(wanted, outs):
        for i, (k, other) in enumerate(group):
            place = 1 - core if other else core
            head, _ = head_of(assignment, owner, owner ^ k, place, heads_own)
            copies.append((g.at[head], out.at[i]))
    if with_momentum:
        for s in range(outs[-1].shape[0]):
            copies.append((momentum.at[s * CORES + 1 - core], outs[-1].at[s]))
    copies = [pltpu.make_async_copy(a, b, sem.at[i]) for i, (a, b) in enumerate(copies)]
    for copy in copies:
        copy.start()
    for copy in copies:
        copy.wait()


def fetch(assignment, g, momentum, wanted, with_momentum):
    out_shape = [jax.ShapeDtypeStruct((len(group),) + g.shape[1:], g.dtype) for group in wanted]
    count = sum(len(group) for group in wanted)
    if with_momentum:
        sources = momentum.shape[0] // CORES
        out_shape.append(jax.ShapeDtypeStruct((sources,) + momentum.shape[1:], momentum.dtype))
        count += sources
    return pl.pallas_call(
        functools.partial(fetch_kernel, g.shape[0], wanted, with_momentum),
        in_specs=[SMEM, ANY, ANY],
        out_specs=[VMEM] * len(out_shape),
        out_shape=out_shape,
        scratch_shapes=[pltpu.SemaphoreType.DMA((count,))],
        compiler_params=PARAMS,
        name="fetch_heads",
    )(assignment, g, momentum)


def offsets(bits):
    result = [0]
    for bit in reversed(bits):
        result = result + [r | (1 << bit) for r in result]
    return result


def pair_kernel(orders, aligned, own, sibling, *outs):
    _, chip, _ = whereabouts()
    width = outs[0].shape[-1]
    for a, bits in enumerate(orders):
        keep, away = outs[2 * a : 2 * a + 2]
        blocks = []
        for offset in offsets(bits):
            to = chip ^ offset
            if aligned:
                rows = pl.ds(pl.multiple_of(to * width, 128), width)
                first, second = own[a, :, rows], sibling[a, :, rows]
            else:
                first, second = own[a, to], sibling[a, to]
            blocks.append(first.astype(jnp.float32) + second.astype(jnp.float32))
            if len(blocks) <= keep.shape[0]:
                keep[len(blocks) - 1] = blocks[-1]
        encode(blocks[keep.shape[0] :], away)


def halves(count, cols, width):
    return [
        jax.ShapeDtypeStruct((count, cols, width), jnp.float32),
        jax.ShapeDtypeStruct((count * cols + SCALE_ROWS, width), jnp.int16),
    ]


def pair_sums(own, sibling, orders, chips):
    aligned = own.ndim == 3
    cols = own.shape[-2]
    width = own.shape[-1] // chips if aligned else own.shape[-1]
    return pl.pallas_call(
        functools.partial(pair_kernel, orders, aligned),
        in_specs=[VMEM, VMEM],
        out_specs=[VMEM] * 4,
        out_shape=halves(chips // 2, cols, width) * 2,
        compiler_params=PARAMS,
        name="pair_sum",
    )(own, sibling)


def plane_kernel(plain, *refs):
    outs = list(refs[4:])
    for a in range(2):
        keep, away = refs[2 * a : 2 * a + 2]
        count = keep.shape[0]
        blocks = [keep[i] + part for i, part in enumerate(decode(away, count))]
        if count > 1:
            half = outs.pop(0)
            for i in range(count // 2):
                half[i] = blocks[i]
            encode(blocks[count // 2 :], outs.pop(0))
        elif plain[a]:
            outs.pop(0)[...] = blocks[0]
        else:
            encode(blocks, outs.pop(0))


def plane_sums(state, plain):
    count, cols, width = state[0].shape
    if count > 1:
        out_shape = halves(count // 2, cols, width) * 2
    else:
        coded = jax.ShapeDtypeStruct((cols + SCALE_ROWS, width), jnp.int16)
        out_shape = [jax.ShapeDtypeStruct((cols, width), jnp.float32) if p else coded for p in plain]
    return pl.pallas_call(
        functools.partial(plane_kernel, plain),
        in_specs=[VMEM] * 4,
        out_specs=[VMEM] * len(out_shape),
        out_shape=out_shape,
        compiler_params=PARAMS,
        name="plane_sum",
    )(*state)


def turn_kernel(own, sibling, out, both):
    _, _, core = whereabouts()
    rows = own.shape[1]
    for s in range(sibling.shape[0]):
        both[pl.ds(pl.multiple_of(core * rows, 16), rows)] = own[s * CORES + core]
        both[pl.ds(pl.multiple_of((1 - core) * rows, 16), rows)] = sibling[s]
        out[s] = both[...].T


def turn(own, sibling):
    sources, rows, cols = sibling.shape
    return pl.pallas_call(
        turn_kernel,
        in_specs=[VMEM, VMEM],
        out_specs=VMEM,
        out_shape=jax.ShapeDtypeStruct((sources, cols, CORES * rows), jnp.float32),
        scratch_shapes=[pltpu.VMEM((CORES * rows, cols), jnp.float32)],
        compiler_params=PARAMS,
        name="turn_momentum",
    )(own, sibling)


def pack(matrix, out):
    cols = matrix.shape[0]
    rest = cols - LEFT
    out[:cols] = matrix[:, :LEFT].astype(out.dtype)
    for f in range(2):
        part = matrix[LEFT + f * rest // 2 : LEFT + (f + 1) * rest // 2, LEFT:]
        out[cols : cols + rest // 2, f * rest : (f + 1) * rest] = part.astype(out.dtype)


def unpack(packed, out):
    cols = out.shape[0]
    rest = cols - LEFT
    out[:, :LEFT] = packed[:cols]
    out[:LEFT, LEFT:] = packed[LEFT:cols].T
    for f in range(2):
        part = packed[cols : cols + rest // 2, f * rest : (f + 1) * rest]
        out[LEFT + f * rest // 2 : LEFT + (f + 1) * rest // 2, LEFT:] = part


def gram_kernel(chips, heads_own, assignment, old, near, *refs):
    sources = old.shape[0]
    arrived, refs = refs[: sources - 1], refs[sources - 1 :]
    (new, here), away, packed = refs[:2], refs[2:-1], refs[-1]
    owner, chip, core = whereabouts()
    for k in range(sources):
        source = owner ^ k
        grad = near[...] if k == 0 else decode(arrived[k - 1], 1)[0]
        kept = old[source]
        _, held = head_of(assignment, source, owner, 0, heads_own)
        new[source] = jnp.where(held > core, MOMENTUM_RATE * kept + grad, kept)
    for k in range(chips):
        value = new[lax.rem(chip ^ k, sources)].astype(jnp.bfloat16)
        gram = lax.dot_general(
            value, value, (((1,), (1,)), ((), ())), preferred_element_type=jnp.float32
        )
        if k == 0:
            pack(gram, here)
        else:
            pack(gram, packed)
            encode([packed[...]], away[k - 1])


def grams(assignment, old, near, arrived, chips, heads_own):
    cols = old.shape[1]
    rows = cols + (cols - LEFT) // 2
    coded = jax.ShapeDtypeStruct((rows + SCALE_ROWS, LEFT), jnp.int16)
    return pl.pallas_call(
        functools.partial(gram_kernel, chips, heads_own),
        in_specs=[SMEM] + [VMEM] * (2 + len(arrived)),
        out_specs=[VMEM] * (1 + chips),
        out_shape=[
            jax.ShapeDtypeStruct(old.shape, jnp.float32),
            jax.ShapeDtypeStruct((rows, LEFT), jnp.float32),
        ]
        + [coded] * (chips - 1),
        scratch_shapes=[pltpu.VMEM((rows, LEFT), jnp.float32)],
        compiler_params=PARAMS,
        name="refresh_and_gram",
    )(assignment, old, near, *arrived)


def small_dot(a, b):
    return lax.dot_general(
        a.astype(jnp.bfloat16), b.astype(jnp.bfloat16), (((1,), (0,)), ((), ())),
        preferred_element_type=jnp.float32,
    )


def newton_kernel(here, *refs):
    away, (out, square) = refs[:-2], refs[-2:]
    cols = square.shape[0]
    total = here[...]
    for block in away:
        total = total + decode(block, 1)[0]
    unpack(total, square)
    gram = square[...]
    row = lax.broadcasted_iota(jnp.int32, gram.shape, 0)
    column = lax.broadcasted_iota(jnp.int32, gram.shape, 1)
    square_sum = jnp.sum(jnp.where(row == column, gram, 0.0), axis=(0, 1), keepdims=True)
    norm = jnp.sqrt(square_sum) + 1e-07
    inverse = 1.0 / norm
    gram = jnp.where(norm < jnp.inf, gram * inverse * inverse, 0.0)
    first = QUINTIC_B * gram + QUINTIC_C * small_dot(gram, gram)
    twice = (2.0 * QUINTIC_A) * first + small_dot(first, first)
    gram = (QUINTIC_A * QUINTIC_A) * gram + small_dot(gram, twice)
    second = QUINTIC_B * gram + QUINTIC_C * small_dot(gram, gram)
    result = QUINTIC_A * (first + second) + small_dot(first, second)
    pack(result, out)
    high = norm.astype(jnp.bfloat16).astype(jnp.float32)
    middle = (norm - high).astype(jnp.bfloat16).astype(jnp.float32)
    low = norm - high - middle
    row = lax.broadcasted_iota(jnp.int32, (SCALE_ROWS, LEFT), 0)
    scales = jnp.where(row == 0, high, jnp.where(row == 1, middle, jnp.where(row == 2, low, 0.0)))
    out[out.shape[0] - SCALE_ROWS :] = scales.astype(jnp.bfloat16)


def newton(here, away, cols):
    return pl.pallas_call(
        newton_kernel,
        in_specs=[VMEM] * (1 + len(away)),
        out_specs=VMEM,
        out_shape=jax.ShapeDtypeStruct((here.shape[0] + SCALE_ROWS, LEFT), jnp.bfloat16),
        scratch_shapes=[pltpu.VMEM((cols, cols), jnp.float32)],
        compiler_params=PARAMS,
        name="newton_schulz",
    )(here, *away)


def back_kernel(new, own, sibling, both):
    _, _, core = whereabouts()
    rows = own.shape[1]
    for s in range(own.shape[0]):
        both[...] = new[s].T
        own[s] = both[pl.ds(pl.multiple_of(core * rows, 16), rows)]
        sibling[s] = both[pl.ds(pl.multiple_of((1 - core) * rows, 16), rows)]


def turn_back(new):
    sources, cols, width = new.shape
    half = jax.ShapeDtypeStruct((sources, width // CORES, cols), jnp.float32)
    return pl.pallas_call(
        back_kernel,
        in_specs=[VMEM],
        out_specs=[VMEM, VMEM],
        out_shape=[half, half],
        scratch_shapes=[pltpu.VMEM((width, cols), jnp.float32)],
        compiler_params=PARAMS,
        name="turn_back",
    )(new)


def merge_kernel(own, sibling, out):
    _, _, core = whereabouts()
    for s in range(own.shape[0]):
        out[s * CORES + core] = own[s]
        out[s * CORES + 1 - core] = sibling[s]


def merge(own, sibling):
    sources, rows, cols = own.shape
    return pl.pallas_call(
        merge_kernel,
        in_specs=[VMEM, VMEM],
        out_specs=VMEM,
        out_shape=jax.ShapeDtypeStruct((sources * CORES, rows, cols), jnp.float32),
        compiler_params=PARAMS,
        name="merge_momentum",
    )(own, sibling)


def head_scale(peak, head, shape):
    return jnp.minimum(1.0, LOGIT_CAP / jnp.full(shape, peak[0, head], jnp.float32))


def weight_kernel(chips, heads_own, kn_count, rows_all, assignment, peak, momentum, weight, *refs):
    blocks, (out, matrix) = refs[:-2], refs[-2:]
    slots, _, cols = weight.shape
    sources = slots // CORES
    step_size = 0.04 * math.sqrt(max(rows_all, cols))
    owner, chip, core = whereabouts()
    column = lax.broadcasted_iota(jnp.int32, (1, cols), 1)

    def update(k, c):
        source, place = chip ^ k, core ^ c
        slot = source * CORES + place
        head, held = head_of(assignment, source, owner, place, heads_own)
        block = blocks[c * chips + k]
        parts = block[block.shape[0] - SCALE_ROWS :].astype(jnp.float32)
        norm = parts[0:1, 0:1] + parts[1:2, 0:1] + parts[2:3, 0:1]
        unpack(block[: block.shape[0] - SCALE_ROWS].astype(jnp.float32), matrix)
        start = (momentum[slot] / norm).astype(jnp.bfloat16)
        result = (QUINTIC_A * QUINTIC_A) * start.astype(jnp.float32) + small_dot(start, matrix[...])
        gamma = head_scale(peak, source * heads_own + head, (1, cols))
        scale = jnp.where(column < kn_count, jnp.sqrt(gamma), gamma)
        old = weight[slot]
        new = (WEIGHT_KEEP * old - step_size * result) * scale
        out[slot] = jnp.where(held > place, new, old)

    for c in range(CORES):
        for k in range(chips):
            if sources == chips:
                update(k, c)
            else:
                pl.when((chip ^ k) < sources)(functools.partial(update, k, c))


def weights(assignment, peak, momentum, weight, blocks, heads_own, kn_count):
    chips = len(blocks) // CORES
    _, rows, cols = weight.shape
    return pl.pallas_call(
        functools.partial(weight_kernel, chips, heads_own, kn_count, rows * chips * CORES),
        in_specs=[SMEM] * 2 + [VMEM] * (2 + len(blocks)),
        out_specs=VMEM,
        out_shape=jax.ShapeDtypeStruct(weight.shape, jnp.float32),
        scratch_shapes=[pltpu.VMEM((cols, cols), jnp.float32)],
        compiler_params=PARAMS,
        name="update_weight",
    )(assignment, peak, momentum, weight, *blocks)


def key_kernel(peak, weight, out):
    owner, _, _ = whereabouts()
    heads_own, _, cols = weight.shape
    for i in range(heads_own):
        gamma = head_scale(peak, owner * heads_own + i, (1, cols))
        out[i] = weight[i] * jnp.sqrt(gamma)


def keys(peak, weight):
    return pl.pallas_call(
        key_kernel,
        in_specs=[SMEM, VMEM],
        out_specs=VMEM,
        out_shape=jax.ShapeDtypeStruct(weight.shape, jnp.float32),
        compiler_params=PARAMS,
        name="scale_keys",
    )(peak, weight)


def body(grad_partials, assignment, momentum, q_weight, k_weight, max_logits):
    heads_own = grad_partials.shape[2]
    sources = lax.axis_size("owner")
    devices = lax.axis_size("dp") * lax.axis_size("context")
    chips = devices // CORES
    levels = chips.bit_length() - 1
    orders = (list(range(levels)), list(range(levels))[::-1])
    assignment = assignment.T

    def swap(value, bits):
        return lax.ppermute(value, PLANE, [(i, i ^ bits) for i in range(devices)])

    g = jnp.transpose(grad_partials[0], (1, 2, 0))
    if (g.shape[2] // chips) % 128:
        g = jnp.transpose(g.reshape(g.shape[:2] + (chips, g.shape[2] // chips)), (0, 2, 1, 3))
    order = list(range(sources))[::-1]
    pairs = [order[at : at + 2] for at in range(0, sources, 2)]
    others = {}
    (others[0],) = fetch(assignment, g, momentum, [[(k, True) for k in pairs[0]]], False)
    wanted = [[(k, True) for k in pair] for pair in pairs[1:]]
    wanted += [[(k, False) for k in pair] for pair in pairs]
    *fetched, outgoing = fetch(assignment, g, momentum, wanted, True)
    for i in range(1, len(pairs)):
        others[i] = fetched[i - 1]
    own = fetched[len(pairs) - 1 :]

    near, arrived = None, {}
    peak = max_logits
    sibling_old = None
    for i, ks in enumerate(pairs):
        sibling = swap(others[i], 1)
        if i == 1:
            parts = lax.axis_size("context")
            bit = 1
            while bit < parts:
                perm = [(j, j ^ bit) for j in range(parts)]
                peak = jnp.maximum(peak, lax.ppermute(peak, "context", perm))
                bit *= 2
            sibling_old = swap(outgoing, 1)
            sibling, peak = lax.optimization_barrier((sibling, peak))
        state = list(pair_sums(own[i], sibling, orders, chips))
        for level in range(levels):
            for a in range(2):
                state[2 * a + 1] = swap(state[2 * a + 1], CORES << orders[a][level])
            state = list(plane_sums(state, [k == 0 for k in ks]))
        for k, total in zip(ks, state):
            if k == 0:
                near = total
            else:
                arrived[k] = lax.ppermute(total, "owner", [(j, j ^ k) for j in range(sources)])

    turned = turn(momentum, sibling_old)
    arrived = [arrived[k] for k in range(1, sources)]
    new, here, *away = grams(assignment, turned, near, arrived, chips, heads_own)
    away = [swap(value, CORES * (k + 1)) for k, value in enumerate(away)]
    own_new, sibling_new = turn_back(new)
    momentum_out = merge(own_new, swap(sibling_new, 1))
    k_weight_out = keys(peak, k_weight)

    result = newton(here, away, momentum.shape[2])
    results = [result] + [swap(result, CORES * k) for k in range(1, chips)]
    results += [swap(value, 1) for value in results]
    q_weight_out = weights(
        assignment, peak, momentum_out, q_weight, results, heads_own, k_weight.shape[2]
    )
    return (momentum_out, q_weight_out, k_weight_out)


def solution(mesh):
    rows = P("owner", ("dp", "context"), None)
    return jax.shard_map(
        body,
        mesh=mesh,
        in_specs=(
            P(("dp", "context"), None, "owner", None),
            P(),
            rows,
            rows,
            rows,
            P("context", None),
        ),
        out_specs=(rows, rows, rows),
        check_vma=False,
    )
```

time: 243 us -> 78.8 us (0.32)
  waiting for transfers between devices: 146 us -> 32.2 us
  local copies, waits for them, and re-layouts: 34 us -> 4.17 us
  starting transfers between devices: 4.65 us -> 25 us
  blocking collectives: 18.5 us -> 0 us
  Pallas kernels: 0 us -> 15.4 us
  matrix products: 14.1 us -> 0 us
  between operations: 14.2 us -> 0.79 us
  other arithmetic: 11.7 us -> 0.01 us
    unnamed x3 -> x0, waiting for transfers between devices: 78.5 us -> none
    all_gather x1 -> x0, waiting for transfers between devices: 38.8 us -> none  [orthogonalize(): gathered = lax.all_gather(iterate, ('dp', 'context'), axis=1, tiled=True)]
    ppermute x0 -> x27, waiting for transfers between devices: none -> 32.2 us  [the longest x22 22 us: swap(): return lax.ppermute(value, PLANE, [(i, i ^ bits) for i in range(devices)])]
    all_to_all x1 -> x0, waiting for transfers between devices: 28.3 us -> none  [body(): lax.all_to_all(outgoing, 'owner', split_axis=0, concat_axis=0, tiled=True)]
    ppermute x0 -> x27, starting transfers between devices: none -> 25 us  [the longest x22 16.3 us: swap(): return lax.ppermute(value, PLANE, [(i, i ^ bits) for i in range(devices)])]
    pallas_call x0 -> x15, Pallas kernels: none -> 15.4 us  [the longest x2 4.48 us: fetch(): pl.pallas_call(functools.partial(fetch_kernel, g.shape[0], wanted, with_m...]
    unnamed x14 -> x16, local copies, waits for them, and re-layouts: 19.5 us -> 4.17 us
    dot_general x7 -> x0, matrix products: 14.1 us -> none  [the longest x2 6.69 us: quintic(): jnp.einsum('nrk,nrl->nkl', whole, whole, preferred_element_type=jnp.float32)]
  transfers between devices with their start and end apart: 3 -> 27, of which waited for: 3 -> 16; matrix products, arithmetic and copies ran while one was open for 3% -> 0% of each run, Pallas kernels for 0% -> 10%
where the time goes in v2:
time: 78.8 us; the launch traced here: 77.6 us
  waiting for transfers between devices  32.2 us (41%)
  starting transfers between devices  25 us (32%)
  Pallas kernels  15.4 us (20%)
  local copies, waits for them, and re-layouts  4.17 us (5%)
  between operations  0.79 us (1%)
    ppermute x22, waiting for transfers between devices, swap(): return lax.ppermute(value, PLANE, [(i, i ^ bits) for i in range(devices)])  22 us
    ppermute x22, starting transfers between devices, swap(): return lax.ppermute(value, PLANE, [(i, i ^ bits) for i in range(devices)])  16.3 us
    ppermute x3, waiting for transfers between devices, body(): lax.ppermute(total, 'owner', [(j, j ^ k) for j in range(sources)])  6.37 us
    ppermute x3, starting transfers between devices, body(): lax.ppermute(total, 'owner', [(j, j ^ k) for j in range(sources)])  5.64 us
    pallas_call x2, Pallas kernels, fetch(): pl.pallas_call(functools.partial(fetch_kernel, g.shape[0], wanted, with_m...  4.48 us
    unnamed x16, local copies, waits for them, and re-layouts  4.17 us
    ppermute x2, waiting for transfers between devices, body(): peak = jnp.maximum(peak, lax.ppermute(peak, 'context', perm))  3.84 us
    ppermute x2, starting transfers between devices, body(): peak = jnp.maximum(peak, lax.ppermute(peak, 'context', perm))  3.09 us
  transfers between devices with their start and end apart: 27, of which 16 were waited for; matrix products, arithmetic and copies ran while one was open for 0% of the time, Pallas kernels for 10%

profile of v2, /device:TPU:0, one launch (start us, length us, event | category | flops | bytes accessed | tf_op | source)
XLA Modules:
  0.0 77.6 jit_solution(18324591569456371983)
XLA Ops:
  0.6 0.0 copy-start
  0.6 1.4 %copy-done = f32[8,192,192]{2,1,0:T(8,128)S(1)} copy-done((f32[8,192,192]{2,1,0:T(8,128)S(1)}, f32[8,192,192]{2,1,0:T(8,128)}, u32[]{:S(2)}) %copy-start) | copy-done | bytes 1179672
  2.0 0.7 copy-done.5
  2.7 2.6 %fetch_heads.2 = (bf16[2,192,1536]{2,1,0:T(8,128)(2,1)S(1)}, bf16[2,192,1536]{2,1,0:T(8,128)(2,1)S(1)}, bf16[2,192,1536]{2,1,0:T(8,128)(2,1)S(1)}, f32[4,192,192]{2,1,0:T(8,128)S(1)}) custom-call(s32[1,32]{1,0:T(1,128)S(1)} %bitcast.4, bf16[8,192,1536]{2,1,0:T(8,128)(2,1)} %bitcast.8, f32[8,192,192]{2,1,0:T(8,128)S(1)} %copy-done), custom_call_target="tpu_custom_call" | custom-call | tf_op jit(solution)/shard_map/fetch_heads/pallas_call | solution.py:94
  5.3 0.0 copy-start.7
  5.4 0.5 collective-permute-start.1
  5.9 1.8 %fetch_heads.3 = bf16[2,192,1536]{2,1,0:T(8,128)(2,1)S(1)} custom-call(s32[1,32]{1,0:T(1,128)S(1)} %bitcast.5, bf16[8,192,1536]{2,1,0:T(8,128)(2,1)} %bitcast.9, f32[8,192,192]{2,1,0:T(8,128)S(1)} %copy-done), custom_call_target="tpu_custom_call" | custom-call | tf_op jit(solution)/shard_map/fetch_heads/pallas_call | solution.py:94
  7.7 0.1 collective-permute-start.9
  7.8 0.5 collective-permute-start.2
  8.3 2.3 %collective-permute-done.2 = f32[1,32]{1,0:T(1,128)S(1)} collective-permute-done((f32[1,32]{1,0:T(1,128)S(1)}, f32[1,32]{1,0:T(1,128)S(1)}, u32[]{:S(2)}, u32[]{:S(2)}) %collective-permute-start.2) | collective-permute-done | bytes 160 | tf_op jit(solution)/shard_map/ppermute | solution.py:463
  10.6 2.6 %collective-permute-start.3 = (f32[1,32]{1,0:T(1,128)S(1)}, f32[1,32]{1,0:T(1,128)S(1)}, u32[]{:S(2)}, u32[]{:S(2)}) collective-permute-start(f32[1,32]{1,0:T(1,128)S(1)} %max.6), channel_id=1, source_target_pairs={{0,2},{1,3},{2,0},{3,1},{4,6},{5,7},{6,4},{7,5},{8,10},{9,11},{10,... | collective-permute-start | bytes 392 | tf_op jit(solution)/shard_map/ppermute | solution.py:463
  13.3 1.5 %collective-permute-done.3 = f32[1,32]{1,0:T(1,128)S(1)} collective-permute-done((f32[1,32]{1,0:T(1,128)S(1)}, f32[1,32]{1,0:T(1,128)S(1)}, u32[]{:S(2)}, u32[]{:S(2)}) %collective-permute-start.3) | collective-permute-done | bytes 160 | tf_op jit(solution)/shard_map/ppermute | solution.py:463
  14.8 0.0 collective-permute-done.1.sibling
  14.8 0.5 pair_sum.2
  15.3 2.1 %collective-permute-start.4 = (s16[400,384]{1,0:T(8,128)(2,1)S(1)}, s16[400,384]{1,0:T(8,128)(2,1)S(1)}, u32[]{:S(2)}, u32[]{:S(2)}) collective-permute-start(s16[400,384]{1,0:T(8,128)(2,1)S(1)} %get-tuple-element.41), channel_id=1, source_target_pairs={{0,2},{1,3},{2,0},{3,1},{16,18},{17,19},{18,16},{19,17},{4,6},{5,7... | collective-permute-start | bytes 921608 | tf_op jit(solution)/shard_map/ppermute | solution.py:437
  17.4 1.5 %collective-permute-start.5 = (s16[400,384]{1,0:T(8,128)(2,1)S(1)}, s16[400,384]{1,0:T(8,128)(2,1)S(1)}, u32[]{:S(2)}, u32[]{:S(2)}) collective-permute-start(s16[400,384]{1,0:T(8,128)(2,1)S(1)} %get-tuple-element.43), channel_id=1, source_target_pairs={{0,16},{1,17},{2,18},{3,19},{16,0},{17,1},{18,2},{19,3},{4,20},{5,... | collective-permute-start | bytes 921608 | tf_op jit(solution)/shard_map/ppermute | solution.py:437
  18.9 0.0 collective-permute-done.9.sibling
  18.9 0.5 pair_sum.3
  19.4 0.6 collective-permute-start.10
  20.0 0.0 collective-permute-start.11
  20.0 5.5 %collective-permute-done.4.refs_1_ = s16[400,384]{1,0:T(8,128)(2,1)S(1)} collective-permute-done((s16[400,384]{1,0:T(8,128)(2,1)S(1)}, s16[400,384]{1,0:T(8,128)(2,1)S(1)}, u32[]{:S(2)}, u32[]{:S(2)}) %collective-permute-start.4) | collective-permute-done | bytes 307232 | tf_op jit(solution)/shard_map/ppermute | solution.py:437
  25.5 2.0 %collective-permute-done.5.refs_3_ = s16[400,384]{1,0:T(8,128)(2,1)S(1)} collective-permute-done((s16[400,384]{1,0:T(8,128)(2,1)S(1)}, s16[400,384]{1,0:T(8,128)(2,1)S(1)}, u32[]{:S(2)}, u32[]{:S(2)}) %collective-permute-start.5) | collective-permute-done | bytes 307232 | tf_op jit(solution)/shard_map/ppermute | solution.py:437
  27.6 0.3 plane_sum.4
  27.8 1.6 %collective-permute-start.6 = (s16[208,384]{1,0:T(8,128)(2,1)S(1)}, s16[208,384]{1,0:T(8,128)(2,1)S(1)}, u32[]{:S(2)}, u32[]{:S(2)}) collective-permute-start(s16[208,384]{1,0:T(8,128)(2,1)S(1)} %get-tuple-element.45), channel_id=1, source_target_pairs={{0,16},{1,17},{2,18},{3,19},{16,0},{17,1},{18,2},{19,3},{4,20},{5,... | collective-permute-start | bytes 479240 | tf_op jit(solution)/shard_map/ppermute | solution.py:437
  29.4 0.5 collective-permute-start.7
  30.0 2.2 %collective-permute-done.10.refs_1_ = s16[400,384]{1,0:T(8,128)(2,1)S(1)} collective-permute-done((s16[400,384]{1,0:T(8,128)(2,1)S(1)}, s16[400,384]{1,0:T(8,128)(2,1)S(1)}, u32[]{:S(2)}, u32[]{:S(2)}) %collective-permute-start.10) | collective-permute-done | bytes 307232 | tf_op jit(solution)/shard_map/ppermute | solution.py:437
  32.1 2.0 %collective-permute-done.11.refs_3_ = s16[400,384]{1,0:T(8,128)(2,1)S(1)} collective-permute-done((s16[400,384]{1,0:T(8,128)(2,1)S(1)}, s16[400,384]{1,0:T(8,128)(2,1)S(1)}, u32[]{:S(2)}, u32[]{:S(2)}) %collective-permute-start.11) | collective-permute-done | bytes 307232 | tf_op jit(solution)/shard_map/ppermute | solution.py:437
  34.1 0.3 plane_sum.6
  34.4 0.0 copy-start.1
  34.4 1.6 %collective-permute-start.12 = (s16[208,384]{1,0:T(8,128)(2,1)S(1)}, s16[208,384]{1,0:T(8,128)(2,1)S(1)}, u32[]{:S(2)}, u32[]{:S(2)}) collective-permute-start(s16[208,384]{1,0:T(8,128)(2,1)S(1)} %get-tuple-element.56), channel_id=1, source_target_pairs={{0,16},{1,17},{2,18},{3,19},{16,0},{17,1},{18,2},{19,3},{4,20},{5,... | collective-permute-start | bytes 479240 | tf_op jit(solution)/shard_map/ppermute | solution.py:437
  36.0 0.5 collective-permute-start.13
  36.6 0.6 collective-permute-done.6.refs_1_
  37.2 0.2 plane_sum.5
  37.3 1.6 %collective-permute-start.8 = (s16[208,384]{1,0:T(8,128)(2,1)S(1)}, s16[208,384]{1,0:T(8,128)(2,1)S(1)}, u32[]{:S(2)}, u32[]{:S(2)}) collective-permute-start(s16[208,384]{1,0:T(8,128)(2,1)S(1)} %get-tuple-element.49), channel_id=1, source_target_pairs={{0,4},{4,0},{8,12},{12,8},{1,5},{5,1},{9,13},{13,9},{2,6},{6,2},{1... | collective-permute-start | bytes 479240 | tf_op jit(solution)/shard_map/ppermute | solution.py:476
  39.0 0.8 %collective-permute-done.12.refs_1_ = s16[208,384]{1,0:T(8,128)(2,1)S(1)} collective-permute-done((s16[208,384]{1,0:T(8,128)(2,1)S(1)}, s16[208,384]{1,0:T(8,128)(2,1)S(1)}, u32[]{:S(2)}, u32[]{:S(2)}) %collective-permute-start.12) | collective-permute-done | bytes 159776 | tf_op jit(solution)/shard_map/ppermute | solution.py:437
  39.8 1.5 %collective-permute-done.13.refs_3_ = s16[208,384]{1,0:T(8,128)(2,1)S(1)} collective-permute-done((s16[208,384]{1,0:T(8,128)(2,1)S(1)}, s16[208,384]{1,0:T(8,128)(2,1)S(1)}, u32[]{:S(2)}, u32[]{:S(2)}) %collective-permute-start.13) | collective-permute-done | bytes 159776 | tf_op jit(solution)/shard_map/ppermute | solution.py:437
  41.3 0.2 plane_sum.7
  41.5 2.7 %collective-permute-start.14 = (s16[208,384]{1,0:T(8,128)(2,1)S(1)}, s16[208,384]{1,0:T(8,128)(2,1)S(1)}, u32[]{:S(2)}, u32[]{:S(2)}) collective-permute-start(s16[208,384]{1,0:T(8,128)(2,1)S(1)} %get-tuple-element.59), channel_id=1, source_target_pairs={{0,8},{4,12},{8,0},{12,4},{1,9},{5,13},{9,1},{13,5},{2,10},{6,14},... | collective-permute-start | bytes 479240 | tf_op jit(solution)/shard_map/ppermute | solution.py:476
  44.2 1.3 %collective-permute-start.15 = (s16[208,384]{1,0:T(8,128)(2,1)S(1)}, s16[208,384]{1,0:T(8,128)(2,1)S(1)}, u32[]{:S(2)}, u32[]{:S(2)}) collective-permute-start(s16[208,384]{1,0:T(8,128)(2,1)S(1)} %get-tuple-element.60), channel_id=1, source_target_pairs={{0,12},{4,8},{8,4},{12,0},{1,13},{5,9},{9,5},{13,1},{2,14},{6,10},... | collective-permute-start | bytes 479240 | tf_op jit(solution)/shard_map/ppermute | solution.py:476
  45.5 0.0 collective-permute-done.sibling
  45.5 0.7 turn_momentum.1.old
  46.3 6.4 %collective-permute-done.14.refs_1_ = s16[208,384]{1,0:T(8,128)(2,1)S(1)} collective-permute-done((s16[208,384]{1,0:T(8,128)(2,1)S(1)}, s16[208,384]{1,0:T(8,128)(2,1)S(1)}, u32[]{:S(2)}, u32[]{:S(2)}) %collective-permute-start.14) | collective-permute-done | bytes 159776 | tf_op jit(solution)/shard_map/ppermute | solution.py:476
  52.6 1.4 %refresh_and_gram.1 = (f32[4,192,384]{2,1,0:T(8,128)S(1)}, f32[224,128]{1,0:T(8,128)S(1)}, s16[240,128]{1,0:T(8,128)(2,1)S(1)}, s16[240,128]{1,0:T(8,128)(2,1)S(1)}, s16[240,128]{1,0:T(8,128)(2,1)S(1)}) custom-call(s32[1,32]{1,0:T(1,128)S(1)} %bitcast.6, f32[4,192,384]{2,1,0:T(8,128)S(1)} %turn_momentum.1.old, f32[192,384]{1,0:T(8,128)S(1)} %get-tuple-element.48.near, ...), custom_call_target="tpu_custom_call" | custom-call | tf_op jit(solution)/shard_map/refresh_and_gram/pallas_call | solution.py:254
  54.1 0.0 copy-start.4
  54.1 0.7 turn_back.1
  54.8 0.1 collective-permute-start.16
  54.9 0.7 collective-permute-start.17
  55.6 1.4 %collective-permute-start.18 = (s16[240,128]{1,0:T(8,128)(2,1)S(1)}, s16[240,128]{1,0:T(8,128)(2,1)S(1)}, u32[]{:S(2)}, u32[]{:S(2)}) collective-permute-start(s16[240,128]{1,0:T(8,128)(2,1)S(1)} %get-tuple-element.67), channel_id=1, source_target_pairs={{0,16},{1,17},{2,18},{3,19},{16,0},{17,1},{18,2},{19,3},{4,20},{5,... | collective-permute-start | bytes 184328 | tf_op jit(solution)/shard_map/ppermute | solution.py:437
  57.0 1.4 %collective-permute-start.19 = (s16[240,128]{1,0:T(8,128)(2,1)S(1)}, s16[240,128]{1,0:T(8,128)(2,1)S(1)}, u32[]{:S(2)}, u32[]{:S(2)}) collective-permute-start(s16[240,128]{1,0:T(8,128)(2,1)S(1)} %get-tuple-element.68), channel_id=1, source_target_pairs={{0,18},{1,19},{2,16},{3,17},{16,2},{17,3},{18,0},{19,1},{4,22},{5,... | collective-permute-start | bytes 184328 | tf_op jit(solution)/shard_map/ppermute | solution.py:437
  58.4 0.9 %collective-permute-done.17.refs_0_ = s16[240,128]{1,0:T(8,128)(2,1)S(1)} collective-permute-done((s16[240,128]{1,0:T(8,128)(2,1)S(1)}, s16[240,128]{1,0:T(8,128)(2,1)S(1)}, u32[]{:S(2)}, u32[]{:S(2)}) %collective-permute-start.17) | collective-permute-done | bytes 61472 | tf_op jit(solution)/shard_map/ppermute | solution.py:437
  59.3 0.5 collective-permute-done.18.refs_1_
  59.8 2.3 %collective-permute-done.19.refs_2_ = s16[240,128]{1,0:T(8,128)(2,1)S(1)} collective-permute-done((s16[240,128]{1,0:T(8,128)(2,1)S(1)}, s16[240,128]{1,0:T(8,128)(2,1)S(1)}, u32[]{:S(2)}, u32[]{:S(2)}) %collective-permute-start.19) | collective-permute-done | bytes 61472 | tf_op jit(solution)/shard_map/ppermute | solution.py:437
  62.1 1.2 %newton_schulz.1.refs_0_ = bf16[240,128]{1,0:T(8,128)(2,1)S(1)} custom-call(f32[224,128]{1,0:T(8,128)S(1)} %get-tuple-element.65.here, s16[240,128]{1,0:T(8,128)(2,1)S(1)} %collective-permute-done.17.refs_0_, s16[240,128]{1,0:T(8,128)(2,1)S(1)} %collective-permute-done.18.refs_1_, s16[240,128]{1,0:T(8,128)(2,1)S(1)} %collective-permute-done.19.refs_2_), custom_call_target="tpu_custom_call" | custom-call | tf_op jit(solution)/shard_map/newton_schulz/pallas_call | solution.py:305
  63.3 1.5 %collective-permute-start.20 = (bf16[240,128]{1,0:T(8,128)(2,1)S(1)}, bf16[240,128]{1,0:T(8,128)(2,1)S(1)}, u32[]{:S(2)}, u32[]{:S(2)}) collective-permute-start(bf16[240,128]{1,0:T(8,128)(2,1)S(1)} %newton_schulz.1.refs_0_), channel_id=1, source_target_pairs={{0,2},{1,3},{2,0},{3,1},{16,18},{17,19},{18,16},{19,17},{4,6},{5,7... | collective-permute-start | bytes 184328 | tf_op jit(solution)/shard_map/ppermute | solution.py:437
  64.8 0.5 collective-permute-start.21
  65.3 1.5 %collective-permute-start.22 = (bf16[240,128]{1,0:T(8,128)(2,1)S(1)}, bf16[240,128]{1,0:T(8,128)(2,1)S(1)}, u32[]{:S(2)}, u32[]{:S(2)}) collective-permute-start(bf16[240,128]{1,0:T(8,128)(2,1)S(1)} %newton_schulz.1.refs_0_), channel_id=1, source_target_pairs={{0,18},{1,19},{2,16},{3,17},{16,2},{17,3},{18,0},{19,1},{4,22},{5,... | collective-permute-start | bytes 184328 | tf_op jit(solution)/shard_map/ppermute | solution.py:437
  66.8 1.2 %collective-permute-done.20.refs_1_ = bf16[240,128]{1,0:T(8,128)(2,1)S(1)} collective-permute-done((bf16[240,128]{1,0:T(8,128)(2,1)S(1)}, bf16[240,128]{1,0:T(8,128)(2,1)S(1)}, u32[]{:S(2)}, u32[]{:S(2)}) %collective-permute-start.20) | collective-permute-done | bytes 61472 | tf_op jit(solution)/shard_map/ppermute | solution.py:437
  68.0 1.0 %collective-permute-done.21.refs_2_ = bf16[240,128]{1,0:T(8,128)(2,1)S(1)} collective-permute-done((bf16[240,128]{1,0:T(8,128)(2,1)S(1)}, bf16[240,128]{1,0:T(8,128)(2,1)S(1)}, u32[]{:S(2)}, u32[]{:S(2)}) %collective-permute-start.21) | collective-permute-done | bytes 61472 | tf_op jit(solution)/shard_map/ppermute | solution.py:437
  69.0 1.4 %collective-permute-done.22.refs_3_ = bf16[240,128]{1,0:T(8,128)(2,1)S(1)} collective-permute-done((bf16[240,128]{1,0:T(8,128)(2,1)S(1)}, bf16[240,128]{1,0:T(8,128)(2,1)S(1)}, u32[]{:S(2)}, u32[]{:S(2)}) %collective-permute-start.22) | collective-permute-done | bytes 61472 | tf_op jit(solution)/shard_map/ppermute | solution.py:437
  70.4 1.3 %scale_keys.1 = f32[8,64,128]{2,1,0:T(8,128)} custom-call(f32[1,32]{1,0:T(1,128)S(1)} %max.7.peak, f32[8,64,128]{2,1,0:T(8,128)S(1)} %copy-done.4), custom_call_target="tpu_custom_call" | custom-call | tf_op jit(solution)/shard_map/scale_keys/pallas_call | solution.py:417
  71.7 1.3 %merge_momentum.1.momentum = f32[8,192,192]{2,1,0:T(8,128)} custom-call(f32[4,192,192]{2,1,0:T(8,128)S(1)} %get-tuple-element.62.own, f32[4,192,192]{2,1,0:T(8,128)S(1)} %collective-permute-done.16.sibling), custom_call_target="tpu_custom_call" | custom-call | tf_op jit(solution)/shard_map/merge_momentum/pallas_call | solution.py:348
  73.0 0.7 copy-done.3
  73.7 1.4 %copy-done.2 = f32[8,192,192]{2,1,0:T(8,128)S(1)} copy-done((f32[8,192,192]{2,1,0:T(8,128)S(1)}, f32[8,192,192]{2,1,0:T(8,128)}, u32[]{:S(2)}) %copy-start.2) | copy-done | bytes 1179672
  75.1 2.6 %update_weight.1 = f32[8,192,192]{2,1,0:T(8,128)} custom-call(s32[1,32]{1,0:T(1,128)S(1)} %bitcast.7, f32[1,32]{1,0:T(1,128)S(1)} %max.7.peak, f32[8,192,192]{2,1,0:T(8,128)S(1)} %copy-done.2, f32[8,192,192]{2,1,0:T(8,128)S(1)} %copy-done.3, bf16[240,128]{1,0:T(8,128)(2,1)S(1)} %newton_schulz.1.refs_0_, ...), custom_call_target="tpu_custom_call" | custom-call | tf_op jit(solution)/shard_map/update_weight/pallas_call | solution.py:397
  (23 shorter events, 0.1 us)
Async XLA Ops:
  0.6 1.4 %copy-start = (f32[8,192,192]{2,1,0:T(8,128)S(1)}, f32[8,192,192]{2,1,0:T(8,128)}, u32[]{:S(2)}) copy-start(f32[8,192,192]{2,1,0:T(8,128)} %momentum.3) | copy-start | bytes 3538948
  2.0 0.7 copy-start.5
  5.3 2.5 %copy-start.7 = (f32[1,32]{1,0:T(1,128)S(1)}, f32[1,32]{1,0:T(1,128)}, u32[]{:S(2)}) copy-start(f32[1,32]{1,0:T(1,128)} %param.11) | copy-start | bytes 388
  5.4 9.4 %collective-permute-start.1 = (bf16[2,192,1536]{2,1,0:T(8,128)(2,1)S(1)}, bf16[2,192,1536]{2,1,0:T(8,128)(2,1)S(1)}, u32[]{:S(2)}, u32[]{:S(2)}) collective-permute-start(bf16[2,192,1536]{2,1,0:T(8,128)(2,1)S(1)} %get-tuple-element.38), channel_id=1, source_target_pairs={{0,1},{1,0},{2,3},{3,2},{16,17},{17,16},{18,19},{19,18},{4,5},{5,4... | collective-permute-start | bytes 3538952 | tf_op jit(solution)/shard_map/ppermute | solution.py:437
  7.7 11.2 %collective-permute-start.9 = (bf16[2,192,1536]{2,1,0:T(8,128)(2,1)S(1)}, bf16[2,192,1536]{2,1,0:T(8,128)(2,1)S(1)}, u32[]{:S(2)}, u32[]{:S(2)}) collective-permute-start(bf16[2,192,1536]{2,1,0:T(8,128)(2,1)S(1)} %fetch_heads.3), channel_id=1, source_target_pairs={{0,1},{1,0},{2,3},{3,2},{16,17},{17,16},{18,19},{19,18},{4,5},{5,4... | collective-permute-start | bytes 3538952 | tf_op jit(solution)/shard_map/ppermute | solution.py:437
  7.8 2.8 %collective-permute-start.2 = (f32[1,32]{1,0:T(1,128)S(1)}, f32[1,32]{1,0:T(1,128)S(1)}, u32[]{:S(2)}, u32[]{:S(2)}) collective-permute-start(f32[1,32]{1,0:T(1,128)S(1)} %copy-done.7), channel_id=1, source_target_pairs={{0,1},{1,0},{2,3},{3,2},{4,5},{5,4},{6,7},{7,6},{8,9},{9,8},{10,11... | collective-permute-start | bytes 392 | tf_op jit(solution)/shard_map/ppermute | solution.py:463
  10.6 4.1 %collective-permute-start.3 = (f32[1,32]{1,0:T(1,128)S(1)}, f32[1,32]{1,0:T(1,128)S(1)}, u32[]{:S(2)}, u32[]{:S(2)}) collective-permute-start(f32[1,32]{1,0:T(1,128)S(1)} %max.6), channel_id=1, source_target_pairs={{0,2},{1,3},{2,0},{3,1},{4,6},{5,7},{6,4},{7,5},{8,10},{9,11},{10,... | collective-permute-start | bytes 392 | tf_op jit(solution)/shard_map/ppermute | solution.py:463
  15.3 10.3 %collective-permute-start.4 = (s16[400,384]{1,0:T(8,128)(2,1)S(1)}, s16[400,384]{1,0:T(8,128)(2,1)S(1)}, u32[]{:S(2)}, u32[]{:S(2)}) collective-permute-start(s16[400,384]{1,0:T(8,128)(2,1)S(1)} %get-tuple-element.41), channel_id=1, source_target_pairs={{0,2},{1,3},{2,0},{3,1},{16,18},{17,19},{18,16},{19,17},{4,6},{5,7... | collective-permute-start | bytes 921608 | tf_op jit(solution)/shard_map/ppermute | solution.py:437
  17.4 10.2 %collective-permute-start.5 = (s16[400,384]{1,0:T(8,128)(2,1)S(1)}, s16[400,384]{1,0:T(8,128)(2,1)S(1)}, u32[]{:S(2)}, u32[]{:S(2)}) collective-permute-start(s16[400,384]{1,0:T(8,128)(2,1)S(1)} %get-tuple-element.43), channel_id=1, source_target_pairs={{0,16},{1,17},{2,18},{3,19},{16,0},{17,1},{18,2},{19,3},{4,20},{5,... | collective-permute-start | bytes 921608 | tf_op jit(solution)/shard_map/ppermute | solution.py:437
  19.4 12.8 %collective-permute-start.10 = (s16[400,384]{1,0:T(8,128)(2,1)S(1)}, s16[400,384]{1,0:T(8,128)(2,1)S(1)}, u32[]{:S(2)}, u32[]{:S(2)}) collective-permute-start(s16[400,384]{1,0:T(8,128)(2,1)S(1)} %get-tuple-element.52), channel_id=1, source_target_pairs={{0,2},{1,3},{2,0},{3,1},{16,18},{17,19},{18,16},{19,17},{4,6},{5,7... | collective-permute-start | bytes 921608 | tf_op jit(solution)/shard_map/ppermute | solution.py:437
  20.0 14.2 %collective-permute-start.11 = (s16[400,384]{1,0:T(8,128)(2,1)S(1)}, s16[400,384]{1,0:T(8,128)(2,1)S(1)}, u32[]{:S(2)}, u32[]{:S(2)}) collective-permute-start(s16[400,384]{1,0:T(8,128)(2,1)S(1)} %get-tuple-element.54), channel_id=1, source_target_pairs={{0,16},{1,17},{2,18},{3,19},{16,0},{17,1},{18,2},{19,3},{4,20},{5,... | collective-permute-start | bytes 921608 | tf_op jit(solution)/shard_map/ppermute | solution.py:437
  20.0 25.5 %collective-permute-start = (f32[4,192,192]{2,1,0:T(8,128)S(1)}, f32[4,192,192]{2,1,0:T(8,128)S(1)}, u32[]{:S(2)}, u32[]{:S(2)}) collective-permute-start(f32[4,192,192]{2,1,0:T(8,128)S(1)} %get-tuple-element.36), channel_id=1, source_target_pairs={{0,1},{1,0},{2,3},{3,2},{16,17},{17,16},{18,19},{19,18},{4,5},{5,4... | collective-permute-start | bytes 1769480 | tf_op jit(solution)/shard_map/ppermute | solution.py:437
  27.8 9.3 %collective-permute-start.6 = (s16[208,384]{1,0:T(8,128)(2,1)S(1)}, s16[208,384]{1,0:T(8,128)(2,1)S(1)}, u32[]{:S(2)}, u32[]{:S(2)}) collective-permute-start(s16[208,384]{1,0:T(8,128)(2,1)S(1)} %get-tuple-element.45), channel_id=1, source_target_pairs={{0,16},{1,17},{2,18},{3,19},{16,0},{17,1},{18,2},{19,3},{4,20},{5,... | collective-permute-start | bytes 479240 | tf_op jit(solution)/shard_map/ppermute | solution.py:437
  29.4 7.7 %collective-permute-start.7 = (s16[208,384]{1,0:T(8,128)(2,1)S(1)}, s16[208,384]{1,0:T(8,128)(2,1)S(1)}, u32[]{:S(2)}, u32[]{:S(2)}) collective-permute-start(s16[208,384]{1,0:T(8,128)(2,1)S(1)} %get-tuple-element.47), channel_id=1, source_target_pairs={{0,2},{1,3},{2,0},{3,1},{16,18},{17,19},{18,16},{19,17},{4,6},{5,7... | collective-permute-start | bytes 479240 | tf_op jit(solution)/shard_map/ppermute | solution.py:437
  34.4 11.1 %copy-start.1 = (f32[8,192,192]{2,1,0:T(8,128)S(1)}, f32[8,192,192]{2,1,0:T(8,128)}, u32[]{:S(2)}) copy-start(f32[8,192,192]{2,1,0:T(8,128)} %momentum.3) | copy-start | bytes 3538948
  34.4 5.3 %collective-permute-start.12 = (s16[208,384]{1,0:T(8,128)(2,1)S(1)}, s16[208,384]{1,0:T(8,128)(2,1)S(1)}, u32[]{:S(2)}, u32[]{:S(2)}) collective-permute-start(s16[208,384]{1,0:T(8,128)(2,1)S(1)} %get-tuple-element.56), channel_id=1, source_target_pairs={{0,16},{1,17},{2,18},{3,19},{16,0},{17,1},{18,2},{19,3},{4,20},{5,... | collective-permute-start | bytes 479240 | tf_op jit(solution)/shard_map/ppermute | solution.py:437
  36.0 5.3 %collective-permute-start.13 = (s16[208,384]{1,0:T(8,128)(2,1)S(1)}, s16[208,384]{1,0:T(8,128)(2,1)S(1)}, u32[]{:S(2)}, u32[]{:S(2)}) collective-permute-start(s16[208,384]{1,0:T(8,128)(2,1)S(1)} %get-tuple-element.58), channel_id=1, source_target_pairs={{0,2},{1,3},{2,0},{3,1},{16,18},{17,19},{18,16},{19,17},{4,6},{5,7... | collective-permute-start | bytes 479240 | tf_op jit(solution)/shard_map/ppermute | solution.py:437
  37.3 8.9 %collective-permute-start.8 = (s16[208,384]{1,0:T(8,128)(2,1)S(1)}, s16[208,384]{1,0:T(8,128)(2,1)S(1)}, u32[]{:S(2)}, u32[]{:S(2)}) collective-permute-start(s16[208,384]{1,0:T(8,128)(2,1)S(1)} %get-tuple-element.49), channel_id=1, source_target_pairs={{0,4},{4,0},{8,12},{12,8},{1,5},{5,1},{9,13},{13,9},{2,6},{6,2},{1... | collective-permute-start | bytes 479240 | tf_op jit(solution)/shard_map/ppermute | solution.py:476
  41.5 11.1 %collective-permute-start.14 = (s16[208,384]{1,0:T(8,128)(2,1)S(1)}, s16[208,384]{1,0:T(8,128)(2,1)S(1)}, u32[]{:S(2)}, u32[]{:S(2)}) collective-permute-start(s16[208,384]{1,0:T(8,128)(2,1)S(1)} %get-tuple-element.59), channel_id=1, source_target_pairs={{0,8},{4,12},{8,0},{12,4},{1,9},{5,13},{9,1},{13,5},{2,10},{6,14},... | collective-permute-start | bytes 479240 | tf_op jit(solution)/shard_map/ppermute | solution.py:476
  44.2 8.5 %copy-start.6 = (s32[32,1]{0,1:T(1,128)S(1)}, s32[32,1]{0,1:T(1,128)}, u32[]{:S(2)}) copy-start(s32[32,1]{0,1:T(1,128)} %param.7) | copy-start | bytes 388
  44.2 8.5 %collective-permute-start.15 = (s16[208,384]{1,0:T(8,128)(2,1)S(1)}, s16[208,384]{1,0:T(8,128)(2,1)S(1)}, u32[]{:S(2)}, u32[]{:S(2)}) collective-permute-start(s16[208,384]{1,0:T(8,128)(2,1)S(1)} %get-tuple-element.60), channel_id=1, source_target_pairs={{0,12},{4,8},{8,4},{12,0},{1,13},{5,9},{9,5},{13,1},{2,14},{6,10},... | collective-permute-start | bytes 479240 | tf_op jit(solution)/shard_map/ppermute | solution.py:476
  54.1 16.3 %copy-start.4 = (f32[8,64,128]{2,1,0:T(8,128)S(1)}, f32[8,64,128]{2,1,0:T(8,128)}, u32[]{:S(2)}) copy-start(f32[8,64,128]{2,1,0:T(8,128)} %weight.3) | copy-start | bytes 786436
  54.8 16.9 %collective-permute-start.16 = (f32[4,192,192]{2,1,0:T(8,128)S(1)}, f32[4,192,192]{2,1,0:T(8,128)S(1)}, u32[]{:S(2)}, u32[]{:S(2)}) collective-permute-start(f32[4,192,192]{2,1,0:T(8,128)S(1)} %get-tuple-element.63), channel_id=1, source_target_pairs={{0,1},{1,0},{2,3},{3,2},{16,17},{17,16},{18,19},{19,18},{4,5},{5,4... | collective-permute-start | bytes 1769480 | tf_op jit(solution)/shard_map/ppermute | solution.py:437
  54.9 4.4 %collective-permute-start.17 = (s16[240,128]{1,0:T(8,128)(2,1)S(1)}, s16[240,128]{1,0:T(8,128)(2,1)S(1)}, u32[]{:S(2)}, u32[]{:S(2)}) collective-permute-start(s16[240,128]{1,0:T(8,128)(2,1)S(1)} %get-tuple-element.66), channel_id=1, source_target_pairs={{0,2},{1,3},{2,0},{3,1},{16,18},{17,19},{18,16},{19,17},{4,6},{5,7... | collective-permute-start | bytes 184328 | tf_op jit(solution)/shard_map/ppermute | solution.py:437
  55.6 4.2 %collective-permute-start.18 = (s16[240,128]{1,0:T(8,128)(2,1)S(1)}, s16[240,128]{1,0:T(8,128)(2,1)S(1)}, u32[]{:S(2)}, u32[]{:S(2)}) collective-permute-start(s16[240,128]{1,0:T(8,128)(2,1)S(1)} %get-tuple-element.67), channel_id=1, source_target_pairs={{0,16},{1,17},{2,18},{3,19},{16,0},{17,1},{18,2},{19,3},{4,20},{5,... | collective-permute-start | bytes 184328 | tf_op jit(solution)/shard_map/ppermute | solution.py:437
  57.0 5.1 %collective-permute-start.19 = (s16[240,128]{1,0:T(8,128)(2,1)S(1)}, s16[240,128]{1,0:T(8,128)(2,1)S(1)}, u32[]{:S(2)}, u32[]{:S(2)}) collective-permute-start(s16[240,128]{1,0:T(8,128)(2,1)S(1)} %get-tuple-element.68), channel_id=1, source_target_pairs={{0,18},{1,19},{2,16},{3,17},{16,2},{17,3},{18,0},{19,1},{4,22},{5,... | collective-permute-start | bytes 184328 | tf_op jit(solution)/shard_map/ppermute | solution.py:437
  63.3 4.7 %collective-permute-start.20 = (bf16[240,128]{1,0:T(8,128)(2,1)S(1)}, bf16[240,128]{1,0:T(8,128)(2,1)S(1)}, u32[]{:S(2)}, u32[]{:S(2)}) collective-permute-start(bf16[240,128]{1,0:T(8,128)(2,1)S(1)} %newton_schulz.1.refs_0_), channel_id=1, source_target_pairs={{0,2},{1,3},{2,0},{3,1},{16,18},{17,19},{18,16},{19,17},{4,6},{5,7... | collective-permute-start | bytes 184328 | tf_op jit(solution)/shard_map/ppermute | solution.py:437
  64.8 4.2 %collective-permute-start.21 = (bf16[240,128]{1,0:T(8,128)(2,1)S(1)}, bf16[240,128]{1,0:T(8,128)(2,1)S(1)}, u32[]{:S(2)}, u32[]{:S(2)}) collective-permute-start(bf16[240,128]{1,0:T(8,128)(2,1)S(1)} %newton_schulz.1.refs_0_), channel_id=1, source_target_pairs={{0,16},{1,17},{2,18},{3,19},{16,0},{17,1},{18,2},{19,3},{4,20},{5,... | collective-permute-start | bytes 184328 | tf_op jit(solution)/shard_map/ppermute | solution.py:437
  65.3 5.1 %collective-permute-start.22 = (bf16[240,128]{1,0:T(8,128)(2,1)S(1)}, bf16[240,128]{1,0:T(8,128)(2,1)S(1)}, u32[]{:S(2)}, u32[]{:S(2)}) collective-permute-start(bf16[240,128]{1,0:T(8,128)(2,1)S(1)} %newton_schulz.1.refs_0_), channel_id=1, source_target_pairs={{0,18},{1,19},{2,16},{3,17},{16,2},{17,3},{18,0},{19,1},{4,22},{5,... | collective-permute-start | bytes 184328 | tf_op jit(solution)/shard_map/ppermute | solution.py:437
  66.8 6.2 %collective-permute-start.23 = (bf16[240,128]{1,0:T(8,128)(2,1)S(1)}, bf16[240,128]{1,0:T(8,128)(2,1)S(1)}, u32[]{:S(2)}, u32[]{:S(2)}) collective-permute-start(bf16[240,128]{1,0:T(8,128)(2,1)S(1)} %newton_schulz.1.refs_0_), channel_id=1, source_target_pairs={{0,1},{1,0},{2,3},{3,2},{16,17},{17,16},{18,19},{19,18},{4,5},{5,4... | collective-permute-start | bytes 184328 | tf_op jit(solution)/shard_map/ppermute | solution.py:437
  68.0 4.9 %collective-permute-start.24 = (bf16[240,128]{1,0:T(8,128)(2,1)S(1)}, bf16[240,128]{1,0:T(8,128)(2,1)S(1)}, u32[]{:S(2)}, u32[]{:S(2)}) collective-permute-start(bf16[240,128]{1,0:T(8,128)(2,1)S(1)} %collective-permute-done.20.refs_1_), channel_id=1, source_target_pairs={{0,1},{1,0},{2,3},{3,2},{16,17},{17,16},{18,19},{19,18},{4,5},{5,4... | collective-permute-start | bytes 184328 | tf_op jit(solution)/shard_map/ppermute | solution.py:437
  69.0 4.0 %collective-permute-start.25 = (bf16[240,128]{1,0:T(8,128)(2,1)S(1)}, bf16[240,128]{1,0:T(8,128)(2,1)S(1)}, u32[]{:S(2)}, u32[]{:S(2)}) collective-permute-start(bf16[240,128]{1,0:T(8,128)(2,1)S(1)} %collective-permute-done.21.refs_2_), channel_id=1, source_target_pairs={{0,1},{1,0},{2,3},{3,2},{16,17},{17,16},{18,19},{19,18},{4,5},{5,4... | collective-permute-start | bytes 184328 | tf_op jit(solution)/shard_map/ppermute | solution.py:437
  70.4 2.6 %collective-permute-start.26 = (bf16[240,128]{1,0:T(8,128)(2,1)S(1)}, bf16[240,128]{1,0:T(8,128)(2,1)S(1)}, u32[]{:S(2)}, u32[]{:S(2)}) collective-permute-start(bf16[240,128]{1,0:T(8,128)(2,1)S(1)} %collective-permute-done.22.refs_3_), channel_id=1, source_target_pairs={{0,1},{1,0},{2,3},{3,2},{16,17},{17,16},{18,19},{19,18},{4,5},{5,4... | collective-permute-start | bytes 184328 | tf_op jit(solution)/shard_map/ppermute | solution.py:437
  71.7 2.0 %copy-start.3 = (f32[8,192,192]{2,1,0:T(8,128)S(1)}, f32[8,192,192]{2,1,0:T(8,128)}, u32[]{:S(2)}) copy-start(f32[8,192,192]{2,1,0:T(8,128)} %weight.2) | copy-start | bytes 3538948
  73.7 1.4 %copy-start.2 = (f32[8,192,192]{2,1,0:T(8,128)S(1)}, f32[8,192,192]{2,1,0:T(8,128)}, u32[]{:S(2)}) copy-start(f32[8,192,192]{2,1,0:T(8,128)} %merge_momentum.1.momentum) | copy-start | bytes 3538948

commit v3 on v2

v3 whole, which is shorter than its diff:
```python
import functools
import math

import jax
import jax.numpy as jnp
from jax import lax
from jax.experimental import pallas as pl
from jax.experimental.pallas import tpu as pltpu
from jax.sharding import PartitionSpec as P

ITERS = 2
MOMENTUM_RATE = 0.95
WEIGHT_KEEP = 0.98
LOGIT_CAP = 100.0
QUINTIC_A = 3.4445
QUINTIC_B = -4.775
QUINTIC_C = 2.0315

CORES = 2
PLANE = ("dp", "context")
SCALE_ROWS = 16
LEVELS = 14.99
STEPS = 8.0
NOTE_UNITS = (64.0, 64.0 * 32768.0, 64.0 * 32768.0 * 32768.0)
GROUPS = 4
LEFT = 128

SMEM = pl.BlockSpec(memory_space=pltpu.SMEM)
VMEM = pl.BlockSpec(memory_space=pltpu.VMEM)
ANY = pl.BlockSpec(memory_space=pl.ANY)
HBM = pl.BlockSpec(memory_space=pltpu.HBM)
PARAMS = pltpu.CompilerParams(vmem_limit_bytes=36 * 1024 * 1024)
FIRST = pltpu.CompilerParams(vmem_limit_bytes=52 * 1024 * 1024)
SECOND = pltpu.CompilerParams(vmem_limit_bytes=44 * 1024 * 1024)


def whereabouts():
    device = lax.axis_index("dp") * lax.axis_size("context") + lax.axis_index("context")
    return lax.axis_index("owner"), device // CORES, device % CORES


def call(kernel, name, ins, outs, scratch=(), after=(), aliases=None, params=PARAMS):
    count = len(ins)

    def whole(*refs):
        kernel(*refs[:count], *refs[count + len(after) :])

    return pl.pallas_call(
        whole,
        in_specs=[spec for spec, _ in ins] + [ANY] * len(after),
        out_specs=[spec for spec, _, _ in outs],
        out_shape=[jax.ShapeDtypeStruct(shape, dtype) for _, shape, dtype in outs],
        scratch_shapes=list(scratch),
        input_output_aliases=aliases or {},
        compiler_params=params,
        name=name,
    )(*[array for _, array in ins], *after)


def head_of(assignment, block, who, place, heads_own):
    found, seen = 0, 0
    for i in range(heads_own):
        hit = (assignment[0, block * heads_own + i] == who).astype(jnp.int32)
        found = jnp.where((hit == 1) & (seen == place), i, found)
        seen = seen + hit
    return found, seen


def encode(parts, out, note=None):
    top = functools.reduce(jnp.maximum, [jnp.max(jnp.abs(p), axis=0, keepdims=True) for p in parts])
    level = jnp.clip(jnp.ceil(STEPS * jnp.log2(top)), -100.0 * STEPS, 128.0 * STEPS)
    factor = jnp.exp2(LEVELS - level * (1.0 / STEPS))
    at = 0
    for p in parts:
        out[at : at + p.shape[0]] = jnp.round(p * factor).astype(jnp.int32).astype(jnp.int16)
        at += p.shape[0]
    rows = jnp.broadcast_to(level, (SCALE_ROWS, level.shape[1]))
    if note is not None:
        row = lax.broadcasted_iota(jnp.int32, rows.shape, 0)
        rest = note * NOTE_UNITS[0]
        for i, unit in enumerate(NOTE_UNITS):
            whole = jnp.floor(rest)
            rows = jnp.where(row == i + 1, whole, rows)
            rest = (rest - whole) * 32768.0
    out[at:] = rows.astype(jnp.int32).astype(jnp.int16)


def noted(block, width):
    rows = block[block.shape[0] - SCALE_ROWS :].astype(jnp.int32).astype(jnp.float32)
    parts = [rows[i + 1 : i + 2, :width] / unit for i, unit in enumerate(NOTE_UNITS)]
    return parts[0] + (parts[1] + parts[2])


def decode(block, count):
    size = (block.shape[0] - SCALE_ROWS) // count
    level = block[size * count :].astype(jnp.int32).astype(jnp.float32)[0:1]
    factor = jnp.exp2(level * (1.0 / STEPS) - LEVELS)
    return [
        block[i * size : (i + 1) * size].astype(jnp.int32).astype(jnp.float32) * factor
        for i in range(count)
    ]


def fetch_kernel(heads_own, wanted, assignment, g, *refs):
    owner, _, core = whereabouts()
    token, outs, sem = refs[-2], refs[:-2], refs[-1]
    token[...] = jnp.zeros_like(token)
    copies = []
    for group, out in zip(wanted, outs[-len(wanted) :]):
        for i, (k, other) in enumerate(group):
            place = 1 - core if other else core
            head, _ = head_of(assignment, owner, owner ^ k, place, heads_own)
            copies.append(pltpu.make_async_copy(g.at[head], out.at[i], sem.at[len(copies)]))
            copies[-1].start()
    if len(outs) > len(wanted):
        momentum, logits, old = outs[:3]
        cols = momentum.shape[2]
        for s in range(old.shape[0]):
            old[s, :, :cols] = momentum[s * CORES + 1 - core]
        old[0, 0:1, cols : cols + logits.shape[1]] = logits[...]
    for copy in copies:
        copy.wait()


def fetch(assignment, g, wanted, rest=(), after=()):
    outs = [(VMEM, (len(group),) + g.shape[1:], g.dtype) for group in wanted]
    count = sum(len(group) for group in wanted)
    ins = [(SMEM, assignment), (ANY, g)]
    outs.append((VMEM, (8, LEFT), jnp.float32))
    if rest:
        momentum, logits = rest
        slots, rows, _ = momentum.shape
        outs = [(VMEM, (slots // CORES, rows, 2 * LEFT), momentum.dtype)] + outs
        ins += [(VMEM, momentum), (VMEM, logits)]
    return call(
        functools.partial(fetch_kernel, g.shape[0], wanted),
        "fetch_heads",
        ins,
        outs,
        [pltpu.SemaphoreType.DMA((count,))],
        after,
        params=SECOND if after else FIRST,
    )


def pair_kernel(chips, aligned, heads, passed, own, sibling, *refs):
    _, chip, _ = whereabouts()
    note = None
    refs = refs[passed : len(refs) - passed] if passed else refs
    if len(refs) > chips:
        logits, padded = refs[0], refs[-1]
        padded[...] = jnp.zeros_like(padded)
        padded[:, : logits.shape[1]] = logits[...]
        note, refs = padded[...], refs[1:-1]
    here, away = refs[0], refs[1:]
    width = here.shape[-1]
    for k in range(chips):
        to = chip ^ k
        blocks = []
        for mine, theirs in heads:
            if aligned:
                rows = pl.ds(pl.multiple_of(to * width, 128), width)
                first, second = own[mine, :, rows], sibling[theirs, :, rows]
            else:
                first, second = own[mine, to], sibling[theirs, to]
            blocks.append(first.astype(jnp.float32) + second.astype(jnp.float32))
        if k == 0:
            for i, block in enumerate(blocks):
                here[i] = block
        else:
            encode(blocks, away[k - 1], note if k == 1 else None)


def pair_sums(own, sibling, heads, chips, after, note, passed):
    aligned = own.ndim == 3
    cols = own.shape[-2]
    width = own.shape[-1] // chips if aligned else own.shape[-1]
    coded = (VMEM, (len(heads) * cols + SCALE_ROWS, width), jnp.int16)
    outs = [(VMEM, (len(heads), cols, width), jnp.float32)] + [coded] * (chips - 1)
    return call(
        functools.partial(pair_kernel, chips, aligned, heads, len(passed)),
        "pair_sum",
        [(VMEM, own), (VMEM, sibling)]
        + [(ANY, value) for value in passed]
        + [(VMEM, value) for value in note],
        outs + [(ANY, value.shape, value.dtype) for value in passed],
        [pltpu.VMEM((1, width), jnp.float32) for _ in note],
        after=after,
        aliases={2 + i: chips + i for i in range(len(passed))},
    )


def plane_kernel(plain, noting, here, *refs):
    outs = refs[-len(plain) - noting :]
    away = refs[: len(refs) - len(outs)]
    if noting:
        logits, away = away[-1], away[:-1]
        peak, outs = outs[-1], outs[:-1]
        peak[...] = jnp.maximum(logits[...], noted(away[0], logits.shape[1]))
    blocks = [here[i] for i in range(len(plain))]
    for value in away:
        blocks = [a + b for a, b in zip(blocks, decode(value, len(plain)))]
    for is_plain, block, out in zip(plain, blocks, outs):
        if is_plain:
            out[...] = block
        else:
            encode([block], out)


def plane_sums(here, away, plain, after, note):
    _, cols, width = here.shape
    coded = (VMEM, (cols + SCALE_ROWS, width), jnp.int16)
    outs = [(VMEM, (cols, width), jnp.float32) if p else coded for p in plain]
    return call(
        functools.partial(plane_kernel, plain, len(note)),
        "plane_sum",
        [(VMEM, value) for value in (here, *away, *note)],
        outs + [(VMEM, value.shape, value.dtype) for value in note],
        after=after,
    )


def turn_kernel(own, sibling, logits, out, peak, both):
    _, _, core = whereabouts()
    rows = own.shape[1]
    for s in range(sibling.shape[0]):
        both[pl.ds(pl.multiple_of(core * rows, 16), rows)] = own[s * CORES + core]
        both[pl.ds(pl.multiple_of((1 - core) * rows, 16), rows)] = sibling[s, :, : own.shape[2]]
        out[s] = both[...].T
    cols = own.shape[2]
    peak[...] = jnp.maximum(logits[...], sibling[0, 0:1, cols : cols + logits.shape[1]])


def turn(own, sibling, logits):
    sources = sibling.shape[0]
    _, rows, cols = own.shape
    return call(
        turn_kernel,
        "turn_momentum",
        [(VMEM, own), (VMEM, sibling), (VMEM, logits)],
        [(VMEM, (sources, cols, CORES * rows), jnp.float32), (VMEM, logits.shape, logits.dtype)],
        [pltpu.VMEM((CORES * rows, cols), jnp.float32)],
    )


def pack(matrix, out):
    cols = matrix.shape[0]
    rest = cols - LEFT
    out[:cols] = matrix[:, :LEFT].astype(out.dtype)
    for f in range(2):
        part = matrix[LEFT + f * rest // 2 : LEFT + (f + 1) * rest // 2, LEFT:]
        out[cols : cols + rest // 2, f * rest : (f + 1) * rest] = part.astype(out.dtype)


def unpack(packed, out):
    cols = out.shape[0]
    rest = cols - LEFT
    out[:, :LEFT] = packed[:cols]
    out[:LEFT, LEFT:] = packed[LEFT:cols].astype(jnp.float32).T.astype(out.dtype)
    for f in range(2):
        part = packed[cols : cols + rest // 2, f * rest : (f + 1) * rest]
        out[LEFT + f * rest // 2 : LEFT + (f + 1) * rest // 2, LEFT:] = part


def gram_kernel(chips, heads_own, assignment, old, near, *refs):
    sources = old.shape[0]
    arrived, refs = refs[: sources - 1], refs[sources - 1 :]
    (new, here), away, packed = refs[:2], refs[2:-1], refs[-1]
    owner, chip, core = whereabouts()
    for k in range(sources):
        source = owner ^ k
        grad = near[...] if k == 0 else decode(arrived[k - 1], 1)[0]
        kept = old[source]
        _, held = head_of(assignment, source, owner, 0, heads_own)
        new[source] = jnp.where(held > core, MOMENTUM_RATE * kept + grad, kept)
    for k in range(chips):
        value = new[lax.rem(chip ^ k, sources)].astype(jnp.bfloat16)
        gram = lax.dot_general(
            value, value, (((1,), (1,)), ((), ())), preferred_element_type=jnp.float32
        )
        if k == 0:
            pack(gram, here)
        else:
            pack(gram, packed)
            encode([packed[...]], away[k - 1])


def grams(assignment, old, near, arrived, chips, heads_own, after):
    cols = old.shape[1]
    rows = cols + (cols - LEFT) // 2
    coded = (VMEM, (rows + SCALE_ROWS, LEFT), jnp.int16)
    return call(
        functools.partial(gram_kernel, chips, heads_own),
        "refresh_and_gram",
        [(SMEM, assignment)] + [(VMEM, value) for value in (old, near, *arrived)],
        [(VMEM, old.shape, jnp.float32), (VMEM, (rows, LEFT), jnp.float32)] + [coded] * (chips - 1),
        [pltpu.VMEM((rows, LEFT), jnp.float32)],
        after,
    )


def small_dot(a, b):
    return lax.dot_general(
        a.astype(jnp.bfloat16), b.astype(jnp.bfloat16), (((1,), (0,)), ((), ())),
        preferred_element_type=jnp.float32,
    )


def newton_kernel(here, *refs):
    away, (out, square) = refs[:-2], refs[-2:]
    cols = square.shape[0]
    total = here[...]
    for block in away:
        total = total + decode(block, 1)[0]
    unpack(total, square)
    gram = square[...]
    row = lax.broadcasted_iota(jnp.int32, gram.shape, 0)
    column = lax.broadcasted_iota(jnp.int32, gram.shape, 1)
    square_sum = jnp.sum(jnp.where(row == column, gram, 0.0), axis=(0, 1), keepdims=True)
    norm = jnp.sqrt(square_sum) + 1e-07
    inverse = 1.0 / norm
    gram = jnp.where(norm < jnp.inf, gram * inverse * inverse, 0.0)
    first = QUINTIC_B * gram + QUINTIC_C * small_dot(gram, gram)
    twice = (2.0 * QUINTIC_A) * first + small_dot(first, first)
    gram = (QUINTIC_A * QUINTIC_A) * gram + small_dot(gram, twice)
    second = QUINTIC_B * gram + QUINTIC_C * small_dot(gram, gram)
    result = QUINTIC_A * (first + second) + small_dot(first, second)
    pack(result, out)
    high = norm.astype(jnp.bfloat16).astype(jnp.float32)
    middle = (norm - high).astype(jnp.bfloat16).astype(jnp.float32)
    low = norm - high - middle
    row = lax.broadcasted_iota(jnp.int32, (SCALE_ROWS, LEFT), 0)
    scales = jnp.where(row == 0, high, jnp.where(row == 1, middle, jnp.where(row == 2, low, 0.0)))
    out[out.shape[0] - SCALE_ROWS :] = scales.astype(jnp.bfloat16)


def newton(here, away, cols, after):
    (out,) = call(
        newton_kernel,
        "newton_schulz",
        [(VMEM, value) for value in (here, *away)],
        [(VMEM, (here.shape[0] + SCALE_ROWS, LEFT), jnp.bfloat16)],
        [pltpu.VMEM((cols, cols), jnp.float32)],
        after,
    )
    return out


def back_kernel(new, own, sibling, both):
    _, _, core = whereabouts()
    rows = own.shape[1]
    for s in range(own.shape[0]):
        both[...] = new[s].T
        own[s] = both[pl.ds(pl.multiple_of(core * rows, 16), rows)]
        sibling[s] = both[pl.ds(pl.multiple_of((1 - core) * rows, 16), rows)]


def turn_back(new, after):
    sources, cols, width = new.shape
    half = (VMEM, (sources, width // CORES, cols), jnp.float32)
    return call(
        back_kernel,
        "turn_back",
        [(VMEM, new)],
        [half, half],
        [pltpu.VMEM((width, cols), jnp.float32)],
        after,
    )


def head_scale(peak, head, shape):
    return jnp.minimum(1.0, LOGIT_CAP / jnp.full(shape, peak[0, head], jnp.float32))


def base_kernel(heads_own, kn_count, assignment, peak, weight, out, scales):
    owner, _, _ = whereabouts()
    slots, _, cols = weight.shape
    column = lax.broadcasted_iota(jnp.int32, (1, cols), 1)
    for slot in range(slots):
        source, place = slot // CORES, slot % CORES
        head, held = head_of(assignment, source, owner, place, heads_own)
        gamma = head_scale(peak, source * heads_own + head, (1, cols))
        scale = jnp.where(column < kn_count, jnp.sqrt(gamma), gamma)
        old = weight[slot]
        out[slot] = jnp.where(held > place, (WEIGHT_KEEP * old) * scale, old)
        scales[slot : slot + 1] = jnp.where(held > place, scale, 0.0)


def bases(assignment, peak, weight, heads_own, kn_count):
    slots, _, cols = weight.shape
    return call(
        functools.partial(base_kernel, heads_own, kn_count),
        "scale_weight",
        [(SMEM, assignment), (SMEM, peak), (VMEM, weight)],
        [(VMEM, weight.shape, jnp.float32), (VMEM, (slots, cols), jnp.float32)],
    )


def weight_kernel(chips, other, rows_all, base, scales, momentum, *refs):
    blocks, refs = refs[:chips], refs[chips:]
    out, matrix, result, sem = refs[-4:]
    slots, _, cols = base.shape
    sources = slots // CORES
    step_size = 0.04 * math.sqrt(max(rows_all, cols))
    _, chip, core = whereabouts()
    place = 1 - core if other else core
    def written(k):
        return pltpu.make_async_copy(result.at[k], out.at[(chip ^ k) * CORES + place], sem.at[k])

    def update(k):
        source = chip ^ k
        slot = source * CORES + place
        block = blocks[k]
        parts = block[block.shape[0] - SCALE_ROWS :].astype(jnp.float32)
        norm = parts[0:1, 0:1] + parts[1:2, 0:1] + parts[2:3, 0:1]
        unpack(block[: block.shape[0] - SCALE_ROWS], matrix.at[k])
        start = (momentum[source] * (1.0 / norm)).astype(jnp.bfloat16)
        step = (QUINTIC_A * QUINTIC_A) * start.astype(jnp.float32) + small_dot(start, matrix[k])
        result[k] = base[slot] - step * (step_size * scales[pl.ds(slot, 1)])
        written(k).start()

    def only(k, act):
        if sources == chips:
            act()
        else:
            pl.when((chip ^ k) < sources)(act)

    for k in range(chips):
        only(k, functools.partial(update, k))
    for k in range(chips):
        only(k, lambda k=k: written(k).wait())


def weights(base, scales, momentum, blocks, filled=None, after=()):
    chips = len(blocks)
    slots, rows, cols = base.shape
    other = filled is not None
    ins = [(VMEM, value) for value in (base, scales, momentum, *blocks)]
    aliases = None
    if other:
        aliases = {len(ins): 0}
        ins.append((HBM, filled))
    (out,) = call(
        functools.partial(weight_kernel, chips, other, rows * chips * CORES),
        "update_weight",
        ins,
        [(HBM, base.shape, jnp.float32)],
        [
            pltpu.VMEM((chips, cols, cols), jnp.bfloat16),
            pltpu.VMEM((chips, rows, cols), jnp.float32),
            pltpu.SemaphoreType.DMA((chips,)),
        ],
        after,
        aliases,
    )
    return out


def merge_kernel(own, sibling, out, token, sem):
    token[...] = jnp.zeros_like(token)
    _, _, core = whereabouts()
    copies = []
    for s in range(own.shape[0]):
        for half, place in ((own, core), (sibling, 1 - core)):
            to = out.at[s * CORES + place]
            copies.append(pltpu.make_async_copy(half.at[s], to, sem.at[len(copies)]))
            copies[-1].start()
    for copy in copies:
        copy.wait()


def merge(own, sibling):
    sources, rows, cols = own.shape
    return call(
        merge_kernel,
        "merge_momentum",
        [(VMEM, own), (VMEM, sibling)],
        [(HBM, (sources * CORES, rows, cols), jnp.float32), (VMEM, (8, LEFT), jnp.float32)],
        [pltpu.SemaphoreType.DMA((sources * CORES,))],
    )


def key_kernel(peak, weight, out):
    owner, _, _ = whereabouts()
    heads_own, _, cols = weight.shape
    for i in range(heads_own):
        gamma = head_scale(peak, owner * heads_own + i, (1, cols))
        out[i] = weight[i] * jnp.sqrt(gamma)


def keys(peak, weight):
    (out,) = call(
        key_kernel,
        "scale_keys",
        [(SMEM, peak), (VMEM, weight)],
        [(VMEM, weight.shape, jnp.float32)],
    )
    return out


def body(grad_partials, assignment, momentum, q_weight, k_weight, max_logits):
    heads_own = grad_partials.shape[2]
    sources = lax.axis_size("owner")
    devices = lax.axis_size("dp") * lax.axis_size("context")
    chips = devices // CORES
    assignment = assignment.T

    def swap(value, bits):
        return lax.ppermute(value, PLANE, [(i, i ^ bits) for i in range(devices)])

    g = jnp.transpose(grad_partials[0], (1, 2, 0))
    if (g.shape[2] // chips) % 128:
        g = jnp.transpose(g.reshape(g.shape[:2] + (chips, g.shape[2] // chips)), (0, 2, 1, 3))
    order = list(range(sources))[::-1]
    size = max(1, sources // GROUPS)
    groups = [order[at : at + size] for at in range(0, sources, size)]
    first, token = fetch(assignment, g, [[(k, True) for k in groups[0]]])
    wanted = [[(k, True) for k in order[size:]], [(k, False) for k in groups[0]]]
    old, others, *own, _ = fetch(assignment, g, wanted, (momentum, max_logits), [token])
    siblings = [swap(first, 1)]

    near, arrived, before, sent = None, {}, [], []
    for i, ks in enumerate(groups):
        heads = [(j, j + (size * (i - 1) if i else 0)) for j in range(len(ks))]
        passed = [others, old] if i == 0 else []
        note = [peak] if i == len(groups) - 2 else []
        values = pair_sums(own[i], siblings[min(i, 1)], heads, chips, before, note, passed)
        here, away = values[0], values[1:chips]
        if i == 0:
            others, old = values[chips:]
            wanted = [[(k, False) for k in ks] for ks in groups[1:]]
            own += fetch(assignment, g, wanted, after=[away[0]])
            siblings.append(swap(others, 1))
            turned, peak = turn(momentum, swap(old, 1), max_logits)
        away = [swap(value, CORES * (k + 1)) for k, value in enumerate(away)]
        before = away[:2] if i else [away[0], turned]
        totals = list(plane_sums(here, away, [k == 0 for k in ks], sent, note))
        if note:
            peak = totals.pop()
            base, scales = bases(assignment, peak, q_weight, heads_own, k_weight.shape[2])
            k_weight_out = keys(peak, k_weight)
        sent = []
        for k, total in zip(ks, totals):
            if k == 0:
                near = total
            else:
                arrived[k] = lax.ppermute(total, "owner", [(j, j ^ k) for j in range(sources)])
                sent.append(arrived[k])
        if note:
            sent += [base, k_weight_out]

    arrived = [arrived[k] for k in range(1, sources)]
    new, here, *away = grams(assignment, turned, near, arrived, chips, heads_own, [])
    away = [swap(value, CORES * (k + 1)) for k, value in enumerate(away)]
    result = newton(here, away, momentum.shape[2], [])
    own_new, sibling_new = turn_back(new, [result])

    sibling_new = swap(sibling_new, 1)
    results = [result] + [swap(result, CORES * k) for k in range(1, chips)]
    sibling_results = [swap(value, 1) for value in results]
    momentum_out, token = merge(own_new, sibling_new)
    q_weight_out = weights(base, scales, own_new, results, after=[token])
    q_weight_out = weights(base, scales, sibling_new, sibling_results, q_weight_out)
    return (momentum_out, q_weight_out, k_weight_out)


def solution(mesh):
    rows = P("owner", ("dp", "context"), None)
    return jax.shard_map(
        body,
        mesh=mesh,
        in_specs=(
            P(("dp", "context"), None, "owner", None),
            P(),
            rows,
            rows,
            rows,
            P("context", None),
        ),
        out_specs=(rows, rows, rows),
        check_vma=False,
    )
```

time: 78.8 us -> 67.1 us (0.85); the launches traced: 77.6 us -> 66.9 us
  waiting for transfers between devices: 32.2 us -> 17.5 us
  starting transfers between devices: 25 us -> 29.4 us
  local copies, waits for them, and re-layouts: 4.17 us -> 2.14 us
  Pallas kernels: 15.4 us -> 17 us
    ppermute x22 -> x26, starting transfers between devices: 16.3 us -> 25.1 us  [swap(): return lax.ppermute(value, PLANE, [(i, i ^ bits) for i in range(devices)])]
    ppermute x22 -> x26, waiting for transfers between devices: 22 us -> 14.7 us  [swap(): return lax.ppermute(value, PLANE, [(i, i ^ bits) for i in range(devices)])]
    ppermute x2 -> x0, waiting for transfers between devices: 3.84 us -> none  [body(): peak = jnp.maximum(peak, lax.ppermute(peak, 'context', perm))]
    ppermute x3, waiting for transfers between devices: 6.37 us -> 2.83 us  [body(): lax.ppermute(total, 'owner', [(j, j ^ k) for j in range(sources)])]
    ppermute x2 -> x0, starting transfers between devices: 3.09 us -> none  [body(): peak = jnp.maximum(peak, lax.ppermute(peak, 'context', perm))]
    unnamed x16 -> x18, local copies, waits for them, and re-layouts: 4.17 us -> 2.14 us
    pallas_call x15 -> x20, Pallas kernels: 15.4 us -> 17 us  [call(): pl.pallas_call(whole, in_specs=[spec for spec, _ in ins] + [ANY] * len(af...]
    ppermute x3, starting transfers between devices: 5.64 us -> 4.39 us  [body(): lax.ppermute(total, 'owner', [(j, j ^ k) for j in range(sources)])]
  transfers between devices with their start and end apart: 27 -> 29, of which waited for: 16 -> 15; matrix products, arithmetic and copies ran while one was open for 0% -> 0% of each run, Pallas kernels for 10% -> 15%
where the time goes in v3:
time: 67.1 us; the launch traced here: 66.9 us
  starting transfers between devices  29.4 us (44%)
  waiting for transfers between devices  17.5 us (26%)
  Pallas kernels  17 us (25%)
  local copies, waits for them, and re-layouts  2.14 us (3%)
  between operations  0.87 us (1%)
    ppermute x26, starting transfers between devices, swap(): return lax.ppermute(value, PLANE, [(i, i ^ bits) for i in range(devices)])  25.1 us
    pallas_call x20, Pallas kernels, call(): pl.pallas_call(whole, in_specs=[spec for spec, _ in ins] + [ANY] * len(af...  17 us
    ppermute x26, waiting for transfers between devices, swap(): return lax.ppermute(value, PLANE, [(i, i ^ bits) for i in range(devices)])  14.7 us
    ppermute x3, starting transfers between devices, body(): lax.ppermute(total, 'owner', [(j, j ^ k) for j in range(sources)])  4.39 us
    ppermute x3, waiting for transfers between devices, body(): lax.ppermute(total, 'owner', [(j, j ^ k) for j in range(sources)])  2.83 us
    unnamed x18, local copies, waits for them, and re-layouts  2.14 us
  transfers between devices with their start and end apart: 29, of which 15 were waited for; matrix products, arithmetic and copies ran while one was open for 0% of the time, Pallas kernels for 15%

profile of v3, /device:TPU:0, one launch (start us, length us, event | category | flops | bytes accessed | tf_op | source)
XLA Modules:
  0.0 66.9 jit_solution(11628735218216098726)
XLA Ops:
  0.6 0.6 copy-done.6
  1.3 1.9 %fetch_heads.3 = (bf16[1,192,1536]{2,1,0:T(8,128)(2,1)S(1)}, f32[8,128]{1,0:T(8,128)S(1)}) custom-call(s32[1,32]{1,0:T(1,128)S(1)} %bitcast.7, bf16[8,192,1536]{2,1,0:T(8,128)(2,1)} %bitcast.4), custom_call_target="tpu_custom_call" | custom-call | tf_op jit(solution)/shard_map/fetch_heads/pallas_call | solution.py:48
  3.2 0.5 collective-permute-start
  3.7 0.1 copy-done
  3.8 1.4 %copy-done.1 = f32[8,192,192]{2,1,0:T(8,128)S(1)} copy-done((f32[8,192,192]{2,1,0:T(8,128)S(1)}, f32[8,192,192]{2,1,0:T(8,128)}, u32[]{:S(2)}) %copy-start.1) | copy-done | bytes 1179672
  5.2 1.8 %fetch_heads.4 = (f32[4,192,256]{2,1,0:T(8,128)S(1)}, bf16[3,192,1536]{2,1,0:T(8,128)(2,1)S(1)}, bf16[1,192,1536]{2,1,0:T(8,128)(2,1)S(1)}, f32[8,128]{1,0:T(8,128)}) custom-call(s32[1,32]{1,0:T(1,128)S(1)} %bitcast.8, bf16[8,192,1536]{2,1,0:T(8,128)(2,1)S(1)} %bitcast.5, f32[8,192,192]{2,1,0:T(8,128)S(1)} %copy-done.1, f32[1,32]{1,0:T(1,128)S(1)} %copy-done.8, ...), custom_call_target="tpu_custom_call" | custom-call | tf_op jit(solution)/shard_map/fetch_heads/pallas_call | solution.py:48
  7.1 0.3 pair_sum.4
  7.4 0.5 collective-permute-start.2
  7.9 0.1 collective-permute-start.1
  8.0 2.9 %collective-permute-start.3 = (s16[208,384]{1,0:T(8,128)(2,1)S(1)}, s16[208,384]{1,0:T(8,128)(2,1)S(1)}, u32[]{:S(2)}, u32[]{:S(2)}) collective-permute-start(s16[208,384]{1,0:T(8,128)(2,1)S(1)} %get-tuple-element.51.refs_2_), channel_id=1, source_target_pairs={{0,2},{1,3},{2,0},{3,1},{16,18},{17,19},{18,16},{19,17},{4,6},{5,7... | collective-permute-start | bytes 479240 | tf_op jit(solution)/shard_map/ppermute | solution.py:509
  10.9 1.5 %collective-permute-start.13 = (s16[208,384]{1,0:T(8,128)(2,1)S(1)}, s16[208,384]{1,0:T(8,128)(2,1)S(1)}, u32[]{:S(2)}, u32[]{:S(2)}) collective-permute-start(s16[208,384]{1,0:T(8,128)(2,1)S(1)} %get-tuple-element.70), channel_id=1, source_target_pairs={{0,16},{1,17},{2,18},{3,19},{16,0},{17,1},{18,2},{19,3},{4,20},{5,... | collective-permute-start | bytes 479240 | tf_op jit(solution)/shard_map/ppermute | solution.py:509
  12.4 1.6 %fetch_heads.5 = (bf16[1,192,1536]{2,1,0:T(8,128)(2,1)S(1)}, bf16[1,192,1536]{2,1,0:T(8,128)(2,1)S(1)}, bf16[1,192,1536]{2,1,0:T(8,128)(2,1)S(1)}, f32[8,128]{1,0:T(8,128)}) custom-call(s32[1,32]{1,0:T(1,128)S(1)} %bitcast.9, bf16[8,192,1536]{2,1,0:T(8,128)(2,1)S(1)} %bitcast.6, s16[208,384]{1,0:T(8,128)(2,1)S(1)} %get-tuple-element.51.refs_2_), custom_call_target="tpu_custom_call" | custom-call | tf_op jit(solution)/shard_map/fetch_heads/pallas_call | solution.py:48
  14.0 0.7 %turn_momentum.1 = (f32[4,192,384]{2,1,0:T(8,128)S(1)}, f32[1,32]{1,0:T(1,128)S(1)}) custom-call(f32[8,192,192]{2,1,0:T(8,128)S(1)} %copy-done.2, f32[4,192,256]{2,1,0:T(8,128)S(1)} %collective-permute-done.1.refs_1_, f32[1,32]{1,0:T(1,128)S(1)} %copy-done.8), custom_call_target="tpu_custom_call" | custom-call | tf_op jit(solution)/shard_map/turn_momentum/pallas_call | solution.py:48
  14.8 1.0 %collective-permute-done.3.refs_2_.refs_1_ = s16[208,384]{1,0:T(8,128)(2,1)S(1)} collective-permute-done((s16[208,384]{1,0:T(8,128)(2,1)S(1)}, s16[208,384]{1,0:T(8,128)(2,1)S(1)}, u32[]{:S(2)}, u32[]{:S(2)}) %collective-permute-start.3) | collective-permute-done | bytes 159776 | tf_op jit(solution)/shard_map/ppermute | solution.py:509
  15.8 0.3 pair_sum.5
  16.1 2.1 %collective-permute-start.4 = (s16[208,384]{1,0:T(8,128)(2,1)S(1)}, s16[208,384]{1,0:T(8,128)(2,1)S(1)}, u32[]{:S(2)}, u32[]{:S(2)}) collective-permute-start(s16[208,384]{1,0:T(8,128)(2,1)S(1)} %get-tuple-element.57), channel_id=1, source_target_pairs={{0,2},{1,3},{2,0},{3,1},{16,18},{17,19},{18,16},{19,17},{4,6},{5,7... | collective-permute-start | bytes 479240 | tf_op jit(solution)/shard_map/ppermute | solution.py:509
  18.2 1.5 %collective-permute-start.5 = (s16[208,384]{1,0:T(8,128)(2,1)S(1)}, s16[208,384]{1,0:T(8,128)(2,1)S(1)}, u32[]{:S(2)}, u32[]{:S(2)}) collective-permute-start(s16[208,384]{1,0:T(8,128)(2,1)S(1)} %get-tuple-element.58), channel_id=1, source_target_pairs={{0,16},{1,17},{2,18},{3,19},{16,0},{17,1},{18,2},{19,3},{4,20},{5,... | collective-permute-start | bytes 479240 | tf_op jit(solution)/shard_map/ppermute | solution.py:509
  19.7 0.4 collective-permute-done.13.refs_2_
  20.1 0.7 %collective-permute-done.14.refs_3_ = s16[208,384]{1,0:T(8,128)(2,1)S(1)} collective-permute-done((s16[208,384]{1,0:T(8,128)(2,1)S(1)}, s16[208,384]{1,0:T(8,128)(2,1)S(1)}, u32[]{:S(2)}, u32[]{:S(2)}) %collective-permute-start.14) | collective-permute-done | bytes 159776 | tf_op jit(solution)/shard_map/ppermute | solution.py:509
  20.8 0.2 plane_sum.4
  21.0 3.7 %collective-permute-start.15 = (s16[208,384]{1,0:T(8,128)(2,1)S(1)}, s16[208,384]{1,0:T(8,128)(2,1)S(1)}, u32[]{:S(2)}, u32[]{:S(2)}) collective-permute-start(s16[208,384]{1,0:T(8,128)(2,1)S(1)} %plane_sum.4), channel_id=1, source_target_pairs={{0,12},{4,8},{8,4},{12,0},{1,13},{5,9},{9,5},{13,1},{2,14},{6,10},... | collective-permute-start | bytes 479240 | tf_op jit(solution)/shard_map/ppermute | solution.py:547
  24.6 1.4 %collective-permute-start.12 = (s16[208,384]{1,0:T(8,128)(2,1)S(1)}, s16[208,384]{1,0:T(8,128)(2,1)S(1)}, u32[]{:S(2)}, u32[]{:S(2)}) collective-permute-start(s16[208,384]{1,0:T(8,128)(2,1)S(1)} %get-tuple-element.68), channel_id=1, source_target_pairs={{0,18},{1,19},{2,16},{3,17},{16,2},{17,3},{18,0},{19,1},{4,22},{5,... | collective-permute-start | bytes 479240 | tf_op jit(solution)/shard_map/ppermute | solution.py:509
  26.1 0.3 pair_sum.6
  26.4 1.7 %collective-permute-start.6 = (s16[208,384]{1,0:T(8,128)(2,1)S(1)}, s16[208,384]{1,0:T(8,128)(2,1)S(1)}, u32[]{:S(2)}, u32[]{:S(2)}) collective-permute-start(s16[208,384]{1,0:T(8,128)(2,1)S(1)} %get-tuple-element.59), channel_id=1, source_target_pairs={{0,2},{1,3},{2,0},{3,1},{16,18},{17,19},{18,16},{19,17},{4,6},{5,7... | collective-permute-start | bytes 479240 | tf_op jit(solution)/shard_map/ppermute | solution.py:509
  28.1 0.4 collective-permute-start.7
  28.5 1.4 %collective-permute-start.11 = (s16[208,384]{1,0:T(8,128)(2,1)S(1)}, s16[208,384]{1,0:T(8,128)(2,1)S(1)}, u32[]{:S(2)}, u32[]{:S(2)}) collective-permute-start(s16[208,384]{1,0:T(8,128)(2,1)S(1)} %get-tuple-element.66), channel_id=1, source_target_pairs={{0,18},{1,19},{2,16},{3,17},{16,2},{17,3},{18,0},{19,1},{4,22},{5,... | collective-permute-start | bytes 479240 | tf_op jit(solution)/shard_map/ppermute | solution.py:509
  29.9 2.8 %collective-permute-done.12.refs_3_ = s16[208,384]{1,0:T(8,128)(2,1)S(1)} collective-permute-done((s16[208,384]{1,0:T(8,128)(2,1)S(1)}, s16[208,384]{1,0:T(8,128)(2,1)S(1)}, u32[]{:S(2)}, u32[]{:S(2)}) %collective-permute-start.12) | collective-permute-done | bytes 159776 | tf_op jit(solution)/shard_map/ppermute | solution.py:509
  32.7 0.2 plane_sum.5
  32.9 0.1 collective-permute-start.16
  33.0 1.5 %collective-permute-done.6.refs_2_.refs_1_ = s16[208,384]{1,0:T(8,128)(2,1)S(1)} collective-permute-done((s16[208,384]{1,0:T(8,128)(2,1)S(1)}, s16[208,384]{1,0:T(8,128)(2,1)S(1)}, u32[]{:S(2)}, u32[]{:S(2)}) %collective-permute-start.6) | collective-permute-done | bytes 159776 | tf_op jit(solution)/shard_map/ppermute | solution.py:509
  34.5 0.3 collective-permute-done.7.refs_3_.refs_2_
  34.8 0.3 pair_sum.7
  35.0 1.5 %collective-permute-start.8 = (s16[208,384]{1,0:T(8,128)(2,1)S(1)}, s16[208,384]{1,0:T(8,128)(2,1)S(1)}, u32[]{:S(2)}, u32[]{:S(2)}) collective-permute-start(s16[208,384]{1,0:T(8,128)(2,1)S(1)} %get-tuple-element.62), channel_id=1, source_target_pairs={{0,2},{1,3},{2,0},{3,1},{16,18},{17,19},{18,16},{19,17},{4,6},{5,7... | collective-permute-start | bytes 479240 | tf_op jit(solution)/shard_map/ppermute | solution.py:509
  36.6 0.7 %collective-permute-start.9 = (s16[208,384]{1,0:T(8,128)(2,1)S(1)}, s16[208,384]{1,0:T(8,128)(2,1)S(1)}, u32[]{:S(2)}, u32[]{:S(2)}) collective-permute-start(s16[208,384]{1,0:T(8,128)(2,1)S(1)} %get-tuple-element.63), channel_id=1, source_target_pairs={{0,16},{1,17},{2,18},{3,19},{16,0},{17,1},{18,2},{19,3},{4,20},{5,... | collective-permute-start | bytes 479240 | tf_op jit(solution)/shard_map/ppermute | solution.py:509
  37.2 1.4 %collective-permute-start.10 = (s16[208,384]{1,0:T(8,128)(2,1)S(1)}, s16[208,384]{1,0:T(8,128)(2,1)S(1)}, u32[]{:S(2)}, u32[]{:S(2)}) collective-permute-start(s16[208,384]{1,0:T(8,128)(2,1)S(1)} %get-tuple-element.64), channel_id=1, source_target_pairs={{0,18},{1,19},{2,16},{3,17},{16,2},{17,3},{18,0},{19,1},{4,22},{5,... | collective-permute-start | bytes 479240 | tf_op jit(solution)/shard_map/ppermute | solution.py:509
  38.6 1.3 %collective-permute-done.16.refs_5_.refs_4_ = s16[208,384]{1,0:T(8,128)(2,1)S(1)} collective-permute-done((s16[208,384]{1,0:T(8,128)(2,1)S(1)}, s16[208,384]{1,0:T(8,128)(2,1)S(1)}, u32[]{:S(2)}, u32[]{:S(2)}) %collective-permute-start.16) | collective-permute-done | bytes 159776 | tf_op jit(solution)/shard_map/ppermute | solution.py:547
  39.9 0.2 plane_sum.6
  40.1 0.7 collective-permute-start.17
  40.8 1.3 %scale_keys.1.refs_6_ = f32[8,64,128]{2,1,0:T(8,128)} custom-call(f32[1,32]{1,0:T(1,128)S(1)} %get-tuple-element.73.refs_1_.refs_0_, f32[8,64,128]{2,1,0:T(8,128)S(1)} %copy-done.5), custom_call_target="tpu_custom_call" | custom-call | tf_op jit(solution)/shard_map/scale_keys/pallas_call | solution.py:48
  42.1 0.8 %scale_weight.1 = (f32[8,192,192]{2,1,0:T(8,128)S(1)}, f32[8,192]{1,0:T(8,128)S(1)}) custom-call(s32[1,32]{1,0:T(1,128)S(1)} %bitcast.10, f32[1,32]{1,0:T(1,128)S(1)} %get-tuple-element.73.refs_1_.refs_0_, f32[8,192,192]{2,1,0:T(8,128)S(1)} %copy-done.3), custom_call_target="tpu_custom_call" | custom-call | tf_op jit(solution)/shard_map/scale_weight/pallas_call | solution.py:48
  42.9 1.1 %collective-permute-done.9.refs_2_ = s16[208,384]{1,0:T(8,128)(2,1)S(1)} collective-permute-done((s16[208,384]{1,0:T(8,128)(2,1)S(1)}, s16[208,384]{1,0:T(8,128)(2,1)S(1)}, u32[]{:S(2)}, u32[]{:S(2)}) %collective-permute-start.9) | collective-permute-done | bytes 159776 | tf_op jit(solution)/shard_map/ppermute | solution.py:509
  44.0 1.5 %collective-permute-done.17.refs_4_.refs_3_ = s16[208,384]{1,0:T(8,128)(2,1)S(1)} collective-permute-done((s16[208,384]{1,0:T(8,128)(2,1)S(1)}, s16[208,384]{1,0:T(8,128)(2,1)S(1)}, u32[]{:S(2)}, u32[]{:S(2)}) %collective-permute-start.17) | collective-permute-done | bytes 159776 | tf_op jit(solution)/shard_map/ppermute | solution.py:547
  45.5 0.1 plane_sum.7.refs_2_
  45.6 1.4 %refresh_and_gram.1 = (f32[4,192,384]{2,1,0:T(8,128)S(1)}, f32[224,128]{1,0:T(8,128)S(1)}, s16[240,128]{1,0:T(8,128)(2,1)S(1)}, s16[240,128]{1,0:T(8,128)(2,1)S(1)}, s16[240,128]{1,0:T(8,128)(2,1)S(1)}) custom-call(s32[1,32]{1,0:T(1,128)S(1)} %bitcast.11, f32[4,192,384]{2,1,0:T(8,128)S(1)} %get-tuple-element.50.refs_3_.refs_1_, ...), custom_call_target="tpu_custom_call" | custom-call | tf_op jit(solution)/shard_map/refresh_and_gram/pallas_call | solution.py:48
  47.0 1.5 %collective-permute-start.18 = (s16[240,128]{1,0:T(8,128)(2,1)S(1)}, s16[240,128]{1,0:T(8,128)(2,1)S(1)}, u32[]{:S(2)}, u32[]{:S(2)}) collective-permute-start(s16[240,128]{1,0:T(8,128)(2,1)S(1)} %get-tuple-element.77), channel_id=1, source_target_pairs={{0,2},{1,3},{2,0},{3,1},{16,18},{17,19},{18,16},{19,17},{4,6},{5,7... | collective-permute-start | bytes 184328 | tf_op jit(solution)/shard_map/ppermute | solution.py:509
  48.5 0.3 collective-permute-start.19
  48.9 1.7 %collective-permute-start.20 = (s16[240,128]{1,0:T(8,128)(2,1)S(1)}, s16[240,128]{1,0:T(8,128)(2,1)S(1)}, u32[]{:S(2)}, u32[]{:S(2)}) collective-permute-start(s16[240,128]{1,0:T(8,128)(2,1)S(1)} %get-tuple-element.79), channel_id=1, source_target_pairs={{0,18},{1,19},{2,16},{3,17},{16,2},{17,3},{18,0},{19,1},{4,22},{5,... | collective-permute-start | bytes 184328 | tf_op jit(solution)/shard_map/ppermute | solution.py:509
  50.6 0.7 %collective-permute-done.18.refs_1_ = s16[240,128]{1,0:T(8,128)(2,1)S(1)} collective-permute-done((s16[240,128]{1,0:T(8,128)(2,1)S(1)}, s16[240,128]{1,0:T(8,128)(2,1)S(1)}, u32[]{:S(2)}, u32[]{:S(2)}) %collective-permute-start.18) | collective-permute-done | bytes 61472 | tf_op jit(solution)/shard_map/ppermute | solution.py:509
  51.3 1.4 %collective-permute-done.19.refs_2_ = s16[240,128]{1,0:T(8,128)(2,1)S(1)} collective-permute-done((s16[240,128]{1,0:T(8,128)(2,1)S(1)}, s16[240,128]{1,0:T(8,128)(2,1)S(1)}, u32[]{:S(2)}, u32[]{:S(2)}) %collective-permute-start.19) | collective-permute-done | bytes 61472 | tf_op jit(solution)/shard_map/ppermute | solution.py:509
  52.8 1.2 %collective-permute-done.20.refs_3_ = s16[240,128]{1,0:T(8,128)(2,1)S(1)} collective-permute-done((s16[240,128]{1,0:T(8,128)(2,1)S(1)}, s16[240,128]{1,0:T(8,128)(2,1)S(1)}, u32[]{:S(2)}, u32[]{:S(2)}) %collective-permute-start.20) | collective-permute-done | bytes 61472 | tf_op jit(solution)/shard_map/ppermute | solution.py:509
  54.0 1.2 %newton_schulz.1.refs_1_.refs_3_ = bf16[240,128]{1,0:T(8,128)(2,1)S(1)} custom-call(f32[224,128]{1,0:T(8,128)S(1)} %get-tuple-element.76.refs_0_, s16[240,128]{1,0:T(8,128)(2,1)S(1)} %collective-permute-done.18.refs_1_, s16[240,128]{1,0:T(8,128)(2,1)S(1)} %collective-permute-done.19.refs_2_, s16[240,128]{1,0:T(8,128)(2,1)S(1)} %collective-permute-done.20.refs_3_), custom_call_target="tpu_custom_call" | custom-call | tf_op jit(solution)/shard_map/newton_schulz/pallas_call | solution.py:48
  55.2 0.7 %turn_back.1 = (f32[4,192,192]{2,1,0:T(8,128)S(1)}, f32[4,192,192]{2,1,0:T(8,128)S(1)}) custom-call(f32[4,192,384]{2,1,0:T(8,128)S(1)} %get-tuple-element.75.refs_0_, bf16[240,128]{1,0:T(8,128)(2,1)S(1)} %newton_schulz.1.refs_1_.refs_3_), custom_call_target="tpu_custom_call" | custom-call | tf_op jit(solution)/shard_map/turn_back/pallas_call | solution.py:48
  55.9 0.1 collective-permute-start.21
  56.0 1.8 %collective-permute-start.27 = (bf16[240,128]{1,0:T(8,128)(2,1)S(1)}, bf16[240,128]{1,0:T(8,128)(2,1)S(1)}, u32[]{:S(2)}, u32[]{:S(2)}) collective-permute-start(bf16[240,128]{1,0:T(8,128)(2,1)S(1)} %newton_schulz.1.refs_1_.refs_3_), channel_id=1, source_target_pairs={{0,18},{1,19},{2,16},{3,17},{16,2},{17,3},{18,0},{19,1},{4,22},{5,... | collective-permute-start | bytes 184328 | tf_op jit(solution)/shard_map/ppermute | solution.py:509
  57.7 1.1 %collective-permute-start.25 = (bf16[240,128]{1,0:T(8,128)(2,1)S(1)}, bf16[240,128]{1,0:T(8,128)(2,1)S(1)}, u32[]{:S(2)}, u32[]{:S(2)}) collective-permute-start(bf16[240,128]{1,0:T(8,128)(2,1)S(1)} %newton_schulz.1.refs_1_.refs_3_), channel_id=1, source_target_pairs={{0,16},{1,17},{2,18},{3,19},{16,0},{17,1},{18,2},{19,3},{4,20},{5,... | collective-permute-start | bytes 184328 | tf_op jit(solution)/shard_map/ppermute | solution.py:509
  58.8 0.7 %collective-permute-start.23 = (bf16[240,128]{1,0:T(8,128)(2,1)S(1)}, bf16[240,128]{1,0:T(8,128)(2,1)S(1)}, u32[]{:S(2)}, u32[]{:S(2)}) collective-permute-start(bf16[240,128]{1,0:T(8,128)(2,1)S(1)} %newton_schulz.1.refs_1_.refs_3_), channel_id=1, source_target_pairs={{0,2},{1,3},{2,0},{3,1},{16,18},{17,19},{18,16},{19,17},{4,6},{5,7... | collective-permute-start | bytes 184328 | tf_op jit(solution)/shard_map/ppermute | solution.py:509
  59.5 1.8 %collective-permute-done.27.refs_6_ = bf16[240,128]{1,0:T(8,128)(2,1)S(1)} collective-permute-done((bf16[240,128]{1,0:T(8,128)(2,1)S(1)}, bf16[240,128]{1,0:T(8,128)(2,1)S(1)}, u32[]{:S(2)}, u32[]{:S(2)}) %collective-permute-start.27) | collective-permute-done | bytes 61472 | tf_op jit(solution)/shard_map/ppermute | solution.py:509
  61.4 1.2 %collective-permute-done.25.refs_5_ = bf16[240,128]{1,0:T(8,128)(2,1)S(1)} collective-permute-done((bf16[240,128]{1,0:T(8,128)(2,1)S(1)}, bf16[240,128]{1,0:T(8,128)(2,1)S(1)}, u32[]{:S(2)}, u32[]{:S(2)}) %collective-permute-start.25) | collective-permute-done | bytes 61472 | tf_op jit(solution)/shard_map/ppermute | solution.py:509
  62.6 0.0 collective-permute-start.26
  62.6 0.4 collective-permute-done.23.refs_4_
  63.0 0.1 collective-permute-start.24
  63.1 1.2 %merge_momentum.1 = (f32[8,192,192]{2,1,0:T(8,128)}, f32[8,128]{1,0:T(8,128)S(1)}) custom-call(f32[4,192,192]{2,1,0:T(8,128)S(1)} %get-tuple-element.80.refs_0_.refs_2_, f32[4,192,192]{2,1,0:T(8,128)S(1)} %collective-permute-done.21.refs_1_.refs_2_), custom_call_target="tpu_custom_call" | custom-call | tf_op jit(solution)/shard_map/merge_momentum/pallas_call | solution.py:48
  64.3 1.3 %update_weight.2.refs_7_ = f32[8,192,192]{2,1,0:T(8,128)} custom-call(f32[8,192,192]{2,1,0:T(8,128)S(1)} %get-tuple-element.74.refs_5_.refs_0_, f32[8,192]{1,0:T(8,128)S(1)} %get-tuple-element.83.refs_1_, f32[4,192,192]{2,1,0:T(8,128)S(1)} %get-tuple-element.80.refs_0_.refs_2_, bf16[240,128]{1,0:T(8,128)(2,1)S(1)} %newton_schulz.1.refs_1_.refs_3_, ...), custom_call_target="tpu_custom_call" | custom-call | tf_op jit(solution)/shard_map/update_weight/pallas_call | solution.py:48
  65.6 1.3 %update_weight.3 = f32[8,192,192]{2,1,0:T(8,128)} custom-call(f32[8,192,192]{2,1,0:T(8,128)S(1)} %get-tuple-element.74.refs_5_.refs_0_, f32[8,192]{1,0:T(8,128)S(1)} %get-tuple-element.83.refs_1_, f32[4,192,192]{2,1,0:T(8,128)S(1)} %collective-permute-done.21.refs_1_.refs_2_, ...), custom_call_target="tpu_custom_call", output_to_operand_aliasing={{}: (7, {})} | custom-call | tf_op jit(solution)/shard_map/update_weight/pallas_call | solution.py:48
  (32 shorter events, 0.1 us)
Async XLA Ops:
  0.6 0.7 copy-start.6
  1.3 2.5 %copy-start = (bf16[1,1536,8,192]{1,3,2,0:T(8,128)(2,1)S(1)}, bf16[1,1536,8,192]{1,3,2,0:T(8,128)(2,1)}, u32[]{:S(2)}) copy-start(bf16[1,1536,8,192]{1,3,2,0:T(8,128)(2,1)} %param.6) | copy-start | bytes 14155780
  1.3 2.5 %copy-start.8 = (f32[1,32]{1,0:T(1,128)S(1)}, f32[1,32]{1,0:T(1,128)}, u32[]{:S(2)}) copy-start(f32[1,32]{1,0:T(1,128)} %refs_2_.4) | copy-start | bytes 388
  3.2 3.8 %collective-permute-start = (bf16[1,192,1536]{2,1,0:T(8,128)(2,1)S(1)}, bf16[1,192,1536]{2,1,0:T(8,128)(2,1)S(1)}, u32[]{:S(2)}, u32[]{:S(2)}) collective-permute-start(bf16[1,192,1536]{2,1,0:T(8,128)(2,1)S(1)} %get-tuple-element.46), channel_id=1, source_target_pairs={{0,1},{1,0},{2,3},{3,2},{16,17},{17,16},{18,19},{19,18},{4,5},{5,4... | collective-permute-start | bytes 1769480 | tf_op jit(solution)/shard_map/ppermute | solution.py:509
  3.8 1.4 %copy-start.1 = (f32[8,192,192]{2,1,0:T(8,128)S(1)}, f32[8,192,192]{2,1,0:T(8,128)}, u32[]{:S(2)}) copy-start(f32[8,192,192]{2,1,0:T(8,128)} %refs_0_.1) | copy-start | bytes 3538948
  7.1 5.3 %copy-start.7 = (s32[32,1]{0,1:T(1,128)S(1)}, s32[32,1]{0,1:T(1,128)}, u32[]{:S(2)}) copy-start(s32[32,1]{0,1:T(1,128)} %param.7) | copy-start | bytes 388
  7.4 8.4 %collective-permute-start.2 = (bf16[3,192,1536]{2,1,0:T(8,128)(2,1)S(1)}, bf16[3,192,1536]{2,1,0:T(8,128)(2,1)S(1)}, u32[]{:S(2)}, u32[]{:S(2)}) collective-permute-start(bf16[3,192,1536]{2,1,0:T(8,128)(2,1)S(1)} %get-tuple-element.53), channel_id=1, source_target_pairs={{0,1},{1,0},{2,3},{3,2},{16,17},{17,16},{18,19},{19,18},{4,5},{5,4... | collective-permute-start | bytes 5308424 | tf_op jit(solution)/shard_map/ppermute | solution.py:509
  7.9 6.1 %collective-permute-start.1 = (f32[4,192,256]{2,1,0:T(8,128)S(1)}, f32[4,192,256]{2,1,0:T(8,128)S(1)}, u32[]{:S(2)}, u32[]{:S(2)}) collective-permute-start(f32[4,192,256]{2,1,0:T(8,128)S(1)} %get-tuple-element.49), channel_id=1, source_target_pairs={{0,1},{1,0},{2,3},{3,2},{16,17},{17,16},{18,19},{19,18},{4,5},{5,4... | collective-permute-start | bytes 2359304 | tf_op jit(solution)/shard_map/ppermute | solution.py:509
  8.0 7.8 %collective-permute-start.3 = (s16[208,384]{1,0:T(8,128)(2,1)S(1)}, s16[208,384]{1,0:T(8,128)(2,1)S(1)}, u32[]{:S(2)}, u32[]{:S(2)}) collective-permute-start(s16[208,384]{1,0:T(8,128)(2,1)S(1)} %get-tuple-element.51.refs_2_), channel_id=1, source_target_pairs={{0,2},{1,3},{2,0},{3,1},{16,18},{17,19},{18,16},{19,17},{4,6},{5,7... | collective-permute-start | bytes 479240 | tf_op jit(solution)/shard_map/ppermute | solution.py:509
  10.9 9.2 %collective-permute-start.13 = (s16[208,384]{1,0:T(8,128)(2,1)S(1)}, s16[208,384]{1,0:T(8,128)(2,1)S(1)}, u32[]{:S(2)}, u32[]{:S(2)}) collective-permute-start(s16[208,384]{1,0:T(8,128)(2,1)S(1)} %get-tuple-element.70), channel_id=1, source_target_pairs={{0,16},{1,17},{2,18},{3,19},{16,0},{17,1},{18,2},{19,3},{4,20},{5,... | collective-permute-start | bytes 479240 | tf_op jit(solution)/shard_map/ppermute | solution.py:509
  12.4 1.6 %copy-start.2 = (f32[8,192,192]{2,1,0:T(8,128)S(1)}, f32[8,192,192]{2,1,0:T(8,128)}, u32[]{:S(2)}) copy-start(f32[8,192,192]{2,1,0:T(8,128)} %refs_0_.1) | copy-start | bytes 3538948
  12.4 8.4 %collective-permute-start.14 = (s16[208,384]{1,0:T(8,128)(2,1)S(1)}, s16[208,384]{1,0:T(8,128)(2,1)S(1)}, u32[]{:S(2)}, u32[]{:S(2)}) collective-permute-start(s16[208,384]{1,0:T(8,128)(2,1)S(1)} %get-tuple-element.71), channel_id=1, source_target_pairs={{0,18},{1,19},{2,16},{3,17},{16,2},{17,3},{18,0},{19,1},{4,22},{5,... | collective-permute-start | bytes 479240 | tf_op jit(solution)/shard_map/ppermute | solution.py:509
  16.1 10.0 %collective-permute-start.4 = (s16[208,384]{1,0:T(8,128)(2,1)S(1)}, s16[208,384]{1,0:T(8,128)(2,1)S(1)}, u32[]{:S(2)}, u32[]{:S(2)}) collective-permute-start(s16[208,384]{1,0:T(8,128)(2,1)S(1)} %get-tuple-element.57), channel_id=1, source_target_pairs={{0,2},{1,3},{2,0},{3,1},{16,18},{17,19},{18,16},{19,17},{4,6},{5,7... | collective-permute-start | bytes 479240 | tf_op jit(solution)/shard_map/ppermute | solution.py:509
  18.2 7.9 %collective-permute-start.5 = (s16[208,384]{1,0:T(8,128)(2,1)S(1)}, s16[208,384]{1,0:T(8,128)(2,1)S(1)}, u32[]{:S(2)}, u32[]{:S(2)}) collective-permute-start(s16[208,384]{1,0:T(8,128)(2,1)S(1)} %get-tuple-element.58), channel_id=1, source_target_pairs={{0,16},{1,17},{2,18},{3,19},{16,0},{17,1},{18,2},{19,3},{4,20},{5,... | collective-permute-start | bytes 479240 | tf_op jit(solution)/shard_map/ppermute | solution.py:509
  21.0 9.0 %collective-permute-start.15 = (s16[208,384]{1,0:T(8,128)(2,1)S(1)}, s16[208,384]{1,0:T(8,128)(2,1)S(1)}, u32[]{:S(2)}, u32[]{:S(2)}) collective-permute-start(s16[208,384]{1,0:T(8,128)(2,1)S(1)} %plane_sum.4), channel_id=1, source_target_pairs={{0,12},{4,8},{8,4},{12,0},{1,13},{5,9},{9,5},{13,1},{2,14},{6,10},... | collective-permute-start | bytes 479240 | tf_op jit(solution)/shard_map/ppermute | solution.py:547
  24.6 8.1 %collective-permute-start.12 = (s16[208,384]{1,0:T(8,128)(2,1)S(1)}, s16[208,384]{1,0:T(8,128)(2,1)S(1)}, u32[]{:S(2)}, u32[]{:S(2)}) collective-permute-start(s16[208,384]{1,0:T(8,128)(2,1)S(1)} %get-tuple-element.68), channel_id=1, source_target_pairs={{0,18},{1,19},{2,16},{3,17},{16,2},{17,3},{18,0},{19,1},{4,22},{5,... | collective-permute-start | bytes 479240 | tf_op jit(solution)/shard_map/ppermute | solution.py:509
  26.4 8.1 %collective-permute-start.6 = (s16[208,384]{1,0:T(8,128)(2,1)S(1)}, s16[208,384]{1,0:T(8,128)(2,1)S(1)}, u32[]{:S(2)}, u32[]{:S(2)}) collective-permute-start(s16[208,384]{1,0:T(8,128)(2,1)S(1)} %get-tuple-element.59), channel_id=1, source_target_pairs={{0,2},{1,3},{2,0},{3,1},{16,18},{17,19},{18,16},{19,17},{4,6},{5,7... | collective-permute-start | bytes 479240 | tf_op jit(solution)/shard_map/ppermute | solution.py:509
  28.1 6.7 %collective-permute-start.7 = (s16[208,384]{1,0:T(8,128)(2,1)S(1)}, s16[208,384]{1,0:T(8,128)(2,1)S(1)}, u32[]{:S(2)}, u32[]{:S(2)}) collective-permute-start(s16[208,384]{1,0:T(8,128)(2,1)S(1)} %get-tuple-element.60), channel_id=1, source_target_pairs={{0,16},{1,17},{2,18},{3,19},{16,0},{17,1},{18,2},{19,3},{4,20},{5,... | collective-permute-start | bytes 479240 | tf_op jit(solution)/shard_map/ppermute | solution.py:509
  28.5 10.1 %collective-permute-start.11 = (s16[208,384]{1,0:T(8,128)(2,1)S(1)}, s16[208,384]{1,0:T(8,128)(2,1)S(1)}, u32[]{:S(2)}, u32[]{:S(2)}) collective-permute-start(s16[208,384]{1,0:T(8,128)(2,1)S(1)} %get-tuple-element.66), channel_id=1, source_target_pairs={{0,18},{1,19},{2,16},{3,17},{16,2},{17,3},{18,0},{19,1},{4,22},{5,... | collective-permute-start | bytes 479240 | tf_op jit(solution)/shard_map/ppermute | solution.py:509
  32.9 7.0 %collective-permute-start.16 = (s16[208,384]{1,0:T(8,128)(2,1)S(1)}, s16[208,384]{1,0:T(8,128)(2,1)S(1)}, u32[]{:S(2)}, u32[]{:S(2)}) collective-permute-start(s16[208,384]{1,0:T(8,128)(2,1)S(1)} %plane_sum.5), channel_id=1, source_target_pairs={{0,8},{4,12},{8,0},{12,4},{1,9},{5,13},{9,1},{13,5},{2,10},{6,14},... | collective-permute-start | bytes 479240 | tf_op jit(solution)/shard_map/ppermute | solution.py:547
  34.8 6.0 %copy-start.5 = (f32[8,64,128]{2,1,0:T(8,128)S(1)}, f32[8,64,128]{2,1,0:T(8,128)}, u32[]{:S(2)}) copy-start(f32[8,64,128]{2,1,0:T(8,128)} %refs_1_.1) | copy-start | bytes 786436
  34.8 7.3 %copy-start.3 = (f32[8,192,192]{2,1,0:T(8,128)S(1)}, f32[8,192,192]{2,1,0:T(8,128)}, u32[]{:S(2)}) copy-start(f32[8,192,192]{2,1,0:T(8,128)} %refs_2_.5) | copy-start | bytes 3538948
  35.0 7.8 %collective-permute-start.8 = (s16[208,384]{1,0:T(8,128)(2,1)S(1)}, s16[208,384]{1,0:T(8,128)(2,1)S(1)}, u32[]{:S(2)}, u32[]{:S(2)}) collective-permute-start(s16[208,384]{1,0:T(8,128)(2,1)S(1)} %get-tuple-element.62), channel_id=1, source_target_pairs={{0,2},{1,3},{2,0},{3,1},{16,18},{17,19},{18,16},{19,17},{4,6},{5,7... | collective-permute-start | bytes 479240 | tf_op jit(solution)/shard_map/ppermute | solution.py:509
  36.6 7.4 %collective-permute-start.9 = (s16[208,384]{1,0:T(8,128)(2,1)S(1)}, s16[208,384]{1,0:T(8,128)(2,1)S(1)}, u32[]{:S(2)}, u32[]{:S(2)}) collective-permute-start(s16[208,384]{1,0:T(8,128)(2,1)S(1)} %get-tuple-element.63), channel_id=1, source_target_pairs={{0,16},{1,17},{2,18},{3,19},{16,0},{17,1},{18,2},{19,3},{4,20},{5,... | collective-permute-start | bytes 479240 | tf_op jit(solution)/shard_map/ppermute | solution.py:509
  37.2 6.7 %collective-permute-start.10 = (s16[208,384]{1,0:T(8,128)(2,1)S(1)}, s16[208,384]{1,0:T(8,128)(2,1)S(1)}, u32[]{:S(2)}, u32[]{:S(2)}) collective-permute-start(s16[208,384]{1,0:T(8,128)(2,1)S(1)} %get-tuple-element.64), channel_id=1, source_target_pairs={{0,18},{1,19},{2,16},{3,17},{16,2},{17,3},{18,0},{19,1},{4,22},{5,... | collective-permute-start | bytes 479240 | tf_op jit(solution)/shard_map/ppermute | solution.py:509
  40.1 5.3 %collective-permute-start.17 = (s16[208,384]{1,0:T(8,128)(2,1)S(1)}, s16[208,384]{1,0:T(8,128)(2,1)S(1)}, u32[]{:S(2)}, u32[]{:S(2)}) collective-permute-start(s16[208,384]{1,0:T(8,128)(2,1)S(1)} %get-tuple-element.72), channel_id=1, source_target_pairs={{0,4},{4,0},{8,12},{12,8},{1,5},{5,1},{9,13},{13,9},{2,6},{6,2},{1... | collective-permute-start | bytes 479240 | tf_op jit(solution)/shard_map/ppermute | solution.py:547
  42.1 3.4 %copy-start.4 = (f32[8,64,128]{2,1,0:T(8,128)S(1)}, f32[8,64,128]{2,1,0:T(8,128)}, u32[]{:S(2)}) copy-start(f32[8,64,128]{2,1,0:T(8,128)} %scale_keys.1.refs_6_) | copy-start | bytes 786436
  47.0 4.3 %collective-permute-start.18 = (s16[240,128]{1,0:T(8,128)(2,1)S(1)}, s16[240,128]{1,0:T(8,128)(2,1)S(1)}, u32[]{:S(2)}, u32[]{:S(2)}) collective-permute-start(s16[240,128]{1,0:T(8,128)(2,1)S(1)} %get-tuple-element.77), channel_id=1, source_target_pairs={{0,2},{1,3},{2,0},{3,1},{16,18},{17,19},{18,16},{19,17},{4,6},{5,7... | collective-permute-start | bytes 184328 | tf_op jit(solution)/shard_map/ppermute | solution.py:509
  48.5 4.2 %collective-permute-start.19 = (s16[240,128]{1,0:T(8,128)(2,1)S(1)}, s16[240,128]{1,0:T(8,128)(2,1)S(1)}, u32[]{:S(2)}, u32[]{:S(2)}) collective-permute-start(s16[240,128]{1,0:T(8,128)(2,1)S(1)} %get-tuple-element.78), channel_id=1, source_target_pairs={{0,16},{1,17},{2,18},{3,19},{16,0},{17,1},{18,2},{19,3},{4,20},{5,... | collective-permute-start | bytes 184328 | tf_op jit(solution)/shard_map/ppermute | solution.py:509
  48.9 5.1 %collective-permute-start.20 = (s16[240,128]{1,0:T(8,128)(2,1)S(1)}, s16[240,128]{1,0:T(8,128)(2,1)S(1)}, u32[]{:S(2)}, u32[]{:S(2)}) collective-permute-start(s16[240,128]{1,0:T(8,128)(2,1)S(1)} %get-tuple-element.79), channel_id=1, source_target_pairs={{0,18},{1,19},{2,16},{3,17},{16,2},{17,3},{18,0},{19,1},{4,22},{5,... | collective-permute-start | bytes 184328 | tf_op jit(solution)/shard_map/ppermute | solution.py:509
  55.9 7.2 %collective-permute-start.21 = (f32[4,192,192]{2,1,0:T(8,128)S(1)}, f32[4,192,192]{2,1,0:T(8,128)S(1)}, u32[]{:S(2)}, u32[]{:S(2)}) collective-permute-start(f32[4,192,192]{2,1,0:T(8,128)S(1)} %get-tuple-element.81), channel_id=1, source_target_pairs={{0,1},{1,0},{2,3},{3,2},{16,17},{17,16},{18,19},{19,18},{4,5},{5,4... | collective-permute-start | bytes 1769480 | tf_op jit(solution)/shard_map/ppermute | solution.py:509
  56.0 5.4 %collective-permute-start.27 = (bf16[240,128]{1,0:T(8,128)(2,1)S(1)}, bf16[240,128]{1,0:T(8,128)(2,1)S(1)}, u32[]{:S(2)}, u32[]{:S(2)}) collective-permute-start(bf16[240,128]{1,0:T(8,128)(2,1)S(1)} %newton_schulz.1.refs_1_.refs_3_), channel_id=1, source_target_pairs={{0,18},{1,19},{2,16},{3,17},{16,2},{17,3},{18,0},{19,1},{4,22},{5,... | collective-permute-start | bytes 184328 | tf_op jit(solution)/shard_map/ppermute | solution.py:509
  57.7 4.9 %collective-permute-start.25 = (bf16[240,128]{1,0:T(8,128)(2,1)S(1)}, bf16[240,128]{1,0:T(8,128)(2,1)S(1)}, u32[]{:S(2)}, u32[]{:S(2)}) collective-permute-start(bf16[240,128]{1,0:T(8,128)(2,1)S(1)} %newton_schulz.1.refs_1_.refs_3_), channel_id=1, source_target_pairs={{0,16},{1,17},{2,18},{3,19},{16,0},{17,1},{18,2},{19,3},{4,20},{5,... | collective-permute-start | bytes 184328 | tf_op jit(solution)/shard_map/ppermute | solution.py:509
  58.8 4.2 %collective-permute-start.23 = (bf16[240,128]{1,0:T(8,128)(2,1)S(1)}, bf16[240,128]{1,0:T(8,128)(2,1)S(1)}, u32[]{:S(2)}, u32[]{:S(2)}) collective-permute-start(bf16[240,128]{1,0:T(8,128)(2,1)S(1)} %newton_schulz.1.refs_1_.refs_3_), channel_id=1, source_target_pairs={{0,2},{1,3},{2,0},{3,1},{16,18},{17,19},{18,16},{19,17},{4,6},{5,7... | collective-permute-start | bytes 184328 | tf_op jit(solution)/shard_map/ppermute | solution.py:509
  59.5 6.1 %collective-permute-start.22 = (bf16[240,128]{1,0:T(8,128)(2,1)S(1)}, bf16[240,128]{1,0:T(8,128)(2,1)S(1)}, u32[]{:S(2)}, u32[]{:S(2)}) collective-permute-start(bf16[240,128]{1,0:T(8,128)(2,1)S(1)} %newton_schulz.1.refs_1_.refs_3_), channel_id=1, source_target_pairs={{0,1},{1,0},{2,3},{3,2},{16,17},{17,16},{18,19},{19,18},{4,5},{5,4... | collective-permute-start | bytes 184328 | tf_op jit(solution)/shard_map/ppermute | solution.py:509
  61.4 4.2 %collective-permute-start.28 = (bf16[240,128]{1,0:T(8,128)(2,1)S(1)}, bf16[240,128]{1,0:T(8,128)(2,1)S(1)}, u32[]{:S(2)}, u32[]{:S(2)}) collective-permute-start(bf16[240,128]{1,0:T(8,128)(2,1)S(1)} %collective-permute-done.27.refs_6_), channel_id=1, source_target_pairs={{0,1},{1,0},{2,3},{3,2},{16,17},{17,16},{18,19},{19,18},{4,5},{5,4... | collective-permute-start | bytes 184328 | tf_op jit(solution)/shard_map/ppermute | solution.py:509
  62.6 3.0 %collective-permute-start.26 = (bf16[240,128]{1,0:T(8,128)(2,1)S(1)}, bf16[240,128]{1,0:T(8,128)(2,1)S(1)}, u32[]{:S(2)}, u32[]{:S(2)}) collective-permute-start(bf16[240,128]{1,0:T(8,128)(2,1)S(1)} %collective-permute-done.25.refs_5_), channel_id=1, source_target_pairs={{0,1},{1,0},{2,3},{3,2},{16,17},{17,16},{18,19},{19,18},{4,5},{5,4... | collective-permute-start | bytes 184328 | tf_op jit(solution)/shard_map/ppermute | solution.py:509
  63.0 2.6 %collective-permute-start.24 = (bf16[240,128]{1,0:T(8,128)(2,1)S(1)}, bf16[240,128]{1,0:T(8,128)(2,1)S(1)}, u32[]{:S(2)}, u32[]{:S(2)}) collective-permute-start(bf16[240,128]{1,0:T(8,128)(2,1)S(1)} %collective-permute-done.23.refs_4_), channel_id=1, source_target_pairs={{0,1},{1,0},{2,3},{3,2},{16,17},{17,16},{18,19},{19,18},{4,5},{5,4... | collective-permute-start | bytes 184328 | tf_op jit(solution)/shard_map/ppermute | solution.py:509

commit v4 on v3

--- a/solution.py
+++ b/solution.py
@@ -18,9 +18,11 @@
 
 CORES = 2
 PLANE = ("dp", "context")
-SCALE_ROWS = 16
+NORM_ROWS = 16
+TILE = 16
 LEVELS = 14.99
 STEPS = 8.0
+LOWEST = 100.0 * STEPS
 NOTE_UNITS = (64.0, 64.0 * 32768.0, 64.0 * 32768.0 * 32768.0)
 GROUPS = 4
 LEFT = 128
@@ -66,34 +68,53 @@
     return found, seen
 
 
+def bits_of(number):
+    rows = jnp.broadcast_to(number.astype(jnp.int32), (TILE, number.shape[1]))
+    return lax.shift_right_logical(rows, lax.broadcasted_iota(jnp.int32, rows.shape, 0)) & 1
+
+
+def number_of(rows):
+    bits = rows.astype(jnp.int32) & 1
+    bits = lax.shift_left(bits, lax.broadcasted_iota(jnp.int32, bits.shape, 0))
+    return jnp.sum(bits.astype(jnp.float32), axis=0, keepdims=True)
+
+
 def encode(parts, out, note=None):
     top = functools.reduce(jnp.maximum, [jnp.max(jnp.abs(p), axis=0, keepdims=True) for p in parts])
-    level = jnp.clip(jnp.ceil(STEPS * jnp.log2(top)), -100.0 * STEPS, 128.0 * STEPS)
+    level = jnp.clip(jnp.ceil(STEPS * jnp.log2(top)), -LOWEST, 128.0 * STEPS)
     factor = jnp.exp2(LEVELS - level * (1.0 / STEPS))
+    numbers = [level + LOWEST]
+    if note is not None:
+        rest = note * NOTE_UNITS[0]
+        for _ in NOTE_UNITS:
+            numbers.append(jnp.floor(rest))
+            rest = (rest - numbers[-1]) * 32768.0
     at = 0
     for p in parts:
-        out[at : at + p.shape[0]] = jnp.round(p * factor).astype(jnp.int32).astype(jnp.int16)
+        coded = jnp.round(p * factor).astype(jnp.int32)
+        if at == 0:
+            head = len(numbers) * TILE
+            tiles = [
+                (coded[i * TILE : (i + 1) * TILE] & -2) | bits_of(number)
+                for i, number in enumerate(numbers)
+            ]
+            for i, tile in enumerate(tiles):
+                out[i * TILE : (i + 1) * TILE] = tile.astype(jnp.int16)
+            out[head : p.shape[0]] = coded[head:].astype(jnp.int16)
+        else:
+            out[at : at + p.shape[0]] = coded.astype(jnp.int16)
         at += p.shape[0]
-    rows = jnp.broadcast_to(level, (SCALE_ROWS, level.shape[1]))
-    if note is not None:
-        row = lax.broadcasted_iota(jnp.int32, rows.shape, 0)
-        rest = note * NOTE_UNITS[0]
-        for i, unit in enumerate(NOTE_UNITS):
-            whole = jnp.floor(rest)
-            rows = jnp.where(row == i + 1, whole, rows)
-            rest = (rest - whole) * 32768.0
-    out[at:] = rows.astype(jnp.int32).astype(jnp.int16)
 
 
 def noted(block, width):
-    rows = block[block.shape[0] - SCALE_ROWS :].astype(jnp.int32).astype(jnp.float32)
-    parts = [rows[i + 1 : i + 2, :width] / unit for i, unit in enumerate(NOTE_UNITS)]
+    tiles = [block[i * TILE : (i + 1) * TILE] for i in range(1, 1 + len(NOTE_UNITS))]
+    parts = [number_of(tile)[:, :width] / unit for tile, unit in zip(tiles, NOTE_UNITS)]
     return parts[0] + (parts[1] + parts[2])
 
 
 def decode(block, count):
-    size = (block.shape[0] - SCALE_ROWS) // count
-    level = block[size * count :].astype(jnp.int32).astype(jnp.float32)[0:1]
+    size = block.shape[0] // count
+    level = number_of(block[:TILE]) - LOWEST
     factor = jnp.exp2(level * (1.0 / STEPS) - LEVELS)
     return [
         block[i * size : (i + 1) * size].astype(jnp.int32).astype(jnp.float32) * factor
@@ -104,6 +125,8 @@
 def fetch_kernel(heads_own, wanted, assignment, g, *refs):
     owner, _, core = whereabouts()
     token, outs, sem = refs[-2], refs[:-2], refs[-1]
+    if len(refs) > len(wanted) + 2:
+        token, outs, sem, held, seen = refs[-4], refs[:-4], *refs[-3:]
     token[...] = jnp.zeros_like(token)
     copies = []
     for group, out in zip(wanted, outs[-len(wanted) :]):
@@ -116,10 +139,17 @@
         momentum, logits, old = outs[:3]
         cols = momentum.shape[2]
         for s in range(old.shape[0]):
-            old[s, :, :cols] = momentum[s * CORES + 1 - core]
-        old[0, 0:1, cols : cols + logits.shape[1]] = logits[...]
+            copies.append(
+                pltpu.make_async_copy(momentum.at[s * CORES + 1 - core], held.at[s], sem.at[len(copies)])
+            )
+            copies[-1].start()
+        copies.append(pltpu.make_async_copy(logits, seen, sem.at[len(copies)]))
+        copies[-1].start()
     for copy in copies:
         copy.wait()
+    if len(outs) > len(wanted):
+        old[:, :, :cols] = held[...]
+        old[0, 0:1, cols : cols + logits.shape[1]] = seen[...]
 
 
 def fetch(assignment, g, wanted, rest=(), after=()):
@@ -127,17 +157,23 @@
     count = sum(len(group) for group in wanted)
     ins = [(SMEM, assignment), (ANY, g)]
     outs.append((VMEM, (8, LEFT), jnp.float32))
+    held = []
     if rest:
         momentum, logits = rest
-        slots, rows, _ = momentum.shape
+        slots, rows, cols = momentum.shape
         outs = [(VMEM, (slots // CORES, rows, 2 * LEFT), momentum.dtype)] + outs
-        ins += [(VMEM, momentum), (VMEM, logits)]
+        ins += [(HBM, momentum), (HBM, logits)]
+        count += slots // CORES + 1
+        held = [
+            pltpu.VMEM((slots // CORES, rows, cols), momentum.dtype),
+            pltpu.VMEM(logits.shape, logits.dtype),
+        ]
     return call(
         functools.partial(fetch_kernel, g.shape[0], wanted),
         "fetch_heads",
         ins,
         outs,
-        [pltpu.SemaphoreType.DMA((count,))],
+        [pltpu.SemaphoreType.DMA((count,))] + held,
         after,
         params=SECOND if after else FIRST,
     )
@@ -175,7 +211,7 @@
     aligned = own.ndim == 3
     cols = own.shape[-2]
     width = own.shape[-1] // chips if aligned else own.shape[-1]
-    coded = (VMEM, (len(heads) * cols + SCALE_ROWS, width), jnp.int16)
+    coded = (VMEM, (len(heads) * cols, width), jnp.int16)
     outs = [(VMEM, (len(heads), cols, width), jnp.float32)] + [coded] * (chips - 1)
     return call(
         functools.partial(pair_kernel, chips, aligned, heads, len(passed)),
@@ -209,7 +245,7 @@
 
 def plane_sums(here, away, plain, after, note):
     _, cols, width = here.shape
-    coded = (VMEM, (cols + SCALE_ROWS, width), jnp.int16)
+    coded = (VMEM, (cols, width), jnp.int16)
     outs = [(VMEM, (cols, width), jnp.float32) if p else coded for p in plain]
     return call(
         functools.partial(plane_kernel, plain, len(note)),
@@ -288,7 +324,7 @@
 def grams(assignment, old, near, arrived, chips, heads_own, after):
     cols = old.shape[1]
     rows = cols + (cols - LEFT) // 2
-    coded = (VMEM, (rows + SCALE_ROWS, LEFT), jnp.int16)
+    coded = (VMEM, (rows, LEFT), jnp.int16)
     return call(
         functools.partial(gram_kernel, chips, heads_own),
         "refresh_and_gram",
@@ -329,9 +365,9 @@
     high = norm.astype(jnp.bfloat16).astype(jnp.float32)
     middle = (norm - high).astype(jnp.bfloat16).astype(jnp.float32)
     low = norm - high - middle
-    row = lax.broadcasted_iota(jnp.int32, (SCALE_ROWS, LEFT), 0)
+    row = lax.broadcasted_iota(jnp.int32, (NORM_ROWS, LEFT), 0)
     scales = jnp.where(row == 0, high, jnp.where(row == 1, middle, jnp.where(row == 2, low, 0.0)))
-    out[out.shape[0] - SCALE_ROWS :] = scales.astype(jnp.bfloat16)
+    out[out.shape[0] - NORM_ROWS :] = scales.astype(jnp.bfloat16)
 
 
 def newton(here, away, cols, after):
@@ -339,7 +375,7 @@
         newton_kernel,
         "newton_schulz",
         [(VMEM, value) for value in (here, *away)],
-        [(VMEM, (here.shape[0] + SCALE_ROWS, LEFT), jnp.bfloat16)],
+        [(VMEM, (here.shape[0] + NORM_ROWS, LEFT), jnp.bfloat16)],
         [pltpu.VMEM((cols, cols), jnp.float32)],
         after,
     )
@@ -398,12 +434,19 @@
 
 def weight_kernel(chips, other, rows_all, base, scales, momentum, *refs):
     blocks, refs = refs[:chips], refs[chips:]
-    out, matrix, result, sem = refs[-4:]
+    out, momentum_out, matrix, result, sem, momentum_sem = refs[-6:]
     slots, _, cols = base.shape
     sources = slots // CORES
     step_size = 0.04 * math.sqrt(max(rows_all, cols))
     _, chip, core = whereabouts()
     place = 1 - core if other else core
+    def stored(s):
+        to = momentum_out.at[s * CORES + place]
+        return pltpu.make_async_copy(momentum.at[s], to, momentum_sem.at[s])
+
+    for s in range(sources):
+        stored(s).start()
+
     def written(k):
         return pltpu.make_async_copy(result.at[k], out.at[(chip ^ k) * CORES + place], sem.at[k])
 
@@ -411,9 +454,9 @@
         source = chip ^ k
         slot = source * CORES + place
         block = blocks[k]
-        parts = block[block.shape[0] - SCALE_ROWS :].astype(jnp.float32)
+        parts = block[block.shape[0] - NORM_ROWS :].astype(jnp.float32)
         norm = parts[0:1, 0:1] + parts[1:2, 0:1] + parts[2:3, 0:1]
-        unpack(block[: block.shape[0] - SCALE_ROWS], matrix.at[k])
+        unpack(block[: block.shape[0] - NORM_ROWS], matrix.at[k])
         start = (momentum[source] * (1.0 / norm)).astype(jnp.bfloat16)
         step = (QUINTIC_A * QUINTIC_A) * start.astype(jnp.float32) + small_dot(start, matrix[k])
         result[k] = base[slot] - step * (step_size * scales[pl.ds(slot, 1)])
@@ -429,54 +472,27 @@
         only(k, functools.partial(update, k))
     for k in range(chips):
         only(k, lambda k=k: written(k).wait())
-
-
-def weights(base, scales, momentum, blocks, filled=None, after=()):
+    for s in range(sources):
+        stored(s).wait()
+
+
+def weights(base, scales, momentum, blocks, filled=()):
     chips = len(blocks)
     slots, rows, cols = base.shape
-    other = filled is not None
     ins = [(VMEM, value) for value in (base, scales, momentum, *blocks)]
-    aliases = None
-    if other:
-        aliases = {len(ins): 0}
-        ins.append((HBM, filled))
-    (out,) = call(
-        functools.partial(weight_kernel, chips, other, rows * chips * CORES),
+    aliases = {len(ins) + i: i for i in range(len(filled))}
+    return call(
+        functools.partial(weight_kernel, chips, bool(filled), rows * chips * CORES),
         "update_weight",
-        ins,
-        [(HBM, base.shape, jnp.float32)],
+        ins + [(HBM, value) for value in filled],
+        [(HBM, base.shape, jnp.float32)] * 2,
         [
             pltpu.VMEM((chips, cols, cols), jnp.bfloat16),
             pltpu.VMEM((chips, rows, cols), jnp.float32),
             pltpu.SemaphoreType.DMA((chips,)),
+            pltpu.SemaphoreType.DMA((slots // CORES,)),
         ],
-        after,
-        aliases,
-    )
-    return out
-
-
-def merge_kernel(own, sibling, out, token, sem):
-    token[...] = jnp.zeros_like(token)
-    _, _, core = whereabouts()
-    copies = []
-    for s in range(own.shape[0]):
-        for half, place in ((own, core), (sibling, 1 - core)):
-            to = out.at[s * CORES + place]
-            copies.append(pltpu.make_async_copy(half.at[s], to, sem.at[len(copies)]))
-            copies[-1].start()
-    for copy in copies:
-        copy.wait()
-
-
-def merge(own, sibling):
-    sources, rows, cols = own.shape
-    return call(
-        merge_kernel,
-        "merge_momentum",
-        [(VMEM, own), (VMEM, sibling)],
-        [(HBM, (sources * CORES, rows, cols), jnp.float32), (VMEM, (8, LEFT), jnp.float32)],
-        [pltpu.SemaphoreType.DMA((sources * CORES,))],
+        aliases=aliases,
     )
 
 
@@ -514,24 +530,23 @@
     order = list(range(sources))[::-1]
     size = max(1, sources // GROUPS)
     groups = [order[at : at + size] for at in range(0, sources, size)]
-    first, token = fetch(assignment, g, [[(k, True) for k in groups[0]]])
+    old, first, token = fetch(assignment, g, [[(k, True) for k in groups[0]]], (momentum, max_logits))
     wanted = [[(k, True) for k in order[size:]], [(k, False) for k in groups[0]]]
-    old, others, *own, _ = fetch(assignment, g, wanted, (momentum, max_logits), [token])
+    others, *own, _ = fetch(assignment, g, wanted, after=[token])
     siblings = [swap(first, 1)]
 
     near, arrived, before, sent = None, {}, [], []
     for i, ks in enumerate(groups):
         heads = [(j, j + (size * (i - 1) if i else 0)) for j in range(len(ks))]
-        passed = [others, old] if i == 0 else []
+        passed = [others] if i == 0 else []
         note = [peak] if i == len(groups) - 2 else []
         values = pair_sums(own[i], siblings[min(i, 1)], heads, chips, before, note, passed)
         here, away = values[0], values[1:chips]
         if i == 0:
-            others, old = values[chips:]
+            siblings.append(swap(values[chips], 1))
+            turned, peak = turn(momentum, swap(old, 1), max_logits)
             wanted = [[(k, False) for k in ks] for ks in groups[1:]]
-            own += fetch(assignment, g, wanted, after=[away[0]])
-            siblings.append(swap(others, 1))
-            turned, peak = turn(momentum, swap(old, 1), max_logits)
+            *own[1:], _ = fetch(assignment, g, wanted, after=[away[0]])
         away = [swap(value, CORES * (k + 1)) for k, value in enumerate(away)]
         before = away[:2] if i else [away[0], turned]
         totals = list(plane_sums(here, away, [k == 0 for k in ks], sent, note))
@@ -552,15 +567,14 @@
     arrived = [arrived[k] for k in range(1, sources)]
     new, here, *away = grams(assignment, turned, near, arrived, chips, heads_own, [])
     away = [swap(value, CORES * (k + 1)) for k, value in enumerate(away)]
-    result = newton(here, away, momentum.shape[2], [])
+    result = newton(here, away[::-1], momentum.shape[2], [])
     own_new, sibling_new = turn_back(new, [result])
 
     sibling_new = swap(sibling_new, 1)
     results = [result] + [swap(result, CORES * k) for k in range(1, chips)]
     sibling_results = [swap(value, 1) for value in results]
-    momentum_out, token = merge(own_new, sibling_new)
-    q_weight_out = weights(base, scales, own_new, results, after=[token])
-    q_weight_out = weights(base, scales, sibling_new, sibling_results, q_weight_out)
+    filled = weights(base, scales, own_new, results)
+    q_weight_out, momentum_out = weights(base, scales, sibling_new, sibling_results, filled)
     return (momentum_out, q_weight_out, k_weight_out)
 
 

time: 67.1 us -> 64.8 us (0.966)
  waiting for transfers between devices: 17.5 us -> 16.5 us
  local copies, waits for them, and re-layouts: 2.14 us -> 1.33 us
    unnamed x18, local copies, waits for them, and re-layouts: 2.14 us -> 1.33 us
    ppermute x3, waiting for transfers between devices: 2.83 us -> 2.04 us  [body(): lax.ppermute(total, 'owner', [(j, j ^ k) for j in range(sources)])]
    pallas_call x20 -> x19, Pallas kernels: 17 us -> 16.7 us  [call(): pl.pallas_call(whole, in_specs=[spec for spec, _ in ins] + [ANY] * len(af...]
  transfers between devices with their start and end apart: 29 -> 29, of which waited for: 15 -> 14; matrix products, arithmetic and copies ran while one was open for 0% -> 0% of each run, Pallas kernels for 15% -> 14%
where the time goes in v4:
time: 64.8 us; the launch traced here: 64.6 us
  starting transfers between devices  29.3 us (45%)
  Pallas kernels  16.7 us (26%)
  waiting for transfers between devices  16.5 us (25%)
  local copies, waits for them, and re-layouts  1.33 us (2%)
  between operations  0.89 us (1%)
    ppermute x26, starting transfers between devices, swap(): return lax.ppermute(value, PLANE, [(i, i ^ bits) for i in range(devices)])  25.5 us
    pallas_call x19, Pallas kernels, call(): pl.pallas_call(whole, in_specs=[spec for spec, _ in ins] + [ANY] * len(af...  16.7 us
    ppermute x26, waiting for transfers between devices, swap(): return lax.ppermute(value, PLANE, [(i, i ^ bits) for i in range(devices)])  14.4 us
    ppermute x3, starting transfers between devices, body(): lax.ppermute(total, 'owner', [(j, j ^ k) for j in range(sources)])  3.81 us
    ppermute x3, waiting for transfers between devices, body(): lax.ppermute(total, 'owner', [(j, j ^ k) for j in range(sources)])  2.04 us
    unnamed x18, local copies, waits for them, and re-layouts  1.33 us
  transfers between devices with their start and end apart: 29, of which 14 were waited for; matrix products, arithmetic and copies ran while one was open for 0% of the time, Pallas kernels for 14%

profile of v4, /device:TPU:0, one launch (start us, length us, event | category | flops | bytes accessed | tf_op | source)
XLA Modules:
  0.0 64.6 jit_solution(5749268426654283839)
XLA Ops:
  0.6 0.0 copy-start.5
  0.6 0.6 %copy-done.5 = s32[32,1]{0,1:T(1,128)S(1)} copy-done((s32[32,1]{0,1:T(1,128)S(1)}, s32[32,1]{0,1:T(1,128)}, u32[]{:S(2)}) %copy-start.5) | copy-done | bytes 152
  1.3 0.7 %copy-done.7 = f32[1,32]{1,0:T(1,128)S(1)} copy-done((f32[1,32]{1,0:T(1,128)S(1)}, f32[1,32]{1,0:T(1,128)}, u32[]{:S(2)}) %copy-start.7) | copy-done | bytes 152
  1.9 2.3 %fetch_heads.3 = (f32[4,192,256]{2,1,0:T(8,128)S(1)}, bf16[1,192,1536]{2,1,0:T(8,128)(2,1)S(1)}, f32[8,128]{1,0:T(8,128)S(1)}) custom-call(s32[1,32]{1,0:T(1,128)S(1)} %bitcast.7, bf16[8,192,1536]{2,1,0:T(8,128)(2,1)} %bitcast.4, f32[8,192,192]{2,1,0:T(8,128)} %refs_0_.1, f32[1,32]{1,0:T(1,128)S(1)} %copy-done.7), custom_call_target="tpu_custom_call" | custom-call | tf_op jit(solution)/shard_map/fetch_heads/pallas_call | solution.py:50
  4.3 0.5 collective-permute-start
  4.8 1.7 %fetch_heads.4 = (bf16[3,192,1536]{2,1,0:T(8,128)(2,1)S(1)}, bf16[1,192,1536]{2,1,0:T(8,128)(2,1)S(1)}, f32[8,128]{1,0:T(8,128)}) custom-call(s32[1,32]{1,0:T(1,128)S(1)} %bitcast.8, bf16[8,192,1536]{2,1,0:T(8,128)(2,1)S(1)} %bitcast.5, f32[8,128]{1,0:T(8,128)S(1)} %get-tuple-element.45.refs_2_), custom_call_target="tpu_custom_call" | custom-call | tf_op jit(solution)/shard_map/fetch_heads/pallas_call | solution.py:50
  6.5 0.0 copy-start.6
  6.6 0.0 collective-permute-done.refs_1_
  6.6 0.3 pair_sum.4
  6.9 0.4 collective-permute-start.1
  7.3 0.2 collective-permute-start.2
  7.4 2.9 %collective-permute-start.3 = (s16[192,384]{1,0:T(8,128)(2,1)S(1)}, s16[192,384]{1,0:T(8,128)(2,1)S(1)}, u32[]{:S(2)}, u32[]{:S(2)}) collective-permute-start(s16[192,384]{1,0:T(8,128)(2,1)S(1)} %get-tuple-element.49.refs_2_), channel_id=1, source_target_pairs={{0,2},{1,3},{2,0},{3,1},{16,18},{17,19},{18,16},{19,17},{4,6},{5,7... | collective-permute-start | bytes 442376 | tf_op jit(solution)/shard_map/ppermute | solution.py:525
  10.3 1.5 %collective-permute-start.10 = (s16[192,384]{1,0:T(8,128)(2,1)S(1)}, s16[192,384]{1,0:T(8,128)(2,1)S(1)}, u32[]{:S(2)}, u32[]{:S(2)}) collective-permute-start(s16[192,384]{1,0:T(8,128)(2,1)S(1)} %get-tuple-element.65), channel_id=1, source_target_pairs={{0,16},{1,17},{2,18},{3,19},{16,0},{17,1},{18,2},{19,3},{4,20},{5,... | collective-permute-start | bytes 442376 | tf_op jit(solution)/shard_map/ppermute | solution.py:525
  11.8 1.6 %fetch_heads.5 = (bf16[1,192,1536]{2,1,0:T(8,128)(2,1)S(1)}, bf16[1,192,1536]{2,1,0:T(8,128)(2,1)S(1)}, bf16[1,192,1536]{2,1,0:T(8,128)(2,1)S(1)}, f32[8,128]{1,0:T(8,128)}) custom-call(s32[1,32]{1,0:T(1,128)S(1)} %bitcast.9, bf16[8,192,1536]{2,1,0:T(8,128)(2,1)S(1)} %bitcast.6, s16[192,384]{1,0:T(8,128)(2,1)S(1)} %get-tuple-element.49.refs_2_), custom_call_target="tpu_custom_call" | custom-call | tf_op jit(solution)/shard_map/fetch_heads/pallas_call | solution.py:50
  13.5 0.7 %turn_momentum.1 = (f32[4,192,384]{2,1,0:T(8,128)S(1)}, f32[1,32]{1,0:T(1,128)S(1)}) custom-call(f32[8,192,192]{2,1,0:T(8,128)S(1)} %copy-done.1, f32[4,192,256]{2,1,0:T(8,128)S(1)} %collective-permute-done.2.refs_1_, f32[1,32]{1,0:T(1,128)S(1)} %copy-done.8), custom_call_target="tpu_custom_call" | custom-call | tf_op jit(solution)/shard_map/turn_momentum/pallas_call | solution.py:50
  14.2 0.7 %collective-permute-done.3.refs_2_.refs_1_ = s16[192,384]{1,0:T(8,128)(2,1)S(1)} collective-permute-done((s16[192,384]{1,0:T(8,128)(2,1)S(1)}, s16[192,384]{1,0:T(8,128)(2,1)S(1)}, u32[]{:S(2)}, u32[]{:S(2)}) %collective-permute-start.3) | collective-permute-done | bytes 147488 | tf_op jit(solution)/shard_map/ppermute | solution.py:525
  14.9 0.3 pair_sum.5
  15.2 2.1 %collective-permute-start.4 = (s16[192,384]{1,0:T(8,128)(2,1)S(1)}, s16[192,384]{1,0:T(8,128)(2,1)S(1)}, u32[]{:S(2)}, u32[]{:S(2)}) collective-permute-start(s16[192,384]{1,0:T(8,128)(2,1)S(1)} %get-tuple-element.56), channel_id=1, source_target_pairs={{0,2},{1,3},{2,0},{3,1},{16,18},{17,19},{18,16},{19,17},{4,6},{5,7... | collective-permute-start | bytes 442376 | tf_op jit(solution)/shard_map/ppermute | solution.py:525
  17.3 1.5 %collective-permute-start.5 = (s16[192,384]{1,0:T(8,128)(2,1)S(1)}, s16[192,384]{1,0:T(8,128)(2,1)S(1)}, u32[]{:S(2)}, u32[]{:S(2)}) collective-permute-start(s16[192,384]{1,0:T(8,128)(2,1)S(1)} %get-tuple-element.57), channel_id=1, source_target_pairs={{0,16},{1,17},{2,18},{3,19},{16,0},{17,1},{18,2},{19,3},{4,20},{5,... | collective-permute-start | bytes 442376 | tf_op jit(solution)/shard_map/ppermute | solution.py:525
  18.9 0.1 collective-permute-done.10.refs_2_
  18.9 0.6 collective-permute-done.11.refs_3_
  19.5 0.2 plane_sum.4
  19.8 3.7 %collective-permute-start.12 = (s16[192,384]{1,0:T(8,128)(2,1)S(1)}, s16[192,384]{1,0:T(8,128)(2,1)S(1)}, u32[]{:S(2)}, u32[]{:S(2)}) collective-permute-start(s16[192,384]{1,0:T(8,128)(2,1)S(1)} %plane_sum.4), channel_id=1, source_target_pairs={{0,12},{4,8},{8,4},{12,0},{1,13},{5,9},{9,5},{13,1},{2,14},{6,10},... | collective-permute-start | bytes 442376 | tf_op jit(solution)/shard_map/ppermute | solution.py:562
  23.4 1.5 %collective-permute-start.9 = (s16[192,384]{1,0:T(8,128)(2,1)S(1)}, s16[192,384]{1,0:T(8,128)(2,1)S(1)}, u32[]{:S(2)}, u32[]{:S(2)}) collective-permute-start(s16[192,384]{1,0:T(8,128)(2,1)S(1)} %get-tuple-element.63), channel_id=1, source_target_pairs={{0,18},{1,19},{2,16},{3,17},{16,2},{17,3},{18,0},{19,1},{4,22},{5,... | collective-permute-start | bytes 442376 | tf_op jit(solution)/shard_map/ppermute | solution.py:525
  25.0 0.3 pair_sum.6
  25.3 1.7 %collective-permute-start.6 = (s16[192,384]{1,0:T(8,128)(2,1)S(1)}, s16[192,384]{1,0:T(8,128)(2,1)S(1)}, u32[]{:S(2)}, u32[]{:S(2)}) collective-permute-start(s16[192,384]{1,0:T(8,128)(2,1)S(1)} %get-tuple-element.59), channel_id=1, source_target_pairs={{0,2},{1,3},{2,0},{3,1},{16,18},{17,19},{18,16},{19,17},{4,6},{5,7... | collective-permute-start | bytes 442376 | tf_op jit(solution)/shard_map/ppermute | solution.py:525
  27.0 0.3 collective-permute-start.7
  27.3 1.5 %collective-permute-start.8 = (s16[192,384]{1,0:T(8,128)(2,1)S(1)}, s16[192,384]{1,0:T(8,128)(2,1)S(1)}, u32[]{:S(2)}, u32[]{:S(2)}) collective-permute-start(s16[192,384]{1,0:T(8,128)(2,1)S(1)} %get-tuple-element.61), channel_id=1, source_target_pairs={{0,18},{1,19},{2,16},{3,17},{16,2},{17,3},{18,0},{19,1},{4,22},{5,... | collective-permute-start | bytes 442376 | tf_op jit(solution)/shard_map/ppermute | solution.py:525
  28.9 2.3 %collective-permute-done.9.refs_3_ = s16[192,384]{1,0:T(8,128)(2,1)S(1)} collective-permute-done((s16[192,384]{1,0:T(8,128)(2,1)S(1)}, s16[192,384]{1,0:T(8,128)(2,1)S(1)}, u32[]{:S(2)}, u32[]{:S(2)}) %collective-permute-start.9) | collective-permute-done | bytes 147488 | tf_op jit(solution)/shard_map/ppermute | solution.py:525
  31.2 0.2 plane_sum.5
  31.4 0.1 collective-permute-start.13
  31.4 1.5 %collective-permute-done.6.refs_1_.refs_2_ = s16[192,384]{1,0:T(8,128)(2,1)S(1)} collective-permute-done((s16[192,384]{1,0:T(8,128)(2,1)S(1)}, s16[192,384]{1,0:T(8,128)(2,1)S(1)}, u32[]{:S(2)}, u32[]{:S(2)}) %collective-permute-start.6) | collective-permute-done | bytes 147488 | tf_op jit(solution)/shard_map/ppermute | solution.py:525
  32.9 0.3 collective-permute-done.7.refs_2_.refs_3_
  33.3 0.3 pair_sum.7
  33.6 1.4 %collective-permute-start.14 = (s16[192,384]{1,0:T(8,128)(2,1)S(1)}, s16[192,384]{1,0:T(8,128)(2,1)S(1)}, u32[]{:S(2)}, u32[]{:S(2)}) collective-permute-start(s16[192,384]{1,0:T(8,128)(2,1)S(1)} %get-tuple-element.72), channel_id=1, source_target_pairs={{0,2},{1,3},{2,0},{3,1},{16,18},{17,19},{18,16},{19,17},{4,6},{5,7... | collective-permute-start | bytes 442376 | tf_op jit(solution)/shard_map/ppermute | solution.py:525
  35.0 0.8 %collective-permute-start.15 = (s16[192,384]{1,0:T(8,128)(2,1)S(1)}, s16[192,384]{1,0:T(8,128)(2,1)S(1)}, u32[]{:S(2)}, u32[]{:S(2)}) collective-permute-start(s16[192,384]{1,0:T(8,128)(2,1)S(1)} %get-tuple-element.73), channel_id=1, source_target_pairs={{0,16},{1,17},{2,18},{3,19},{16,0},{17,1},{18,2},{19,3},{4,20},{5,... | collective-permute-start | bytes 442376 | tf_op jit(solution)/shard_map/ppermute | solution.py:525
  35.8 1.3 %collective-permute-start.16 = (s16[192,384]{1,0:T(8,128)(2,1)S(1)}, s16[192,384]{1,0:T(8,128)(2,1)S(1)}, u32[]{:S(2)}, u32[]{:S(2)}) collective-permute-start(s16[192,384]{1,0:T(8,128)(2,1)S(1)} %get-tuple-element.74), channel_id=1, source_target_pairs={{0,18},{1,19},{2,16},{3,17},{16,2},{17,3},{18,0},{19,1},{4,22},{5,... | collective-permute-start | bytes 442376 | tf_op jit(solution)/shard_map/ppermute | solution.py:525
  37.1 1.1 %collective-permute-done.13.refs_5_.refs_4_ = s16[192,384]{1,0:T(8,128)(2,1)S(1)} collective-permute-done((s16[192,384]{1,0:T(8,128)(2,1)S(1)}, s16[192,384]{1,0:T(8,128)(2,1)S(1)}, u32[]{:S(2)}, u32[]{:S(2)}) %collective-permute-start.13) | collective-permute-done | bytes 147488 | tf_op jit(solution)/shard_map/ppermute | solution.py:562
  38.2 0.2 plane_sum.6
  38.4 0.1 collective-permute-start.17
  38.5 1.3 %scale_keys.1.refs_6_ = f32[8,64,128]{2,1,0:T(8,128)} custom-call(f32[1,32]{1,0:T(1,128)S(1)} %get-tuple-element.67.refs_1_.refs_0_, f32[8,64,128]{2,1,0:T(8,128)S(1)} %copy-done.4), custom_call_target="tpu_custom_call" | custom-call | tf_op jit(solution)/shard_map/scale_keys/pallas_call | solution.py:50
  39.8 0.8 %scale_weight.1 = (f32[8,192,192]{2,1,0:T(8,128)S(1)}, f32[8,192]{1,0:T(8,128)S(1)}) custom-call(s32[1,32]{1,0:T(1,128)S(1)} %bitcast.10, f32[1,32]{1,0:T(1,128)S(1)} %get-tuple-element.67.refs_1_.refs_0_, f32[8,192,192]{2,1,0:T(8,128)S(1)} %copy-done.2), custom_call_target="tpu_custom_call" | custom-call | tf_op jit(solution)/shard_map/scale_weight/pallas_call | solution.py:50
  40.6 2.1 %collective-permute-done.15.refs_2_ = s16[192,384]{1,0:T(8,128)(2,1)S(1)} collective-permute-done((s16[192,384]{1,0:T(8,128)(2,1)S(1)}, s16[192,384]{1,0:T(8,128)(2,1)S(1)}, u32[]{:S(2)}, u32[]{:S(2)}) %collective-permute-start.15) | collective-permute-done | bytes 147488 | tf_op jit(solution)/shard_map/ppermute | solution.py:525
  42.6 1.0 %collective-permute-done.17.refs_4_.refs_3_ = s16[192,384]{1,0:T(8,128)(2,1)S(1)} collective-permute-done((s16[192,384]{1,0:T(8,128)(2,1)S(1)}, s16[192,384]{1,0:T(8,128)(2,1)S(1)}, u32[]{:S(2)}, u32[]{:S(2)}) %collective-permute-start.17) | collective-permute-done | bytes 147488 | tf_op jit(solution)/shard_map/ppermute | solution.py:562
  43.6 0.1 plane_sum.7.refs_2_
  43.8 1.5 %refresh_and_gram.1 = (f32[4,192,384]{2,1,0:T(8,128)S(1)}, f32[224,128]{1,0:T(8,128)S(1)}, s16[224,128]{1,0:T(8,128)(2,1)S(1)}, s16[224,128]{1,0:T(8,128)(2,1)S(1)}, s16[224,128]{1,0:T(8,128)(2,1)S(1)}) custom-call(s32[1,32]{1,0:T(1,128)S(1)} %bitcast.11, f32[4,192,384]{2,1,0:T(8,128)S(1)} %get-tuple-element.55.refs_3_.refs_1_, ...), custom_call_target="tpu_custom_call" | custom-call | tf_op jit(solution)/shard_map/refresh_and_gram/pallas_call | solution.py:50
  45.2 1.5 %collective-permute-start.18 = (s16[224,128]{1,0:T(8,128)(2,1)S(1)}, s16[224,128]{1,0:T(8,128)(2,1)S(1)}, u32[]{:S(2)}, u32[]{:S(2)}) collective-permute-start(s16[224,128]{1,0:T(8,128)(2,1)S(1)} %get-tuple-element.78), channel_id=1, source_target_pairs={{0,18},{1,19},{2,16},{3,17},{16,2},{17,3},{18,0},{19,1},{4,22},{5,... | collective-permute-start | bytes 172040 | tf_op jit(solution)/shard_map/ppermute | solution.py:525
  46.7 1.6 %collective-permute-start.19 = (s16[224,128]{1,0:T(8,128)(2,1)S(1)}, s16[224,128]{1,0:T(8,128)(2,1)S(1)}, u32[]{:S(2)}, u32[]{:S(2)}) collective-permute-start(s16[224,128]{1,0:T(8,128)(2,1)S(1)} %get-tuple-element.79), channel_id=1, source_target_pairs={{0,16},{1,17},{2,18},{3,19},{16,0},{17,1},{18,2},{19,3},{4,20},{5,... | collective-permute-start | bytes 172040 | tf_op jit(solution)/shard_map/ppermute | solution.py:525
  48.3 0.5 collective-permute-start.20
  48.8 1.6 %collective-permute-done.18.refs_1_ = s16[224,128]{1,0:T(8,128)(2,1)S(1)} collective-permute-done((s16[224,128]{1,0:T(8,128)(2,1)S(1)}, s16[224,128]{1,0:T(8,128)(2,1)S(1)}, u32[]{:S(2)}, u32[]{:S(2)}) %collective-permute-start.18) | collective-permute-done | bytes 57376 | tf_op jit(solution)/shard_map/ppermute | solution.py:525
  50.4 0.6 collective-permute-done.19.refs_2_
  51.0 1.5 %collective-permute-done.20.refs_3_ = s16[224,128]{1,0:T(8,128)(2,1)S(1)} collective-permute-done((s16[224,128]{1,0:T(8,128)(2,1)S(1)}, s16[224,128]{1,0:T(8,128)(2,1)S(1)}, u32[]{:S(2)}, u32[]{:S(2)}) %collective-permute-start.20) | collective-permute-done | bytes 57376 | tf_op jit(solution)/shard_map/ppermute | solution.py:525
  52.5 1.2 %newton_schulz.1.refs_1_.refs_3_ = bf16[240,128]{1,0:T(8,128)(2,1)S(1)} custom-call(f32[224,128]{1,0:T(8,128)S(1)} %get-tuple-element.77.refs_0_, s16[224,128]{1,0:T(8,128)(2,1)S(1)} %collective-permute-done.18.refs_1_, s16[224,128]{1,0:T(8,128)(2,1)S(1)} %collective-permute-done.19.refs_2_, s16[224,128]{1,0:T(8,128)(2,1)S(1)} %collective-permute-done.20.refs_3_), custom_call_target="tpu_custom_call" | custom-call | tf_op jit(solution)/shard_map/newton_schulz/pallas_call | solution.py:50
  53.7 0.7 %turn_back.1 = (f32[4,192,192]{2,1,0:T(8,128)S(1)}, f32[4,192,192]{2,1,0:T(8,128)S(1)}) custom-call(f32[4,192,384]{2,1,0:T(8,128)S(1)} %get-tuple-element.76.refs_0_, bf16[240,128]{1,0:T(8,128)(2,1)S(1)} %newton_schulz.1.refs_1_.refs_3_), custom_call_target="tpu_custom_call" | custom-call | tf_op jit(solution)/shard_map/turn_back/pallas_call | solution.py:50
  54.4 0.1 collective-permute-start.21
  54.4 1.3 %collective-permute-start.27 = (bf16[240,128]{1,0:T(8,128)(2,1)S(1)}, bf16[240,128]{1,0:T(8,128)(2,1)S(1)}, u32[]{:S(2)}, u32[]{:S(2)}) collective-permute-start(bf16[240,128]{1,0:T(8,128)(2,1)S(1)} %newton_schulz.1.refs_1_.refs_3_), channel_id=1, source_target_pairs={{0,18},{1,19},{2,16},{3,17},{16,2},{17,3},{18,0},{19,1},{4,22},{5,... | collective-permute-start | bytes 184328 | tf_op jit(solution)/shard_map/ppermute | solution.py:525
  55.8 0.7 %collective-permute-start.25 = (bf16[240,128]{1,0:T(8,128)(2,1)S(1)}, bf16[240,128]{1,0:T(8,128)(2,1)S(1)}, u32[]{:S(2)}, u32[]{:S(2)}) collective-permute-start(bf16[240,128]{1,0:T(8,128)(2,1)S(1)} %newton_schulz.1.refs_1_.refs_3_), channel_id=1, source_target_pairs={{0,16},{1,17},{2,18},{3,19},{16,0},{17,1},{18,2},{19,3},{4,20},{5,... | collective-permute-start | bytes 184328 | tf_op jit(solution)/shard_map/ppermute | solution.py:525
  56.4 1.6 %collective-permute-start.23 = (bf16[240,128]{1,0:T(8,128)(2,1)S(1)}, bf16[240,128]{1,0:T(8,128)(2,1)S(1)}, u32[]{:S(2)}, u32[]{:S(2)}) collective-permute-start(bf16[240,128]{1,0:T(8,128)(2,1)S(1)} %newton_schulz.1.refs_1_.refs_3_), channel_id=1, source_target_pairs={{0,2},{1,3},{2,0},{3,1},{16,18},{17,19},{18,16},{19,17},{4,6},{5,7... | collective-permute-start | bytes 184328 | tf_op jit(solution)/shard_map/ppermute | solution.py:525
  58.0 1.9 %collective-permute-done.27.refs_6_ = bf16[240,128]{1,0:T(8,128)(2,1)S(1)} collective-permute-done((bf16[240,128]{1,0:T(8,128)(2,1)S(1)}, bf16[240,128]{1,0:T(8,128)(2,1)S(1)}, u32[]{:S(2)}, u32[]{:S(2)}) %collective-permute-start.27) | collective-permute-done | bytes 61472 | tf_op jit(solution)/shard_map/ppermute | solution.py:525
  59.9 1.2 %collective-permute-done.25.refs_5_ = bf16[240,128]{1,0:T(8,128)(2,1)S(1)} collective-permute-done((bf16[240,128]{1,0:T(8,128)(2,1)S(1)}, bf16[240,128]{1,0:T(8,128)(2,1)S(1)}, u32[]{:S(2)}, u32[]{:S(2)}) %collective-permute-start.25) | collective-permute-done | bytes 61472 | tf_op jit(solution)/shard_map/ppermute | solution.py:525
  61.1 0.0 collective-permute-start.26
  61.1 0.5 collective-permute-start.24
  61.6 1.4 %update_weight.2 = (f32[8,192,192]{2,1,0:T(8,128)}, f32[8,192,192]{2,1,0:T(8,128)}) custom-call(f32[8,192,192]{2,1,0:T(8,128)S(1)} %get-tuple-element.68.refs_5_.refs_0_, f32[8,192]{1,0:T(8,128)S(1)} %get-tuple-element.69.refs_1_, f32[4,192,192]{2,1,0:T(8,128)S(1)} %get-tuple-element.82.refs_2_, bf16[240,128]{1,0:T(8,128)(2,1)S(1)} %newton_schulz.1.refs_1_.refs_3_, ...), custom_call_target="tpu_custom_call" | custom-call | tf_op jit(solution)/shard_map/update_weight/pallas_call | solution.py:50
  63.1 1.5 %update_weight.3 = (f32[8,192,192]{2,1,0:T(8,128)}, f32[8,192,192]{2,1,0:T(8,128)}) custom-call(f32[8,192,192]{2,1,0:T(8,128)S(1)} %get-tuple-element.68.refs_5_.refs_0_, f32[8,192]{1,0:T(8,128)S(1)} %get-tuple-element.69.refs_1_, f32[4,192,192]{2,1,0:T(8,128)S(1)} %collective-permute-done.21.refs_2_, ...), custom_call_target="tpu_custom_call", output_to_operand_aliasing={{0}: (7, {}), {1}: (8, {})} | custom-call | tf_op jit(solution)/shard_map/update_weight/pallas_call | solution.py:50
  (31 shorter events, 0.1 us)
Async XLA Ops:
  0.6 0.7 %copy-start.5 = (s32[32,1]{0,1:T(1,128)S(1)}, s32[32,1]{0,1:T(1,128)}, u32[]{:S(2)}) copy-start(s32[32,1]{0,1:T(1,128)} %param.7) | copy-start | bytes 388
  1.3 0.7 %copy-start.7 = (f32[1,32]{1,0:T(1,128)S(1)}, f32[1,32]{1,0:T(1,128)}, u32[]{:S(2)}) copy-start(f32[1,32]{1,0:T(1,128)} %refs_2_.4) | copy-start | bytes 388
  1.9 2.8 %copy-start = (bf16[1,1536,8,192]{1,3,2,0:T(8,128)(2,1)S(1)}, bf16[1,1536,8,192]{1,3,2,0:T(8,128)(2,1)}, u32[]{:S(2)}) copy-start(bf16[1,1536,8,192]{1,3,2,0:T(8,128)(2,1)} %param.6) | copy-start | bytes 14155780
  4.3 2.3 %collective-permute-start = (bf16[1,192,1536]{2,1,0:T(8,128)(2,1)S(1)}, bf16[1,192,1536]{2,1,0:T(8,128)(2,1)S(1)}, u32[]{:S(2)}, u32[]{:S(2)}) collective-permute-start(bf16[1,192,1536]{2,1,0:T(8,128)(2,1)S(1)} %get-tuple-element.47), channel_id=1, source_target_pairs={{0,1},{1,0},{2,3},{3,2},{16,17},{17,16},{18,19},{19,18},{4,5},{5,4... | collective-permute-start | bytes 1769480 | tf_op jit(solution)/shard_map/ppermute | solution.py:525
  6.5 5.3 %copy-start.6 = (s32[32,1]{0,1:T(1,128)S(1)}, s32[32,1]{0,1:T(1,128)}, u32[]{:S(2)}) copy-start(s32[32,1]{0,1:T(1,128)} %param.7) | copy-start | bytes 388
  6.9 8.1 %collective-permute-start.1 = (bf16[3,192,1536]{2,1,0:T(8,128)(2,1)S(1)}, bf16[3,192,1536]{2,1,0:T(8,128)(2,1)S(1)}, u32[]{:S(2)}, u32[]{:S(2)}) collective-permute-start(bf16[3,192,1536]{2,1,0:T(8,128)(2,1)S(1)} %get-tuple-element.51), channel_id=1, source_target_pairs={{0,1},{1,0},{2,3},{3,2},{16,17},{17,16},{18,19},{19,18},{4,5},{5,4... | collective-permute-start | bytes 5308424 | tf_op jit(solution)/shard_map/ppermute | solution.py:525
  7.3 6.1 %collective-permute-start.2 = (f32[4,192,256]{2,1,0:T(8,128)S(1)}, f32[4,192,256]{2,1,0:T(8,128)S(1)}, u32[]{:S(2)}, u32[]{:S(2)}) collective-permute-start(f32[4,192,256]{2,1,0:T(8,128)S(1)} %get-tuple-element.52), channel_id=1, source_target_pairs={{0,1},{1,0},{2,3},{3,2},{16,17},{17,16},{18,19},{19,18},{4,5},{5,4... | collective-permute-start | bytes 2359304 | tf_op jit(solution)/shard_map/ppermute | solution.py:525
  7.4 7.5 %collective-permute-start.3 = (s16[192,384]{1,0:T(8,128)(2,1)S(1)}, s16[192,384]{1,0:T(8,128)(2,1)S(1)}, u32[]{:S(2)}, u32[]{:S(2)}) collective-permute-start(s16[192,384]{1,0:T(8,128)(2,1)S(1)} %get-tuple-element.49.refs_2_), channel_id=1, source_target_pairs={{0,2},{1,3},{2,0},{3,1},{16,18},{17,19},{18,16},{19,17},{4,6},{5,7... | collective-permute-start | bytes 442376 | tf_op jit(solution)/shard_map/ppermute | solution.py:525
  10.3 8.6 %collective-permute-start.10 = (s16[192,384]{1,0:T(8,128)(2,1)S(1)}, s16[192,384]{1,0:T(8,128)(2,1)S(1)}, u32[]{:S(2)}, u32[]{:S(2)}) collective-permute-start(s16[192,384]{1,0:T(8,128)(2,1)S(1)} %get-tuple-element.65), channel_id=1, source_target_pairs={{0,16},{1,17},{2,18},{3,19},{16,0},{17,1},{18,2},{19,3},{4,20},{5,... | collective-permute-start | bytes 442376 | tf_op jit(solution)/shard_map/ppermute | solution.py:525
  11.8 1.6 %copy-start.1 = (f32[8,192,192]{2,1,0:T(8,128)S(1)}, f32[8,192,192]{2,1,0:T(8,128)}, u32[]{:S(2)}) copy-start(f32[8,192,192]{2,1,0:T(8,128)} %refs_0_.1) | copy-start | bytes 3538948
  11.8 1.6 %copy-start.8 = (f32[1,32]{1,0:T(1,128)S(1)}, f32[1,32]{1,0:T(1,128)}, u32[]{:S(2)}) copy-start(f32[1,32]{1,0:T(1,128)} %refs_2_.4) | copy-start | bytes 388
  11.8 7.7 %collective-permute-start.11 = (s16[192,384]{1,0:T(8,128)(2,1)S(1)}, s16[192,384]{1,0:T(8,128)(2,1)S(1)}, u32[]{:S(2)}, u32[]{:S(2)}) collective-permute-start(s16[192,384]{1,0:T(8,128)(2,1)S(1)} %get-tuple-element.66), channel_id=1, source_target_pairs={{0,18},{1,19},{2,16},{3,17},{16,2},{17,3},{18,0},{19,1},{4,22},{5,... | collective-permute-start | bytes 442376 | tf_op jit(solution)/shard_map/ppermute | solution.py:525
  15.2 9.8 %collective-permute-start.4 = (s16[192,384]{1,0:T(8,128)(2,1)S(1)}, s16[192,384]{1,0:T(8,128)(2,1)S(1)}, u32[]{:S(2)}, u32[]{:S(2)}) collective-permute-start(s16[192,384]{1,0:T(8,128)(2,1)S(1)} %get-tuple-element.56), channel_id=1, source_target_pairs={{0,2},{1,3},{2,0},{3,1},{16,18},{17,19},{18,16},{19,17},{4,6},{5,7... | collective-permute-start | bytes 442376 | tf_op jit(solution)/shard_map/ppermute | solution.py:525
  17.3 7.6 %collective-permute-start.5 = (s16[192,384]{1,0:T(8,128)(2,1)S(1)}, s16[192,384]{1,0:T(8,128)(2,1)S(1)}, u32[]{:S(2)}, u32[]{:S(2)}) collective-permute-start(s16[192,384]{1,0:T(8,128)(2,1)S(1)} %get-tuple-element.57), channel_id=1, source_target_pairs={{0,16},{1,17},{2,18},{3,19},{16,0},{17,1},{18,2},{19,3},{4,20},{5,... | collective-permute-start | bytes 442376 | tf_op jit(solution)/shard_map/ppermute | solution.py:525
  19.8 9.1 %collective-permute-start.12 = (s16[192,384]{1,0:T(8,128)(2,1)S(1)}, s16[192,384]{1,0:T(8,128)(2,1)S(1)}, u32[]{:S(2)}, u32[]{:S(2)}) collective-permute-start(s16[192,384]{1,0:T(8,128)(2,1)S(1)} %plane_sum.4), channel_id=1, source_target_pairs={{0,12},{4,8},{8,4},{12,0},{1,13},{5,9},{9,5},{13,1},{2,14},{6,10},... | collective-permute-start | bytes 442376 | tf_op jit(solution)/shard_map/ppermute | solution.py:562
  23.4 7.7 %collective-permute-start.9 = (s16[192,384]{1,0:T(8,128)(2,1)S(1)}, s16[192,384]{1,0:T(8,128)(2,1)S(1)}, u32[]{:S(2)}, u32[]{:S(2)}) collective-permute-start(s16[192,384]{1,0:T(8,128)(2,1)S(1)} %get-tuple-element.63), channel_id=1, source_target_pairs={{0,18},{1,19},{2,16},{3,17},{16,2},{17,3},{18,0},{19,1},{4,22},{5,... | collective-permute-start | bytes 442376 | tf_op jit(solution)/shard_map/ppermute | solution.py:525
  25.3 7.7 %collective-permute-start.6 = (s16[192,384]{1,0:T(8,128)(2,1)S(1)}, s16[192,384]{1,0:T(8,128)(2,1)S(1)}, u32[]{:S(2)}, u32[]{:S(2)}) collective-permute-start(s16[192,384]{1,0:T(8,128)(2,1)S(1)} %get-tuple-element.59), channel_id=1, source_target_pairs={{0,2},{1,3},{2,0},{3,1},{16,18},{17,19},{18,16},{19,17},{4,6},{5,7... | collective-permute-start | bytes 442376 | tf_op jit(solution)/shard_map/ppermute | solution.py:525
  27.0 6.3 %collective-permute-start.7 = (s16[192,384]{1,0:T(8,128)(2,1)S(1)}, s16[192,384]{1,0:T(8,128)(2,1)S(1)}, u32[]{:S(2)}, u32[]{:S(2)}) collective-permute-start(s16[192,384]{1,0:T(8,128)(2,1)S(1)} %get-tuple-element.60), channel_id=1, source_target_pairs={{0,16},{1,17},{2,18},{3,19},{16,0},{17,1},{18,2},{19,3},{4,20},{5,... | collective-permute-start | bytes 442376 | tf_op jit(solution)/shard_map/ppermute | solution.py:525
  27.3 9.8 %collective-permute-start.8 = (s16[192,384]{1,0:T(8,128)(2,1)S(1)}, s16[192,384]{1,0:T(8,128)(2,1)S(1)}, u32[]{:S(2)}, u32[]{:S(2)}) collective-permute-start(s16[192,384]{1,0:T(8,128)(2,1)S(1)} %get-tuple-element.61), channel_id=1, source_target_pairs={{0,18},{1,19},{2,16},{3,17},{16,2},{17,3},{18,0},{19,1},{4,22},{5,... | collective-permute-start | bytes 442376 | tf_op jit(solution)/shard_map/ppermute | solution.py:525
  31.4 6.8 %collective-permute-start.13 = (s16[192,384]{1,0:T(8,128)(2,1)S(1)}, s16[192,384]{1,0:T(8,128)(2,1)S(1)}, u32[]{:S(2)}, u32[]{:S(2)}) collective-permute-start(s16[192,384]{1,0:T(8,128)(2,1)S(1)} %plane_sum.5), channel_id=1, source_target_pairs={{0,8},{4,12},{8,0},{12,4},{1,9},{5,13},{9,1},{13,5},{2,10},{6,14},... | collective-permute-start | bytes 442376 | tf_op jit(solution)/shard_map/ppermute | solution.py:562
  33.3 5.2 %copy-start.4 = (f32[8,64,128]{2,1,0:T(8,128)S(1)}, f32[8,64,128]{2,1,0:T(8,128)}, u32[]{:S(2)}) copy-start(f32[8,64,128]{2,1,0:T(8,128)} %refs_1_.1) | copy-start | bytes 786436
  33.3 6.5 %copy-start.2 = (f32[8,192,192]{2,1,0:T(8,128)S(1)}, f32[8,192,192]{2,1,0:T(8,128)}, u32[]{:S(2)}) copy-start(f32[8,192,192]{2,1,0:T(8,128)} %refs_2_.5) | copy-start | bytes 3538948
  33.6 7.0 %collective-permute-start.14 = (s16[192,384]{1,0:T(8,128)(2,1)S(1)}, s16[192,384]{1,0:T(8,128)(2,1)S(1)}, u32[]{:S(2)}, u32[]{:S(2)}) collective-permute-start(s16[192,384]{1,0:T(8,128)(2,1)S(1)} %get-tuple-element.72), channel_id=1, source_target_pairs={{0,2},{1,3},{2,0},{3,1},{16,18},{17,19},{18,16},{19,17},{4,6},{5,7... | collective-permute-start | bytes 442376 | tf_op jit(solution)/shard_map/ppermute | solution.py:525
  35.0 7.7 %collective-permute-start.15 = (s16[192,384]{1,0:T(8,128)(2,1)S(1)}, s16[192,384]{1,0:T(8,128)(2,1)S(1)}, u32[]{:S(2)}, u32[]{:S(2)}) collective-permute-start(s16[192,384]{1,0:T(8,128)(2,1)S(1)} %get-tuple-element.73), channel_id=1, source_target_pairs={{0,16},{1,17},{2,18},{3,19},{16,0},{17,1},{18,2},{19,3},{4,20},{5,... | collective-permute-start | bytes 442376 | tf_op jit(solution)/shard_map/ppermute | solution.py:525
  35.8 6.8 %collective-permute-start.16 = (s16[192,384]{1,0:T(8,128)(2,1)S(1)}, s16[192,384]{1,0:T(8,128)(2,1)S(1)}, u32[]{:S(2)}, u32[]{:S(2)}) collective-permute-start(s16[192,384]{1,0:T(8,128)(2,1)S(1)} %get-tuple-element.74), channel_id=1, source_target_pairs={{0,18},{1,19},{2,16},{3,17},{16,2},{17,3},{18,0},{19,1},{4,22},{5,... | collective-permute-start | bytes 442376 | tf_op jit(solution)/shard_map/ppermute | solution.py:525
  38.4 5.2 %collective-permute-start.17 = (s16[192,384]{1,0:T(8,128)(2,1)S(1)}, s16[192,384]{1,0:T(8,128)(2,1)S(1)}, u32[]{:S(2)}, u32[]{:S(2)}) collective-permute-start(s16[192,384]{1,0:T(8,128)(2,1)S(1)} %get-tuple-element.75), channel_id=1, source_target_pairs={{0,4},{4,0},{8,12},{12,8},{1,5},{5,1},{9,13},{13,9},{2,6},{6,2},{1... | collective-permute-start | bytes 442376 | tf_op jit(solution)/shard_map/ppermute | solution.py:562
  39.8 3.8 %copy-start.3 = (f32[8,64,128]{2,1,0:T(8,128)S(1)}, f32[8,64,128]{2,1,0:T(8,128)}, u32[]{:S(2)}) copy-start(f32[8,64,128]{2,1,0:T(8,128)} %scale_keys.1.refs_6_) | copy-start | bytes 786436
  45.2 5.2 %collective-permute-start.18 = (s16[224,128]{1,0:T(8,128)(2,1)S(1)}, s16[224,128]{1,0:T(8,128)(2,1)S(1)}, u32[]{:S(2)}, u32[]{:S(2)}) collective-permute-start(s16[224,128]{1,0:T(8,128)(2,1)S(1)} %get-tuple-element.78), channel_id=1, source_target_pairs={{0,18},{1,19},{2,16},{3,17},{16,2},{17,3},{18,0},{19,1},{4,22},{5,... | collective-permute-start | bytes 172040 | tf_op jit(solution)/shard_map/ppermute | solution.py:525
  46.7 4.3 %collective-permute-start.19 = (s16[224,128]{1,0:T(8,128)(2,1)S(1)}, s16[224,128]{1,0:T(8,128)(2,1)S(1)}, u32[]{:S(2)}, u32[]{:S(2)}) collective-permute-start(s16[224,128]{1,0:T(8,128)(2,1)S(1)} %get-tuple-element.79), channel_id=1, source_target_pairs={{0,16},{1,17},{2,18},{3,19},{16,0},{17,1},{18,2},{19,3},{4,20},{5,... | collective-permute-start | bytes 172040 | tf_op jit(solution)/shard_map/ppermute | solution.py:525
  48.3 4.2 %collective-permute-start.20 = (s16[224,128]{1,0:T(8,128)(2,1)S(1)}, s16[224,128]{1,0:T(8,128)(2,1)S(1)}, u32[]{:S(2)}, u32[]{:S(2)}) collective-permute-start(s16[224,128]{1,0:T(8,128)(2,1)S(1)} %get-tuple-element.80), channel_id=1, source_target_pairs={{0,2},{1,3},{2,0},{3,1},{16,18},{17,19},{18,16},{19,17},{4,6},{5,7... | collective-permute-start | bytes 172040 | tf_op jit(solution)/shard_map/ppermute | solution.py:525
  54.4 8.7 %collective-permute-start.21 = (f32[4,192,192]{2,1,0:T(8,128)S(1)}, f32[4,192,192]{2,1,0:T(8,128)S(1)}, u32[]{:S(2)}, u32[]{:S(2)}) collective-permute-start(f32[4,192,192]{2,1,0:T(8,128)S(1)} %get-tuple-element.81), channel_id=1, source_target_pairs={{0,1},{1,0},{2,3},{3,2},{16,17},{17,16},{18,19},{19,18},{4,5},{5,4... | collective-permute-start | bytes 1769480 | tf_op jit(solution)/shard_map/ppermute | solution.py:525
  54.4 5.4 %collective-permute-start.27 = (bf16[240,128]{1,0:T(8,128)(2,1)S(1)}, bf16[240,128]{1,0:T(8,128)(2,1)S(1)}, u32[]{:S(2)}, u32[]{:S(2)}) collective-permute-start(bf16[240,128]{1,0:T(8,128)(2,1)S(1)} %newton_schulz.1.refs_1_.refs_3_), channel_id=1, source_target_pairs={{0,18},{1,19},{2,16},{3,17},{16,2},{17,3},{18,0},{19,1},{4,22},{5,... | collective-permute-start | bytes 184328 | tf_op jit(solution)/shard_map/ppermute | solution.py:525
  55.8 5.3 %collective-permute-start.25 = (bf16[240,128]{1,0:T(8,128)(2,1)S(1)}, bf16[240,128]{1,0:T(8,128)(2,1)S(1)}, u32[]{:S(2)}, u32[]{:S(2)}) collective-permute-start(bf16[240,128]{1,0:T(8,128)(2,1)S(1)} %newton_schulz.1.refs_1_.refs_3_), channel_id=1, source_target_pairs={{0,16},{1,17},{2,18},{3,19},{16,0},{17,1},{18,2},{19,3},{4,20},{5,... | collective-permute-start | bytes 184328 | tf_op jit(solution)/shard_map/ppermute | solution.py:525
  56.4 4.7 %collective-permute-start.23 = (bf16[240,128]{1,0:T(8,128)(2,1)S(1)}, bf16[240,128]{1,0:T(8,128)(2,1)S(1)}, u32[]{:S(2)}, u32[]{:S(2)}) collective-permute-start(bf16[240,128]{1,0:T(8,128)(2,1)S(1)} %newton_schulz.1.refs_1_.refs_3_), channel_id=1, source_target_pairs={{0,2},{1,3},{2,0},{3,1},{16,18},{17,19},{18,16},{19,17},{4,6},{5,7... | collective-permute-start | bytes 184328 | tf_op jit(solution)/shard_map/ppermute | solution.py:525
  58.0 5.1 %collective-permute-start.22 = (bf16[240,128]{1,0:T(8,128)(2,1)S(1)}, bf16[240,128]{1,0:T(8,128)(2,1)S(1)}, u32[]{:S(2)}, u32[]{:S(2)}) collective-permute-start(bf16[240,128]{1,0:T(8,128)(2,1)S(1)} %newton_schulz.1.refs_1_.refs_3_), channel_id=1, source_target_pairs={{0,1},{1,0},{2,3},{3,2},{16,17},{17,16},{18,19},{19,18},{4,5},{5,4... | collective-permute-start | bytes 184328 | tf_op jit(solution)/shard_map/ppermute | solution.py:525
  59.9 3.2 %collective-permute-start.28 = (bf16[240,128]{1,0:T(8,128)(2,1)S(1)}, bf16[240,128]{1,0:T(8,128)(2,1)S(1)}, u32[]{:S(2)}, u32[]{:S(2)}) collective-permute-start(bf16[240,128]{1,0:T(8,128)(2,1)S(1)} %collective-permute-done.27.refs_6_), channel_id=1, source_target_pairs={{0,1},{1,0},{2,3},{3,2},{16,17},{17,16},{18,19},{19,18},{4,5},{5,4... | collective-permute-start | bytes 184328 | tf_op jit(solution)/shard_map/ppermute | solution.py:525
  61.1 2.0 %collective-permute-start.26 = (bf16[240,128]{1,0:T(8,128)(2,1)S(1)}, bf16[240,128]{1,0:T(8,128)(2,1)S(1)}, u32[]{:S(2)}, u32[]{:S(2)}) collective-permute-start(bf16[240,128]{1,0:T(8,128)(2,1)S(1)} %collective-permute-done.25.refs_5_), channel_id=1, source_target_pairs={{0,1},{1,0},{2,3},{3,2},{16,17},{17,16},{18,19},{19,18},{4,5},{5,4... | collective-permute-start | bytes 184328 | tf_op jit(solution)/shard_map/ppermute | solution.py:525
  61.1 2.0 %collective-permute-start.24 = (bf16[240,128]{1,0:T(8,128)(2,1)S(1)}, bf16[240,128]{1,0:T(8,128)(2,1)S(1)}, u32[]{:S(2)}, u32[]{:S(2)}) collective-permute-start(bf16[240,128]{1,0:T(8,128)(2,1)S(1)} %collective-permute-done.23.refs_4_), channel_id=1, source_target_pairs={{0,1},{1,0},{2,3},{3,2},{16,17},{17,16},{18,19},{19,18},{4,5},{5,4... | collective-permute-start | bytes 184328 | tf_op jit(solution)/shard_map/ppermute | solution.py:525

commit v5 on v4

--- a/solution.py
+++ b/solution.py
@@ -25,6 +25,7 @@
 LOWEST = 100.0 * STEPS
 NOTE_UNITS = (64.0, 64.0 * 32768.0, 64.0 * 32768.0 * 32768.0)
 GROUPS = 4
+TOGETHER = 2
 LEFT = 128
 
 SMEM = pl.BlockSpec(memory_space=pltpu.SMEM)
@@ -298,39 +299,88 @@
         out[LEFT + f * rest // 2 : LEFT + (f + 1) * rest // 2, LEFT:] = part
 
 
-def gram_kernel(chips, heads_own, assignment, old, near, *refs):
-    sources = old.shape[0]
-    arrived, refs = refs[: sources - 1], refs[sources - 1 :]
-    (new, here), away, packed = refs[:2], refs[2:-1], refs[-1]
-    owner, chip, core = whereabouts()
-    for k in range(sources):
-        source = owner ^ k
+def refreshed(heads_own, assignment, old, grad, k):
+    owner, _, core = whereabouts()
+    source = owner ^ k
+    _, held = head_of(assignment, source, owner, 0, heads_own)
+    kept = old[source]
+    return source, jnp.where(held > core, MOMENTUM_RATE * kept + grad, kept)
+
+
+def gram_of(value, packed, coded):
+    value = value.astype(jnp.bfloat16)
+    gram = lax.dot_general(
+        value, value, (((1,), (1,)), ((), ())), preferred_element_type=jnp.float32
+    )
+    pack(gram, packed)
+    encode([packed[...]], coded)
+
+
+def early_kernel(heads_own, ks, assignment, old, *refs):
+    arrived, (new, packed, coded) = refs[: len(ks)], refs[len(ks) :]
+    for i, k in enumerate(ks):
+        _, new[i] = refreshed(heads_own, assignment, old, decode(arrived[i], 1)[0], k)
+        gram_of(new[i], packed.at[i], coded.at[i])
+
+
+def early_grams(assignment, old, arrived, ks, heads_own):
+    _, cols, width = old.shape
+    rows = cols + (cols - LEFT) // 2
+    return call(
+        functools.partial(early_kernel, heads_own, ks),
+        "early_gram",
+        [(SMEM, assignment)] + [(VMEM, value) for value in (old, *arrived)],
+        [
+            (VMEM, (len(ks), cols, width), jnp.float32),
+            (VMEM, (len(ks), rows, LEFT), jnp.float32),
+            (VMEM, (len(ks), rows, LEFT), jnp.int16),
+        ],
+    )
+
+
+def gram_kernel(chips, heads_own, assignment, old, near, early_new, early_packed, early_coded, *refs):
+    sources, count = old.shape[0], early_new.shape[0]
+    late = sources - count
+    arrived, refs = refs[: late - 1], refs[late - 1 :]
+    (new, here), away, (packed, coded) = refs[:2], refs[2:-2], refs[-2:]
+    owner, chip, _ = whereabouts()
+    for k in range(late):
         grad = near[...] if k == 0 else decode(arrived[k - 1], 1)[0]
-        kept = old[source]
-        _, held = head_of(assignment, source, owner, 0, heads_own)
-        new[source] = jnp.where(held > core, MOMENTUM_RATE * kept + grad, kept)
-    for k in range(chips):
-        value = new[lax.rem(chip ^ k, sources)].astype(jnp.bfloat16)
-        gram = lax.dot_general(
-            value, value, (((1,), (1,)), ((), ())), preferred_element_type=jnp.float32
-        )
-        if k == 0:
-            pack(gram, here)
-        else:
-            pack(gram, packed)
-            encode([packed[...]], away[k - 1])
-
-
-def grams(assignment, old, near, arrived, chips, heads_own, after):
-    cols = old.shape[1]
+        source, value = refreshed(heads_own, assignment, old, grad, k)
+        new[source] = value
+        gram_of(value, packed.at[k], coded.at[k])
+    for i in range(count):
+        new[owner ^ (sources - 1 - i)] = early_new[i]
+    for c in range(chips):
+        k = lax.rem(chip ^ c, sources) ^ owner
+
+        def from_early(c=c, k=k):
+            if c == 0:
+                here[...] = early_packed[sources - 1 - k]
+            else:
+                away[c - 1][...] = early_coded[sources - 1 - k]
+
+        def from_late(c=c, k=k):
+            if c == 0:
+                here[...] = packed[k]
+            else:
+                away[c - 1][...] = coded[k]
+
+        pl.when(k >= late)(from_early)
+        pl.when(k < late)(from_late)
+
+
+def grams(assignment, old, near, early, arrived, chips, heads_own, after):
+    sources, cols, _ = old.shape
     rows = cols + (cols - LEFT) // 2
+    late = sources - early[0].shape[0]
     coded = (VMEM, (rows, LEFT), jnp.int16)
     return call(
         functools.partial(gram_kernel, chips, heads_own),
         "refresh_and_gram",
-        [(SMEM, assignment)] + [(VMEM, value) for value in (old, near, *arrived)],
+        [(SMEM, assignment)] + [(VMEM, value) for value in (old, near, *early, *arrived)],
         [(VMEM, old.shape, jnp.float32), (VMEM, (rows, LEFT), jnp.float32)] + [coded] * (chips - 1),
-        [pltpu.VMEM((rows, LEFT), jnp.float32)],
+        [pltpu.VMEM((late, rows, LEFT), jnp.float32), pltpu.VMEM((late, rows, LEFT), jnp.int16)],
         after,
     )
 
@@ -460,7 +510,6 @@
         start = (momentum[source] * (1.0 / norm)).astype(jnp.bfloat16)
         step = (QUINTIC_A * QUINTIC_A) * start.astype(jnp.float32) + small_dot(start, matrix[k])
         result[k] = base[slot] - step * (step_size * scales[pl.ds(slot, 1)])
-        written(k).start()
 
     def only(k, act):
         if sources == chips:
@@ -468,8 +517,11 @@
         else:
             pl.when((chip ^ k) < sources)(act)
 
-    for k in range(chips):
-        only(k, functools.partial(update, k))
+    for first in range(0, chips, TOGETHER):
+        for k in range(first, first + TOGETHER):
+            only(k, functools.partial(update, k))
+        for k in range(first, first + TOGETHER):
+            only(k, lambda k=k: written(k).start())
     for k in range(chips):
         only(k, lambda k=k: written(k).wait())
     for s in range(sources):
@@ -536,6 +588,7 @@
     siblings = [swap(first, 1)]
 
     near, arrived, before, sent = None, {}, [], []
+    first_ks = order[: sources // 2]
     for i, ks in enumerate(groups):
         heads = [(j, j + (size * (i - 1) if i else 0)) for j in range(len(ks))]
         passed = [others] if i == 0 else []
@@ -562,10 +615,11 @@
                 arrived[k] = lax.ppermute(total, "owner", [(j, j ^ k) for j in range(sources)])
                 sent.append(arrived[k])
         if note:
-            sent += [base, k_weight_out]
-
-    arrived = [arrived[k] for k in range(1, sources)]
-    new, here, *away = grams(assignment, turned, near, arrived, chips, heads_own, [])
+            early = early_grams(assignment, turned, [arrived[k] for k in first_ks], first_ks, heads_own)
+            sent += [base, k_weight_out, early[2]]
+
+    arrived = [arrived[k] for k in range(1, sources // 2)]
+    new, here, *away = grams(assignment, turned, near, early, arrived, chips, heads_own, [])
     away = [swap(value, CORES * (k + 1)) for k, value in enumerate(away)]
     result = newton(here, away[::-1], momentum.shape[2], [])
     own_new, sibling_new = turn_back(new, [result])

time: 64.8 us -> 64.4 us (level)
  waiting for transfers between devices: 16.5 us -> 15.4 us
    ppermute x26, waiting for transfers between devices: 14.4 us -> 13.4 us  [swap(): return lax.ppermute(value, PLANE, [(i, i ^ bits) for i in range(devices)])]
    pallas_call x19 -> x20, Pallas kernels: 16.7 us -> 17.3 us  [call(): pl.pallas_call(whole, in_specs=[spec for spec, _ in ins] + [ANY] * len(af...]
  transfers between devices with their start and end apart: 29 -> 29, of which waited for: 14 -> 14; matrix products, arithmetic and copies ran while one was open for 0% -> 0% of each run, Pallas kernels for 14% -> 16%
where the time goes in v5:
time: 64.4 us; the launch traced here: 64.2 us
  starting transfers between devices  29.3 us (45%)
  Pallas kernels  17.3 us (27%)
  waiting for transfers between devices  15.4 us (24%)
  local copies, waits for them, and re-layouts  1.33 us (2%)
  between operations  0.9 us (1%)
    ppermute x26, starting transfers between devices, swap(): return lax.ppermute(value, PLANE, [(i, i ^ bits) for i in range(devices)])  25.5 us
    pallas_call x20, Pallas kernels, call(): pl.pallas_call(whole, in_specs=[spec for spec, _ in ins] + [ANY] * len(af...  17.3 us
    ppermute x26, waiting for transfers between devices, swap(): return lax.ppermute(value, PLANE, [(i, i ^ bits) for i in range(devices)])  13.4 us
    ppermute x3, starting transfers between devices, body(): lax.ppermute(total, 'owner', [(j, j ^ k) for j in range(sources)])  3.81 us
    ppermute x3, waiting for transfers between devices, body(): lax.ppermute(total, 'owner', [(j, j ^ k) for j in range(sources)])  2.04 us
    unnamed x18, local copies, waits for them, and re-layouts  1.33 us
  transfers between devices with their start and end apart: 29, of which 14 were waited for; matrix products, arithmetic and copies ran while one was open for 0% of the time, Pallas kernels for 16%

profile of v5, /device:TPU:0, one launch (start us, length us, event | category | flops | bytes accessed | tf_op | source)
XLA Modules:
  0.0 64.2 jit_solution(6740967230762201657)
XLA Ops:
  0.6 0.0 copy-start.5
  0.6 0.6 %copy-done.5 = s32[32,1]{0,1:T(1,128)S(1)} copy-done((s32[32,1]{0,1:T(1,128)S(1)}, s32[32,1]{0,1:T(1,128)}, u32[]{:S(2)}) %copy-start.5) | copy-done | bytes 152
  1.3 0.7 %copy-done.7 = f32[1,32]{1,0:T(1,128)S(1)} copy-done((f32[1,32]{1,0:T(1,128)S(1)}, f32[1,32]{1,0:T(1,128)}, u32[]{:S(2)}) %copy-start.7) | copy-done | bytes 152
  1.9 2.3 %fetch_heads.3 = (f32[4,192,256]{2,1,0:T(8,128)S(1)}, bf16[1,192,1536]{2,1,0:T(8,128)(2,1)S(1)}, f32[8,128]{1,0:T(8,128)S(1)}) custom-call(s32[1,32]{1,0:T(1,128)S(1)} %bitcast.7, bf16[8,192,1536]{2,1,0:T(8,128)(2,1)} %bitcast.4, f32[8,192,192]{2,1,0:T(8,128)} %refs_0_.1, f32[1,32]{1,0:T(1,128)S(1)} %copy-done.7), custom_call_target="tpu_custom_call" | custom-call | tf_op jit(solution)/shard_map/fetch_heads/pallas_call | solution.py:51
  4.3 0.5 collective-permute-start
  4.8 1.7 %fetch_heads.4 = (bf16[3,192,1536]{2,1,0:T(8,128)(2,1)S(1)}, bf16[1,192,1536]{2,1,0:T(8,128)(2,1)S(1)}, f32[8,128]{1,0:T(8,128)}) custom-call(s32[1,32]{1,0:T(1,128)S(1)} %bitcast.8, bf16[8,192,1536]{2,1,0:T(8,128)(2,1)S(1)} %bitcast.5, f32[8,128]{1,0:T(8,128)S(1)} %get-tuple-element.48.refs_2_), custom_call_target="tpu_custom_call" | custom-call | tf_op jit(solution)/shard_map/fetch_heads/pallas_call | solution.py:51
  6.5 0.0 copy-start.6
  6.6 0.3 pair_sum.4
  6.9 0.4 collective-permute-start.1
  7.3 0.2 collective-permute-start.2
  7.4 2.9 %collective-permute-start.3 = (s16[192,384]{1,0:T(8,128)(2,1)S(1)}, s16[192,384]{1,0:T(8,128)(2,1)S(1)}, u32[]{:S(2)}, u32[]{:S(2)}) collective-permute-start(s16[192,384]{1,0:T(8,128)(2,1)S(1)} %get-tuple-element.52.refs_2_), channel_id=1, source_target_pairs={{0,2},{1,3},{2,0},{3,1},{16,18},{17,19},{18,16},{19,17},{4,6},{5,7... | collective-permute-start | bytes 442376 | tf_op jit(solution)/shard_map/ppermute | solution.py:577
  10.3 1.5 %collective-permute-start.10 = (s16[192,384]{1,0:T(8,128)(2,1)S(1)}, s16[192,384]{1,0:T(8,128)(2,1)S(1)}, u32[]{:S(2)}, u32[]{:S(2)}) collective-permute-start(s16[192,384]{1,0:T(8,128)(2,1)S(1)} %get-tuple-element.68), channel_id=1, source_target_pairs={{0,16},{1,17},{2,18},{3,19},{16,0},{17,1},{18,2},{19,3},{4,20},{5,... | collective-permute-start | bytes 442376 | tf_op jit(solution)/shard_map/ppermute | solution.py:577
  11.8 1.6 %fetch_heads.5 = (bf16[1,192,1536]{2,1,0:T(8,128)(2,1)S(1)}, bf16[1,192,1536]{2,1,0:T(8,128)(2,1)S(1)}, bf16[1,192,1536]{2,1,0:T(8,128)(2,1)S(1)}, f32[8,128]{1,0:T(8,128)}) custom-call(s32[1,32]{1,0:T(1,128)S(1)} %bitcast.9, bf16[8,192,1536]{2,1,0:T(8,128)(2,1)S(1)} %bitcast.6, s16[192,384]{1,0:T(8,128)(2,1)S(1)} %get-tuple-element.52.refs_2_), custom_call_target="tpu_custom_call" | custom-call | tf_op jit(solution)/shard_map/fetch_heads/pallas_call | solution.py:51
  13.5 0.7 %turn_momentum.1 = (f32[4,192,384]{2,1,0:T(8,128)S(1)}, f32[1,32]{1,0:T(1,128)S(1)}) custom-call(f32[8,192,192]{2,1,0:T(8,128)S(1)} %copy-done.1, f32[4,192,256]{2,1,0:T(8,128)S(1)} %collective-permute-done.2.refs_1_, f32[1,32]{1,0:T(1,128)S(1)} %copy-done.8), custom_call_target="tpu_custom_call" | custom-call | tf_op jit(solution)/shard_map/turn_momentum/pallas_call | solution.py:51
  14.2 0.7 %collective-permute-done.3.refs_2_.refs_1_ = s16[192,384]{1,0:T(8,128)(2,1)S(1)} collective-permute-done((s16[192,384]{1,0:T(8,128)(2,1)S(1)}, s16[192,384]{1,0:T(8,128)(2,1)S(1)}, u32[]{:S(2)}, u32[]{:S(2)}) %collective-permute-start.3) | collective-permute-done | bytes 147488 | tf_op jit(solution)/shard_map/ppermute | solution.py:577
  14.9 0.3 pair_sum.5
  15.2 2.1 %collective-permute-start.4 = (s16[192,384]{1,0:T(8,128)(2,1)S(1)}, s16[192,384]{1,0:T(8,128)(2,1)S(1)}, u32[]{:S(2)}, u32[]{:S(2)}) collective-permute-start(s16[192,384]{1,0:T(8,128)(2,1)S(1)} %get-tuple-element.59), channel_id=1, source_target_pairs={{0,2},{1,3},{2,0},{3,1},{16,18},{17,19},{18,16},{19,17},{4,6},{5,7... | collective-permute-start | bytes 442376 | tf_op jit(solution)/shard_map/ppermute | solution.py:577
  17.3 1.5 %collective-permute-start.5 = (s16[192,384]{1,0:T(8,128)(2,1)S(1)}, s16[192,384]{1,0:T(8,128)(2,1)S(1)}, u32[]{:S(2)}, u32[]{:S(2)}) collective-permute-start(s16[192,384]{1,0:T(8,128)(2,1)S(1)} %get-tuple-element.60), channel_id=1, source_target_pairs={{0,16},{1,17},{2,18},{3,19},{16,0},{17,1},{18,2},{19,3},{4,20},{5,... | collective-permute-start | bytes 442376 | tf_op jit(solution)/shard_map/ppermute | solution.py:577
  18.9 0.1 collective-permute-done.10.refs_2_
  18.9 0.6 collective-permute-done.11.refs_3_
  19.5 0.2 plane_sum.4
  19.8 3.7 %collective-permute-start.12 = (s16[192,384]{1,0:T(8,128)(2,1)S(1)}, s16[192,384]{1,0:T(8,128)(2,1)S(1)}, u32[]{:S(2)}, u32[]{:S(2)}) collective-permute-start(s16[192,384]{1,0:T(8,128)(2,1)S(1)} %plane_sum.4), channel_id=1, source_target_pairs={{0,12},{4,8},{8,4},{12,0},{1,13},{5,9},{9,5},{13,1},{2,14},{6,10},... | collective-permute-start | bytes 442376 | tf_op jit(solution)/shard_map/ppermute | solution.py:615
  23.4 1.5 %collective-permute-start.9 = (s16[192,384]{1,0:T(8,128)(2,1)S(1)}, s16[192,384]{1,0:T(8,128)(2,1)S(1)}, u32[]{:S(2)}, u32[]{:S(2)}) collective-permute-start(s16[192,384]{1,0:T(8,128)(2,1)S(1)} %get-tuple-element.66), channel_id=1, source_target_pairs={{0,18},{1,19},{2,16},{3,17},{16,2},{17,3},{18,0},{19,1},{4,22},{5,... | collective-permute-start | bytes 442376 | tf_op jit(solution)/shard_map/ppermute | solution.py:577
  25.0 0.3 pair_sum.6
  25.3 1.7 %collective-permute-start.6 = (s16[192,384]{1,0:T(8,128)(2,1)S(1)}, s16[192,384]{1,0:T(8,128)(2,1)S(1)}, u32[]{:S(2)}, u32[]{:S(2)}) collective-permute-start(s16[192,384]{1,0:T(8,128)(2,1)S(1)} %get-tuple-element.62), channel_id=1, source_target_pairs={{0,2},{1,3},{2,0},{3,1},{16,18},{17,19},{18,16},{19,17},{4,6},{5,7... | collective-permute-start | bytes 442376 | tf_op jit(solution)/shard_map/ppermute | solution.py:577
  27.0 0.3 collective-permute-start.7
  27.3 1.5 %collective-permute-start.8 = (s16[192,384]{1,0:T(8,128)(2,1)S(1)}, s16[192,384]{1,0:T(8,128)(2,1)S(1)}, u32[]{:S(2)}, u32[]{:S(2)}) collective-permute-start(s16[192,384]{1,0:T(8,128)(2,1)S(1)} %get-tuple-element.64), channel_id=1, source_target_pairs={{0,18},{1,19},{2,16},{3,17},{16,2},{17,3},{18,0},{19,1},{4,22},{5,... | collective-permute-start | bytes 442376 | tf_op jit(solution)/shard_map/ppermute | solution.py:577
  28.9 2.3 %collective-permute-done.9.refs_3_ = s16[192,384]{1,0:T(8,128)(2,1)S(1)} collective-permute-done((s16[192,384]{1,0:T(8,128)(2,1)S(1)}, s16[192,384]{1,0:T(8,128)(2,1)S(1)}, u32[]{:S(2)}, u32[]{:S(2)}) %collective-permute-start.9) | collective-permute-done | bytes 147488 | tf_op jit(solution)/shard_map/ppermute | solution.py:577
  31.2 0.2 plane_sum.5
  31.4 0.1 collective-permute-start.13
  31.5 1.5 %collective-permute-done.6.refs_1_.refs_2_ = s16[192,384]{1,0:T(8,128)(2,1)S(1)} collective-permute-done((s16[192,384]{1,0:T(8,128)(2,1)S(1)}, s16[192,384]{1,0:T(8,128)(2,1)S(1)}, u32[]{:S(2)}, u32[]{:S(2)}) %collective-permute-start.6) | collective-permute-done | bytes 147488 | tf_op jit(solution)/shard_map/ppermute | solution.py:577
  32.9 0.3 collective-permute-done.7.refs_2_.refs_3_
  33.3 0.3 pair_sum.7
  33.6 1.4 %collective-permute-start.14 = (s16[192,384]{1,0:T(8,128)(2,1)S(1)}, s16[192,384]{1,0:T(8,128)(2,1)S(1)}, u32[]{:S(2)}, u32[]{:S(2)}) collective-permute-start(s16[192,384]{1,0:T(8,128)(2,1)S(1)} %get-tuple-element.75), channel_id=1, source_target_pairs={{0,2},{1,3},{2,0},{3,1},{16,18},{17,19},{18,16},{19,17},{4,6},{5,7... | collective-permute-start | bytes 442376 | tf_op jit(solution)/shard_map/ppermute | solution.py:577
  35.0 0.8 %collective-permute-start.15 = (s16[192,384]{1,0:T(8,128)(2,1)S(1)}, s16[192,384]{1,0:T(8,128)(2,1)S(1)}, u32[]{:S(2)}, u32[]{:S(2)}) collective-permute-start(s16[192,384]{1,0:T(8,128)(2,1)S(1)} %get-tuple-element.76), channel_id=1, source_target_pairs={{0,16},{1,17},{2,18},{3,19},{16,0},{17,1},{18,2},{19,3},{4,20},{5,... | collective-permute-start | bytes 442376 | tf_op jit(solution)/shard_map/ppermute | solution.py:577
  35.8 1.3 %collective-permute-start.16 = (s16[192,384]{1,0:T(8,128)(2,1)S(1)}, s16[192,384]{1,0:T(8,128)(2,1)S(1)}, u32[]{:S(2)}, u32[]{:S(2)}) collective-permute-start(s16[192,384]{1,0:T(8,128)(2,1)S(1)} %get-tuple-element.77), channel_id=1, source_target_pairs={{0,18},{1,19},{2,16},{3,17},{16,2},{17,3},{18,0},{19,1},{4,22},{5,... | collective-permute-start | bytes 442376 | tf_op jit(solution)/shard_map/ppermute | solution.py:577
  37.1 1.1 %collective-permute-done.13.refs_5_.refs_3_ = s16[192,384]{1,0:T(8,128)(2,1)S(1)} collective-permute-done((s16[192,384]{1,0:T(8,128)(2,1)S(1)}, s16[192,384]{1,0:T(8,128)(2,1)S(1)}, u32[]{:S(2)}, u32[]{:S(2)}) %collective-permute-start.13) | collective-permute-done | bytes 147488 | tf_op jit(solution)/shard_map/ppermute | solution.py:615
  38.2 0.2 plane_sum.6
  38.4 0.1 collective-permute-start.17
  38.5 1.3 %scale_keys.1.refs_6_ = f32[8,64,128]{2,1,0:T(8,128)} custom-call(f32[1,32]{1,0:T(1,128)S(1)} %get-tuple-element.70.refs_1_.refs_0_, f32[8,64,128]{2,1,0:T(8,128)S(1)} %copy-done.4), custom_call_target="tpu_custom_call" | custom-call | tf_op jit(solution)/shard_map/scale_keys/pallas_call | solution.py:51
  39.8 0.8 %scale_weight.1 = (f32[8,192,192]{2,1,0:T(8,128)S(1)}, f32[8,192]{1,0:T(8,128)S(1)}) custom-call(s32[1,32]{1,0:T(1,128)S(1)} %bitcast.10, f32[1,32]{1,0:T(1,128)S(1)} %get-tuple-element.70.refs_1_.refs_0_, f32[8,192,192]{2,1,0:T(8,128)S(1)} %copy-done.2), custom_call_target="tpu_custom_call" | custom-call | tf_op jit(solution)/shard_map/scale_weight/pallas_call | solution.py:51
  40.6 1.0 %early_gram.1 = (f32[2,192,384]{2,1,0:T(8,128)S(1)}, f32[2,224,128]{2,1,0:T(8,128)S(1)}, s16[2,224,128]{2,1,0:T(8,128)(2,1)S(1)}) custom-call(s32[1,32]{1,0:T(1,128)S(1)} %bitcast.11, f32[4,192,384]{2,1,0:T(8,128)S(1)} %get-tuple-element.58.refs_3_.refs_1_, s16[192,384]{1,0:T(8,128)(2,1)S(1)} %collective-permute-done.12.refs_4_.refs_2_, ...), custom_call_target="tpu_custom_call" | custom-call | tf_op jit(solution)/shard_map/early_gram/pallas_call | solution.py:51
  41.6 1.0 %collective-permute-done.15.refs_2_ = s16[192,384]{1,0:T(8,128)(2,1)S(1)} collective-permute-done((s16[192,384]{1,0:T(8,128)(2,1)S(1)}, s16[192,384]{1,0:T(8,128)(2,1)S(1)}, u32[]{:S(2)}, u32[]{:S(2)}) %collective-permute-start.15) | collective-permute-done | bytes 147488 | tf_op jit(solution)/shard_map/ppermute | solution.py:577
  42.6 1.0 %collective-permute-done.17.refs_4_.refs_6_ = s16[192,384]{1,0:T(8,128)(2,1)S(1)} collective-permute-done((s16[192,384]{1,0:T(8,128)(2,1)S(1)}, s16[192,384]{1,0:T(8,128)(2,1)S(1)}, u32[]{:S(2)}, u32[]{:S(2)}) %collective-permute-start.17) | collective-permute-done | bytes 147488 | tf_op jit(solution)/shard_map/ppermute | solution.py:615
  43.6 0.1 plane_sum.7.refs_2_
  43.8 1.1 %refresh_and_gram.1 = (f32[4,192,384]{2,1,0:T(8,128)S(1)}, f32[224,128]{1,0:T(8,128)S(1)}, s16[224,128]{1,0:T(8,128)(2,1)S(1)}, s16[224,128]{1,0:T(8,128)(2,1)S(1)}, s16[224,128]{1,0:T(8,128)(2,1)S(1)}) custom-call(s32[1,32]{1,0:T(1,128)S(1)} %bitcast.12, f32[4,192,384]{2,1,0:T(8,128)S(1)} %get-tuple-element.58.refs_3_.refs_1_, ...), custom_call_target="tpu_custom_call" | custom-call | tf_op jit(solution)/shard_map/refresh_and_gram/pallas_call | solution.py:51
  44.9 1.5 %collective-permute-start.18 = (s16[224,128]{1,0:T(8,128)(2,1)S(1)}, s16[224,128]{1,0:T(8,128)(2,1)S(1)}, u32[]{:S(2)}, u32[]{:S(2)}) collective-permute-start(s16[224,128]{1,0:T(8,128)(2,1)S(1)} %get-tuple-element.84), channel_id=1, source_target_pairs={{0,18},{1,19},{2,16},{3,17},{16,2},{17,3},{18,0},{19,1},{4,22},{5,... | collective-permute-start | bytes 172040 | tf_op jit(solution)/shard_map/ppermute | solution.py:577
  46.4 1.6 %collective-permute-start.19 = (s16[224,128]{1,0:T(8,128)(2,1)S(1)}, s16[224,128]{1,0:T(8,128)(2,1)S(1)}, u32[]{:S(2)}, u32[]{:S(2)}) collective-permute-start(s16[224,128]{1,0:T(8,128)(2,1)S(1)} %get-tuple-element.85), channel_id=1, source_target_pairs={{0,16},{1,17},{2,18},{3,19},{16,0},{17,1},{18,2},{19,3},{4,20},{5,... | collective-permute-start | bytes 172040 | tf_op jit(solution)/shard_map/ppermute | solution.py:577
  48.0 0.5 collective-permute-start.20
  48.5 1.6 %collective-permute-done.18.refs_1_ = s16[224,128]{1,0:T(8,128)(2,1)S(1)} collective-permute-done((s16[224,128]{1,0:T(8,128)(2,1)S(1)}, s16[224,128]{1,0:T(8,128)(2,1)S(1)}, u32[]{:S(2)}, u32[]{:S(2)}) %collective-permute-start.18) | collective-permute-done | bytes 57376 | tf_op jit(solution)/shard_map/ppermute | solution.py:577
  50.1 0.6 collective-permute-done.19.refs_2_
  50.7 1.5 %collective-permute-done.20.refs_3_ = s16[224,128]{1,0:T(8,128)(2,1)S(1)} collective-permute-done((s16[224,128]{1,0:T(8,128)(2,1)S(1)}, s16[224,128]{1,0:T(8,128)(2,1)S(1)}, u32[]{:S(2)}, u32[]{:S(2)}) %collective-permute-start.20) | collective-permute-done | bytes 57376 | tf_op jit(solution)/shard_map/ppermute | solution.py:577
  52.2 1.2 %newton_schulz.1.refs_1_.refs_3_ = bf16[240,128]{1,0:T(8,128)(2,1)S(1)} custom-call(f32[224,128]{1,0:T(8,128)S(1)} %get-tuple-element.83.refs_0_, s16[224,128]{1,0:T(8,128)(2,1)S(1)} %collective-permute-done.18.refs_1_, s16[224,128]{1,0:T(8,128)(2,1)S(1)} %collective-permute-done.19.refs_2_, s16[224,128]{1,0:T(8,128)(2,1)S(1)} %collective-permute-done.20.refs_3_), custom_call_target="tpu_custom_call" | custom-call | tf_op jit(solution)/shard_map/newton_schulz/pallas_call | solution.py:51
  53.3 0.7 %turn_back.1 = (f32[4,192,192]{2,1,0:T(8,128)S(1)}, f32[4,192,192]{2,1,0:T(8,128)S(1)}) custom-call(f32[4,192,384]{2,1,0:T(8,128)S(1)} %get-tuple-element.82.refs_0_, bf16[240,128]{1,0:T(8,128)(2,1)S(1)} %newton_schulz.1.refs_1_.refs_3_), custom_call_target="tpu_custom_call" | custom-call | tf_op jit(solution)/shard_map/turn_back/pallas_call | solution.py:51
  54.1 0.1 collective-permute-start.21
  54.1 1.3 %collective-permute-start.27 = (bf16[240,128]{1,0:T(8,128)(2,1)S(1)}, bf16[240,128]{1,0:T(8,128)(2,1)S(1)}, u32[]{:S(2)}, u32[]{:S(2)}) collective-permute-start(bf16[240,128]{1,0:T(8,128)(2,1)S(1)} %newton_schulz.1.refs_1_.refs_3_), channel_id=1, source_target_pairs={{0,18},{1,19},{2,16},{3,17},{16,2},{17,3},{18,0},{19,1},{4,22},{5,... | collective-permute-start | bytes 184328 | tf_op jit(solution)/shard_map/ppermute | solution.py:577
  55.4 0.7 %collective-permute-start.25 = (bf16[240,128]{1,0:T(8,128)(2,1)S(1)}, bf16[240,128]{1,0:T(8,128)(2,1)S(1)}, u32[]{:S(2)}, u32[]{:S(2)}) collective-permute-start(bf16[240,128]{1,0:T(8,128)(2,1)S(1)} %newton_schulz.1.refs_1_.refs_3_), channel_id=1, source_target_pairs={{0,16},{1,17},{2,18},{3,19},{16,0},{17,1},{18,2},{19,3},{4,20},{5,... | collective-permute-start | bytes 184328 | tf_op jit(solution)/shard_map/ppermute | solution.py:577
  56.1 1.6 %collective-permute-start.23 = (bf16[240,128]{1,0:T(8,128)(2,1)S(1)}, bf16[240,128]{1,0:T(8,128)(2,1)S(1)}, u32[]{:S(2)}, u32[]{:S(2)}) collective-permute-start(bf16[240,128]{1,0:T(8,128)(2,1)S(1)} %newton_schulz.1.refs_1_.refs_3_), channel_id=1, source_target_pairs={{0,2},{1,3},{2,0},{3,1},{16,18},{17,19},{18,16},{19,17},{4,6},{5,7... | collective-permute-start | bytes 184328 | tf_op jit(solution)/shard_map/ppermute | solution.py:577
  57.7 1.9 %collective-permute-done.27.refs_6_ = bf16[240,128]{1,0:T(8,128)(2,1)S(1)} collective-permute-done((bf16[240,128]{1,0:T(8,128)(2,1)S(1)}, bf16[240,128]{1,0:T(8,128)(2,1)S(1)}, u32[]{:S(2)}, u32[]{:S(2)}) %collective-permute-start.27) | collective-permute-done | bytes 61472 | tf_op jit(solution)/shard_map/ppermute | solution.py:577
  59.6 1.2 %collective-permute-done.25.refs_5_ = bf16[240,128]{1,0:T(8,128)(2,1)S(1)} collective-permute-done((bf16[240,128]{1,0:T(8,128)(2,1)S(1)}, bf16[240,128]{1,0:T(8,128)(2,1)S(1)}, u32[]{:S(2)}, u32[]{:S(2)}) %collective-permute-start.25) | collective-permute-done | bytes 61472 | tf_op jit(solution)/shard_map/ppermute | solution.py:577
  60.8 0.0 collective-permute-start.26
  60.8 0.5 collective-permute-start.24
  61.3 1.4 %update_weight.2 = (f32[8,192,192]{2,1,0:T(8,128)}, f32[8,192,192]{2,1,0:T(8,128)}) custom-call(f32[8,192,192]{2,1,0:T(8,128)S(1)} %get-tuple-element.71.refs_5_.refs_0_, f32[8,192]{1,0:T(8,128)S(1)} %get-tuple-element.72.refs_1_, f32[4,192,192]{2,1,0:T(8,128)S(1)} %get-tuple-element.88.refs_2_, bf16[240,128]{1,0:T(8,128)(2,1)S(1)} %newton_schulz.1.refs_1_.refs_3_, ...), custom_call_target="tpu_custom_call" | custom-call | tf_op jit(solution)/shard_map/update_weight/pallas_call | solution.py:51
  62.8 1.4 %update_weight.3 = (f32[8,192,192]{2,1,0:T(8,128)}, f32[8,192,192]{2,1,0:T(8,128)}) custom-call(f32[8,192,192]{2,1,0:T(8,128)S(1)} %get-tuple-element.71.refs_5_.refs_0_, f32[8,192]{1,0:T(8,128)S(1)} %get-tuple-element.72.refs_1_, f32[4,192,192]{2,1,0:T(8,128)S(1)} %collective-permute-done.21.refs_2_, ...), custom_call_target="tpu_custom_call", output_to_operand_aliasing={{0}: (7, {}), {1}: (8, {})} | custom-call | tf_op jit(solution)/shard_map/update_weight/pallas_call | solution.py:51
  (32 shorter events, 0.1 us)
Async XLA Ops:
  0.6 0.7 %copy-start.5 = (s32[32,1]{0,1:T(1,128)S(1)}, s32[32,1]{0,1:T(1,128)}, u32[]{:S(2)}) copy-start(s32[32,1]{0,1:T(1,128)} %param.7) | copy-start | bytes 388
  1.3 0.7 %copy-start.7 = (f32[1,32]{1,0:T(1,128)S(1)}, f32[1,32]{1,0:T(1,128)}, u32[]{:S(2)}) copy-start(f32[1,32]{1,0:T(1,128)} %refs_2_.4) | copy-start | bytes 388
  1.9 2.8 %copy-start = (bf16[1,1536,8,192]{1,3,2,0:T(8,128)(2,1)S(1)}, bf16[1,1536,8,192]{1,3,2,0:T(8,128)(2,1)}, u32[]{:S(2)}) copy-start(bf16[1,1536,8,192]{1,3,2,0:T(8,128)(2,1)} %param.6) | copy-start | bytes 14155780
  4.3 2.3 %collective-permute-start = (bf16[1,192,1536]{2,1,0:T(8,128)(2,1)S(1)}, bf16[1,192,1536]{2,1,0:T(8,128)(2,1)S(1)}, u32[]{:S(2)}, u32[]{:S(2)}) collective-permute-start(bf16[1,192,1536]{2,1,0:T(8,128)(2,1)S(1)} %get-tuple-element.50), channel_id=1, source_target_pairs={{0,1},{1,0},{2,3},{3,2},{16,17},{17,16},{18,19},{19,18},{4,5},{5,4... | collective-permute-start | bytes 1769480 | tf_op jit(solution)/shard_map/ppermute | solution.py:577
  6.5 5.3 %copy-start.6 = (s32[32,1]{0,1:T(1,128)S(1)}, s32[32,1]{0,1:T(1,128)}, u32[]{:S(2)}) copy-start(s32[32,1]{0,1:T(1,128)} %param.7) | copy-start | bytes 388
  6.9 8.1 %collective-permute-start.1 = (bf16[3,192,1536]{2,1,0:T(8,128)(2,1)S(1)}, bf16[3,192,1536]{2,1,0:T(8,128)(2,1)S(1)}, u32[]{:S(2)}, u32[]{:S(2)}) collective-permute-start(bf16[3,192,1536]{2,1,0:T(8,128)(2,1)S(1)} %get-tuple-element.54), channel_id=1, source_target_pairs={{0,1},{1,0},{2,3},{3,2},{16,17},{17,16},{18,19},{19,18},{4,5},{5,4... | collective-permute-start | bytes 5308424 | tf_op jit(solution)/shard_map/ppermute | solution.py:577
  7.3 6.1 %collective-permute-start.2 = (f32[4,192,256]{2,1,0:T(8,128)S(1)}, f32[4,192,256]{2,1,0:T(8,128)S(1)}, u32[]{:S(2)}, u32[]{:S(2)}) collective-permute-start(f32[4,192,256]{2,1,0:T(8,128)S(1)} %get-tuple-element.55), channel_id=1, source_target_pairs={{0,1},{1,0},{2,3},{3,2},{16,17},{17,16},{18,19},{19,18},{4,5},{5,4... | collective-permute-start | bytes 2359304 | tf_op jit(solution)/shard_map/ppermute | solution.py:577
  7.4 7.5 %collective-permute-start.3 = (s16[192,384]{1,0:T(8,128)(2,1)S(1)}, s16[192,384]{1,0:T(8,128)(2,1)S(1)}, u32[]{:S(2)}, u32[]{:S(2)}) collective-permute-start(s16[192,384]{1,0:T(8,128)(2,1)S(1)} %get-tuple-element.52.refs_2_), channel_id=1, source_target_pairs={{0,2},{1,3},{2,0},{3,1},{16,18},{17,19},{18,16},{19,17},{4,6},{5,7... | collective-permute-start | bytes 442376 | tf_op jit(solution)/shard_map/ppermute | solution.py:577
  10.3 8.6 %collective-permute-start.10 = (s16[192,384]{1,0:T(8,128)(2,1)S(1)}, s16[192,384]{1,0:T(8,128)(2,1)S(1)}, u32[]{:S(2)}, u32[]{:S(2)}) collective-permute-start(s16[192,384]{1,0:T(8,128)(2,1)S(1)} %get-tuple-element.68), channel_id=1, source_target_pairs={{0,16},{1,17},{2,18},{3,19},{16,0},{17,1},{18,2},{19,3},{4,20},{5,... | collective-permute-start | bytes 442376 | tf_op jit(solution)/shard_map/ppermute | solution.py:577
  11.8 1.6 %copy-start.1 = (f32[8,192,192]{2,1,0:T(8,128)S(1)}, f32[8,192,192]{2,1,0:T(8,128)}, u32[]{:S(2)}) copy-start(f32[8,192,192]{2,1,0:T(8,128)} %refs_0_.1) | copy-start | bytes 3538948
  11.8 1.6 %copy-start.8 = (f32[1,32]{1,0:T(1,128)S(1)}, f32[1,32]{1,0:T(1,128)}, u32[]{:S(2)}) copy-start(f32[1,32]{1,0:T(1,128)} %refs_2_.4) | copy-start | bytes 388
  11.8 7.7 %collective-permute-start.11 = (s16[192,384]{1,0:T(8,128)(2,1)S(1)}, s16[192,384]{1,0:T(8,128)(2,1)S(1)}, u32[]{:S(2)}, u32[]{:S(2)}) collective-permute-start(s16[192,384]{1,0:T(8,128)(2,1)S(1)} %get-tuple-element.69), channel_id=1, source_target_pairs={{0,18},{1,19},{2,16},{3,17},{16,2},{17,3},{18,0},{19,1},{4,22},{5,... | collective-permute-start | bytes 442376 | tf_op jit(solution)/shard_map/ppermute | solution.py:577
  15.2 9.8 %collective-permute-start.4 = (s16[192,384]{1,0:T(8,128)(2,1)S(1)}, s16[192,384]{1,0:T(8,128)(2,1)S(1)}, u32[]{:S(2)}, u32[]{:S(2)}) collective-permute-start(s16[192,384]{1,0:T(8,128)(2,1)S(1)} %get-tuple-element.59), channel_id=1, source_target_pairs={{0,2},{1,3},{2,0},{3,1},{16,18},{17,19},{18,16},{19,17},{4,6},{5,7... | collective-permute-start | bytes 442376 | tf_op jit(solution)/shard_map/ppermute | solution.py:577
  17.3 7.6 %collective-permute-start.5 = (s16[192,384]{1,0:T(8,128)(2,1)S(1)}, s16[192,384]{1,0:T(8,128)(2,1)S(1)}, u32[]{:S(2)}, u32[]{:S(2)}) collective-permute-start(s16[192,384]{1,0:T(8,128)(2,1)S(1)} %get-tuple-element.60), channel_id=1, source_target_pairs={{0,16},{1,17},{2,18},{3,19},{16,0},{17,1},{18,2},{19,3},{4,20},{5,... | collective-permute-start | bytes 442376 | tf_op jit(solution)/shard_map/ppermute | solution.py:577
  19.8 9.1 %collective-permute-start.12 = (s16[192,384]{1,0:T(8,128)(2,1)S(1)}, s16[192,384]{1,0:T(8,128)(2,1)S(1)}, u32[]{:S(2)}, u32[]{:S(2)}) collective-permute-start(s16[192,384]{1,0:T(8,128)(2,1)S(1)} %plane_sum.4), channel_id=1, source_target_pairs={{0,12},{4,8},{8,4},{12,0},{1,13},{5,9},{9,5},{13,1},{2,14},{6,10},... | collective-permute-start | bytes 442376 | tf_op jit(solution)/shard_map/ppermute | solution.py:615
  23.4 7.7 %collective-permute-start.9 = (s16[192,384]{1,0:T(8,128)(2,1)S(1)}, s16[192,384]{1,0:T(8,128)(2,1)S(1)}, u32[]{:S(2)}, u32[]{:S(2)}) collective-permute-start(s16[192,384]{1,0:T(8,128)(2,1)S(1)} %get-tuple-element.66), channel_id=1, source_target_pairs={{0,18},{1,19},{2,16},{3,17},{16,2},{17,3},{18,0},{19,1},{4,22},{5,... | collective-permute-start | bytes 442376 | tf_op jit(solution)/shard_map/ppermute | solution.py:577
  25.3 7.7 %collective-permute-start.6 = (s16[192,384]{1,0:T(8,128)(2,1)S(1)}, s16[192,384]{1,0:T(8,128)(2,1)S(1)}, u32[]{:S(2)}, u32[]{:S(2)}) collective-permute-start(s16[192,384]{1,0:T(8,128)(2,1)S(1)} %get-tuple-element.62), channel_id=1, source_target_pairs={{0,2},{1,3},{2,0},{3,1},{16,18},{17,19},{18,16},{19,17},{4,6},{5,7... | collective-permute-start | bytes 442376 | tf_op jit(solution)/shard_map/ppermute | solution.py:577
  27.0 6.3 %collective-permute-start.7 = (s16[192,384]{1,0:T(8,128)(2,1)S(1)}, s16[192,384]{1,0:T(8,128)(2,1)S(1)}, u32[]{:S(2)}, u32[]{:S(2)}) collective-permute-start(s16[192,384]{1,0:T(8,128)(2,1)S(1)} %get-tuple-element.63), channel_id=1, source_target_pairs={{0,16},{1,17},{2,18},{3,19},{16,0},{17,1},{18,2},{19,3},{4,20},{5,... | collective-permute-start | bytes 442376 | tf_op jit(solution)/shard_map/ppermute | solution.py:577
  27.3 9.8 %collective-permute-start.8 = (s16[192,384]{1,0:T(8,128)(2,1)S(1)}, s16[192,384]{1,0:T(8,128)(2,1)S(1)}, u32[]{:S(2)}, u32[]{:S(2)}) collective-permute-start(s16[192,384]{1,0:T(8,128)(2,1)S(1)} %get-tuple-element.64), channel_id=1, source_target_pairs={{0,18},{1,19},{2,16},{3,17},{16,2},{17,3},{18,0},{19,1},{4,22},{5,... | collective-permute-start | bytes 442376 | tf_op jit(solution)/shard_map/ppermute | solution.py:577
  31.4 6.8 %collective-permute-start.13 = (s16[192,384]{1,0:T(8,128)(2,1)S(1)}, s16[192,384]{1,0:T(8,128)(2,1)S(1)}, u32[]{:S(2)}, u32[]{:S(2)}) collective-permute-start(s16[192,384]{1,0:T(8,128)(2,1)S(1)} %plane_sum.5), channel_id=1, source_target_pairs={{0,8},{4,12},{8,0},{12,4},{1,9},{5,13},{9,1},{13,5},{2,10},{6,14},... | collective-permute-start | bytes 442376 | tf_op jit(solution)/shard_map/ppermute | solution.py:615
  33.3 5.2 %copy-start.4 = (f32[8,64,128]{2,1,0:T(8,128)S(1)}, f32[8,64,128]{2,1,0:T(8,128)}, u32[]{:S(2)}) copy-start(f32[8,64,128]{2,1,0:T(8,128)} %refs_1_.1) | copy-start | bytes 786436
  33.3 6.5 %copy-start.2 = (f32[8,192,192]{2,1,0:T(8,128)S(1)}, f32[8,192,192]{2,1,0:T(8,128)}, u32[]{:S(2)}) copy-start(f32[8,192,192]{2,1,0:T(8,128)} %refs_2_.5) | copy-start | bytes 3538948
  33.6 8.0 %collective-permute-start.14 = (s16[192,384]{1,0:T(8,128)(2,1)S(1)}, s16[192,384]{1,0:T(8,128)(2,1)S(1)}, u32[]{:S(2)}, u32[]{:S(2)}) collective-permute-start(s16[192,384]{1,0:T(8,128)(2,1)S(1)} %get-tuple-element.75), channel_id=1, source_target_pairs={{0,2},{1,3},{2,0},{3,1},{16,18},{17,19},{18,16},{19,17},{4,6},{5,7... | collective-permute-start | bytes 442376 | tf_op jit(solution)/shard_map/ppermute | solution.py:577
  35.0 7.7 %collective-permute-start.15 = (s16[192,384]{1,0:T(8,128)(2,1)S(1)}, s16[192,384]{1,0:T(8,128)(2,1)S(1)}, u32[]{:S(2)}, u32[]{:S(2)}) collective-permute-start(s16[192,384]{1,0:T(8,128)(2,1)S(1)} %get-tuple-element.76), channel_id=1, source_target_pairs={{0,16},{1,17},{2,18},{3,19},{16,0},{17,1},{18,2},{19,3},{4,20},{5,... | collective-permute-start | bytes 442376 | tf_op jit(solution)/shard_map/ppermute | solution.py:577
  35.8 6.8 %collective-permute-start.16 = (s16[192,384]{1,0:T(8,128)(2,1)S(1)}, s16[192,384]{1,0:T(8,128)(2,1)S(1)}, u32[]{:S(2)}, u32[]{:S(2)}) collective-permute-start(s16[192,384]{1,0:T(8,128)(2,1)S(1)} %get-tuple-element.77), channel_id=1, source_target_pairs={{0,18},{1,19},{2,16},{3,17},{16,2},{17,3},{18,0},{19,1},{4,22},{5,... | collective-permute-start | bytes 442376 | tf_op jit(solution)/shard_map/ppermute | solution.py:577
  38.4 5.2 %collective-permute-start.17 = (s16[192,384]{1,0:T(8,128)(2,1)S(1)}, s16[192,384]{1,0:T(8,128)(2,1)S(1)}, u32[]{:S(2)}, u32[]{:S(2)}) collective-permute-start(s16[192,384]{1,0:T(8,128)(2,1)S(1)} %get-tuple-element.78), channel_id=1, source_target_pairs={{0,4},{4,0},{8,12},{12,8},{1,5},{5,1},{9,13},{13,9},{2,6},{6,2},{1... | collective-permute-start | bytes 442376 | tf_op jit(solution)/shard_map/ppermute | solution.py:615
  39.8 3.8 %copy-start.3 = (f32[8,64,128]{2,1,0:T(8,128)S(1)}, f32[8,64,128]{2,1,0:T(8,128)}, u32[]{:S(2)}) copy-start(f32[8,64,128]{2,1,0:T(8,128)} %scale_keys.1.refs_6_) | copy-start | bytes 786436
  44.9 5.2 %collective-permute-start.18 = (s16[224,128]{1,0:T(8,128)(2,1)S(1)}, s16[224,128]{1,0:T(8,128)(2,1)S(1)}, u32[]{:S(2)}, u32[]{:S(2)}) collective-permute-start(s16[224,128]{1,0:T(8,128)(2,1)S(1)} %get-tuple-element.84), channel_id=1, source_target_pairs={{0,18},{1,19},{2,16},{3,17},{16,2},{17,3},{18,0},{19,1},{4,22},{5,... | collective-permute-start | bytes 172040 | tf_op jit(solution)/shard_map/ppermute | solution.py:577
  46.4 4.3 %collective-permute-start.19 = (s16[224,128]{1,0:T(8,128)(2,1)S(1)}, s16[224,128]{1,0:T(8,128)(2,1)S(1)}, u32[]{:S(2)}, u32[]{:S(2)}) collective-permute-start(s16[224,128]{1,0:T(8,128)(2,1)S(1)} %get-tuple-element.85), channel_id=1, source_target_pairs={{0,16},{1,17},{2,18},{3,19},{16,0},{17,1},{18,2},{19,3},{4,20},{5,... | collective-permute-start | bytes 172040 | tf_op jit(solution)/shard_map/ppermute | solution.py:577
  48.0 4.2 %collective-permute-start.20 = (s16[224,128]{1,0:T(8,128)(2,1)S(1)}, s16[224,128]{1,0:T(8,128)(2,1)S(1)}, u32[]{:S(2)}, u32[]{:S(2)}) collective-permute-start(s16[224,128]{1,0:T(8,128)(2,1)S(1)} %get-tuple-element.86), channel_id=1, source_target_pairs={{0,2},{1,3},{2,0},{3,1},{16,18},{17,19},{18,16},{19,17},{4,6},{5,7... | collective-permute-start | bytes 172040 | tf_op jit(solution)/shard_map/ppermute | solution.py:577
  54.1 8.7 %collective-permute-start.21 = (f32[4,192,192]{2,1,0:T(8,128)S(1)}, f32[4,192,192]{2,1,0:T(8,128)S(1)}, u32[]{:S(2)}, u32[]{:S(2)}) collective-permute-start(f32[4,192,192]{2,1,0:T(8,128)S(1)} %get-tuple-element.87), channel_id=1, source_target_pairs={{0,1},{1,0},{2,3},{3,2},{16,17},{17,16},{18,19},{19,18},{4,5},{5,4... | collective-permute-start | bytes 1769480 | tf_op jit(solution)/shard_map/ppermute | solution.py:577
  54.1 5.4 %collective-permute-start.27 = (bf16[240,128]{1,0:T(8,128)(2,1)S(1)}, bf16[240,128]{1,0:T(8,128)(2,1)S(1)}, u32[]{:S(2)}, u32[]{:S(2)}) collective-permute-start(bf16[240,128]{1,0:T(8,128)(2,1)S(1)} %newton_schulz.1.refs_1_.refs_3_), channel_id=1, source_target_pairs={{0,18},{1,19},{2,16},{3,17},{16,2},{17,3},{18,0},{19,1},{4,22},{5,... | collective-permute-start | bytes 184328 | tf_op jit(solution)/shard_map/ppermute | solution.py:577
  55.4 5.3 %collective-permute-start.25 = (bf16[240,128]{1,0:T(8,128)(2,1)S(1)}, bf16[240,128]{1,0:T(8,128)(2,1)S(1)}, u32[]{:S(2)}, u32[]{:S(2)}) collective-permute-start(bf16[240,128]{1,0:T(8,128)(2,1)S(1)} %newton_schulz.1.refs_1_.refs_3_), channel_id=1, source_target_pairs={{0,16},{1,17},{2,18},{3,19},{16,0},{17,1},{18,2},{19,3},{4,20},{5,... | collective-permute-start | bytes 184328 | tf_op jit(solution)/shard_map/ppermute | solution.py:577
  56.1 4.7 %collective-permute-start.23 = (bf16[240,128]{1,0:T(8,128)(2,1)S(1)}, bf16[240,128]{1,0:T(8,128)(2,1)S(1)}, u32[]{:S(2)}, u32[]{:S(2)}) collective-permute-start(bf16[240,128]{1,0:T(8,128)(2,1)S(1)} %newton_schulz.1.refs_1_.refs_3_), channel_id=1, source_target_pairs={{0,2},{1,3},{2,0},{3,1},{16,18},{17,19},{18,16},{19,17},{4,6},{5,7... | collective-permute-start | bytes 184328 | tf_op jit(solution)/shard_map/ppermute | solution.py:577
  57.7 5.1 %collective-permute-start.22 = (bf16[240,128]{1,0:T(8,128)(2,1)S(1)}, bf16[240,128]{1,0:T(8,128)(2,1)S(1)}, u32[]{:S(2)}, u32[]{:S(2)}) collective-permute-start(bf16[240,128]{1,0:T(8,128)(2,1)S(1)} %newton_schulz.1.refs_1_.refs_3_), channel_id=1, source_target_pairs={{0,1},{1,0},{2,3},{3,2},{16,17},{17,16},{18,19},{19,18},{4,5},{5,4... | collective-permute-start | bytes 184328 | tf_op jit(solution)/shard_map/ppermute | solution.py:577
  59.6 3.2 %collective-permute-start.28 = (bf16[240,128]{1,0:T(8,128)(2,1)S(1)}, bf16[240,128]{1,0:T(8,128)(2,1)S(1)}, u32[]{:S(2)}, u32[]{:S(2)}) collective-permute-start(bf16[240,128]{1,0:T(8,128)(2,1)S(1)} %collective-permute-done.27.refs_6_), channel_id=1, source_target_pairs={{0,1},{1,0},{2,3},{3,2},{16,17},{17,16},{18,19},{19,18},{4,5},{5,4... | collective-permute-start | bytes 184328 | tf_op jit(solution)/shard_map/ppermute | solution.py:577
  60.8 2.0 %collective-permute-start.26 = (bf16[240,128]{1,0:T(8,128)(2,1)S(1)}, bf16[240,128]{1,0:T(8,128)(2,1)S(1)}, u32[]{:S(2)}, u32[]{:S(2)}) collective-permute-start(bf16[240,128]{1,0:T(8,128)(2,1)S(1)} %collective-permute-done.25.refs_5_), channel_id=1, source_target_pairs={{0,1},{1,0},{2,3},{3,2},{16,17},{17,16},{18,19},{19,18},{4,5},{5,4... | collective-permute-start | bytes 184328 | tf_op jit(solution)/shard_map/ppermute | solution.py:577
  60.8 2.0 %collective-permute-start.24 = (bf16[240,128]{1,0:T(8,128)(2,1)S(1)}, bf16[240,128]{1,0:T(8,128)(2,1)S(1)}, u32[]{:S(2)}, u32[]{:S(2)}) collective-permute-start(bf16[240,128]{1,0:T(8,128)(2,1)S(1)} %collective-permute-done.23.refs_4_), channel_id=1, source_target_pairs={{0,1},{1,0},{2,3},{3,2},{16,17},{17,16},{18,19},{19,18},{4,5},{5,4... | collective-permute-start | bytes 184328 | tf_op jit(solution)/shard_map/ppermute | solution.py:577

commit v6 on v5

--- a/solution.py
+++ b/solution.py
@@ -490,12 +490,13 @@
     step_size = 0.04 * math.sqrt(max(rows_all, cols))
     _, chip, core = whereabouts()
     place = 1 - core if other else core
-    def stored(s):
-        to = momentum_out.at[s * CORES + place]
-        return pltpu.make_async_copy(momentum.at[s], to, momentum_sem.at[s])
-
-    for s in range(sources):
-        stored(s).start()
+    stores = []
+    if not other:
+        for s in range(sources):
+            for half, to in ((momentum, place), (refs[0], 1 - place)):
+                to = momentum_out.at[s * CORES + to]
+                stores.append(pltpu.make_async_copy(half.at[s], to, momentum_sem.at[len(stores)]))
+                stores[-1].start()
 
     def written(k):
         return pltpu.make_async_copy(result.at[k], out.at[(chip ^ k) * CORES + place], sem.at[k])
@@ -524,14 +525,14 @@
             only(k, lambda k=k: written(k).start())
     for k in range(chips):
         only(k, lambda k=k: written(k).wait())
-    for s in range(sources):
-        stored(s).wait()
-
-
-def weights(base, scales, momentum, blocks, filled=()):
+    for store in stores:
+        store.wait()
+
+
+def weights(base, scales, momentum, blocks, sibling=(), filled=()):
     chips = len(blocks)
     slots, rows, cols = base.shape
-    ins = [(VMEM, value) for value in (base, scales, momentum, *blocks)]
+    ins = [(VMEM, value) for value in (base, scales, momentum, *blocks, *sibling)]
     aliases = {len(ins) + i: i for i in range(len(filled))}
     return call(
         functools.partial(weight_kernel, chips, bool(filled), rows * chips * CORES),
@@ -542,7 +543,7 @@
             pltpu.VMEM((chips, cols, cols), jnp.bfloat16),
             pltpu.VMEM((chips, rows, cols), jnp.float32),
             pltpu.SemaphoreType.DMA((chips,)),
-            pltpu.SemaphoreType.DMA((slots // CORES,)),
+            pltpu.SemaphoreType.DMA((slots,)),
         ],
         aliases=aliases,
     )
@@ -627,8 +628,8 @@
     sibling_new = swap(sibling_new, 1)
     results = [result] + [swap(result, CORES * k) for k in range(1, chips)]
     sibling_results = [swap(value, 1) for value in results]
-    filled = weights(base, scales, own_new, results)
-    q_weight_out, momentum_out = weights(base, scales, sibling_new, sibling_results, filled)
+    filled = weights(base, scales, own_new, results, [sibling_new])
+    q_weight_out, momentum_out = weights(base, scales, sibling_new, sibling_results, filled=filled)
     return (momentum_out, q_weight_out, k_weight_out)
 
 

time: 64.4 us -> 64.6 us (level)
  no operation moved by 1% of the time
where the time goes in v6:
time: 64.6 us; the launch traced here: 64.4 us
  starting transfers between devices  29.3 us (45%)
  Pallas kernels  17.5 us (27%)
  waiting for transfers between devices  15.4 us (24%)
  local copies, waits for them, and re-layouts  1.33 us (2%)
  between operations  0.89 us (1%)
    ppermute x26, starting transfers between devices, swap(): return lax.ppermute(value, PLANE, [(i, i ^ bits) for i in range(devices)])  25.5 us
    pallas_call x20, Pallas kernels, call(): pl.pallas_call(whole, in_specs=[spec for spec, _ in ins] + [ANY] * len(af...  17.5 us
    ppermute x26, waiting for transfers between devices, swap(): return lax.ppermute(value, PLANE, [(i, i ^ bits) for i in range(devices)])  13.4 us
    ppermute x3, starting transfers between devices, body(): lax.ppermute(total, 'owner', [(j, j ^ k) for j in range(sources)])  3.81 us
    ppermute x3, waiting for transfers between devices, body(): lax.ppermute(total, 'owner', [(j, j ^ k) for j in range(sources)])  2.04 us
    unnamed x18, local copies, waits for them, and re-layouts  1.33 us
  transfers between devices with their start and end apart: 29, of which 14 were waited for; matrix products, arithmetic and copies ran while one was open for 0% of the time, Pallas kernels for 16%

profile of v6, /device:TPU:0, one launch (start us, length us, event | category | flops | bytes accessed | tf_op | source)
XLA Modules:
  0.0 64.4 jit_solution(4140823148145391296)
XLA Ops:
  0.6 0.0 copy-start.5
  0.6 0.6 %copy-done.5 = s32[32,1]{0,1:T(1,128)S(1)} copy-done((s32[32,1]{0,1:T(1,128)S(1)}, s32[32,1]{0,1:T(1,128)}, u32[]{:S(2)}) %copy-start.5) | copy-done | bytes 152
  1.3 0.7 %copy-done.7 = f32[1,32]{1,0:T(1,128)S(1)} copy-done((f32[1,32]{1,0:T(1,128)S(1)}, f32[1,32]{1,0:T(1,128)}, u32[]{:S(2)}) %copy-start.7) | copy-done | bytes 152
  1.9 2.3 %fetch_heads.3 = (f32[4,192,256]{2,1,0:T(8,128)S(1)}, bf16[1,192,1536]{2,1,0:T(8,128)(2,1)S(1)}, f32[8,128]{1,0:T(8,128)S(1)}) custom-call(s32[1,32]{1,0:T(1,128)S(1)} %bitcast.7, bf16[8,192,1536]{2,1,0:T(8,128)(2,1)} %bitcast.4, f32[8,192,192]{2,1,0:T(8,128)} %refs_0_.1, f32[1,32]{1,0:T(1,128)S(1)} %copy-done.7), custom_call_target="tpu_custom_call" | custom-call | tf_op jit(solution)/shard_map/fetch_heads/pallas_call | solution.py:51
  4.3 0.5 collective-permute-start
  4.8 1.7 %fetch_heads.4 = (bf16[3,192,1536]{2,1,0:T(8,128)(2,1)S(1)}, bf16[1,192,1536]{2,1,0:T(8,128)(2,1)S(1)}, f32[8,128]{1,0:T(8,128)}) custom-call(s32[1,32]{1,0:T(1,128)S(1)} %bitcast.8, bf16[8,192,1536]{2,1,0:T(8,128)(2,1)S(1)} %bitcast.5, f32[8,128]{1,0:T(8,128)S(1)} %get-tuple-element.48.refs_2_), custom_call_target="tpu_custom_call" | custom-call | tf_op jit(solution)/shard_map/fetch_heads/pallas_call | solution.py:51
  6.5 0.0 copy-start.6
  6.6 0.3 pair_sum.4
  6.9 0.4 collective-permute-start.1
  7.3 0.2 collective-permute-start.2
  7.4 2.9 %collective-permute-start.3 = (s16[192,384]{1,0:T(8,128)(2,1)S(1)}, s16[192,384]{1,0:T(8,128)(2,1)S(1)}, u32[]{:S(2)}, u32[]{:S(2)}) collective-permute-start(s16[192,384]{1,0:T(8,128)(2,1)S(1)} %get-tuple-element.52.refs_2_), channel_id=1, source_target_pairs={{0,2},{1,3},{2,0},{3,1},{16,18},{17,19},{18,16},{19,17},{4,6},{5,7... | collective-permute-start | bytes 442376 | tf_op jit(solution)/shard_map/ppermute | solution.py:578
  10.3 1.5 %collective-permute-start.10 = (s16[192,384]{1,0:T(8,128)(2,1)S(1)}, s16[192,384]{1,0:T(8,128)(2,1)S(1)}, u32[]{:S(2)}, u32[]{:S(2)}) collective-permute-start(s16[192,384]{1,0:T(8,128)(2,1)S(1)} %get-tuple-element.68), channel_id=1, source_target_pairs={{0,16},{1,17},{2,18},{3,19},{16,0},{17,1},{18,2},{19,3},{4,20},{5,... | collective-permute-start | bytes 442376 | tf_op jit(solution)/shard_map/ppermute | solution.py:578
  11.8 1.6 %fetch_heads.5 = (bf16[1,192,1536]{2,1,0:T(8,128)(2,1)S(1)}, bf16[1,192,1536]{2,1,0:T(8,128)(2,1)S(1)}, bf16[1,192,1536]{2,1,0:T(8,128)(2,1)S(1)}, f32[8,128]{1,0:T(8,128)}) custom-call(s32[1,32]{1,0:T(1,128)S(1)} %bitcast.9, bf16[8,192,1536]{2,1,0:T(8,128)(2,1)S(1)} %bitcast.6, s16[192,384]{1,0:T(8,128)(2,1)S(1)} %get-tuple-element.52.refs_2_), custom_call_target="tpu_custom_call" | custom-call | tf_op jit(solution)/shard_map/fetch_heads/pallas_call | solution.py:51
  13.5 0.7 %turn_momentum.1 = (f32[4,192,384]{2,1,0:T(8,128)S(1)}, f32[1,32]{1,0:T(1,128)S(1)}) custom-call(f32[8,192,192]{2,1,0:T(8,128)S(1)} %copy-done.1, f32[4,192,256]{2,1,0:T(8,128)S(1)} %collective-permute-done.2.refs_1_, f32[1,32]{1,0:T(1,128)S(1)} %copy-done.8), custom_call_target="tpu_custom_call" | custom-call | tf_op jit(solution)/shard_map/turn_momentum/pallas_call | solution.py:51
  14.2 0.7 %collective-permute-done.3.refs_2_.refs_1_ = s16[192,384]{1,0:T(8,128)(2,1)S(1)} collective-permute-done((s16[192,384]{1,0:T(8,128)(2,1)S(1)}, s16[192,384]{1,0:T(8,128)(2,1)S(1)}, u32[]{:S(2)}, u32[]{:S(2)}) %collective-permute-start.3) | collective-permute-done | bytes 147488 | tf_op jit(solution)/shard_map/ppermute | solution.py:578
  14.9 0.3 pair_sum.5
  15.2 2.1 %collective-permute-start.4 = (s16[192,384]{1,0:T(8,128)(2,1)S(1)}, s16[192,384]{1,0:T(8,128)(2,1)S(1)}, u32[]{:S(2)}, u32[]{:S(2)}) collective-permute-start(s16[192,384]{1,0:T(8,128)(2,1)S(1)} %get-tuple-element.59), channel_id=1, source_target_pairs={{0,2},{1,3},{2,0},{3,1},{16,18},{17,19},{18,16},{19,17},{4,6},{5,7... | collective-permute-start | bytes 442376 | tf_op jit(solution)/shard_map/ppermute | solution.py:578
  17.3 1.5 %collective-permute-start.5 = (s16[192,384]{1,0:T(8,128)(2,1)S(1)}, s16[192,384]{1,0:T(8,128)(2,1)S(1)}, u32[]{:S(2)}, u32[]{:S(2)}) collective-permute-start(s16[192,384]{1,0:T(8,128)(2,1)S(1)} %get-tuple-element.60), channel_id=1, source_target_pairs={{0,16},{1,17},{2,18},{3,19},{16,0},{17,1},{18,2},{19,3},{4,20},{5,... | collective-permute-start | bytes 442376 | tf_op jit(solution)/shard_map/ppermute | solution.py:578
  18.9 0.1 collective-permute-done.10.refs_2_
  18.9 0.6 collective-permute-done.11.refs_3_
  19.5 0.2 plane_sum.4
  19.8 3.7 %collective-permute-start.12 = (s16[192,384]{1,0:T(8,128)(2,1)S(1)}, s16[192,384]{1,0:T(8,128)(2,1)S(1)}, u32[]{:S(2)}, u32[]{:S(2)}) collective-permute-start(s16[192,384]{1,0:T(8,128)(2,1)S(1)} %plane_sum.4), channel_id=1, source_target_pairs={{0,12},{4,8},{8,4},{12,0},{1,13},{5,9},{9,5},{13,1},{2,14},{6,10},... | collective-permute-start | bytes 442376 | tf_op jit(solution)/shard_map/ppermute | solution.py:616
  23.4 1.5 %collective-permute-start.9 = (s16[192,384]{1,0:T(8,128)(2,1)S(1)}, s16[192,384]{1,0:T(8,128)(2,1)S(1)}, u32[]{:S(2)}, u32[]{:S(2)}) collective-permute-start(s16[192,384]{1,0:T(8,128)(2,1)S(1)} %get-tuple-element.66), channel_id=1, source_target_pairs={{0,18},{1,19},{2,16},{3,17},{16,2},{17,3},{18,0},{19,1},{4,22},{5,... | collective-permute-start | bytes 442376 | tf_op jit(solution)/shard_map/ppermute | solution.py:578
  25.0 0.3 pair_sum.6
  25.3 1.7 %collective-permute-start.6 = (s16[192,384]{1,0:T(8,128)(2,1)S(1)}, s16[192,384]{1,0:T(8,128)(2,1)S(1)}, u32[]{:S(2)}, u32[]{:S(2)}) collective-permute-start(s16[192,384]{1,0:T(8,128)(2,1)S(1)} %get-tuple-element.62), channel_id=1, source_target_pairs={{0,2},{1,3},{2,0},{3,1},{16,18},{17,19},{18,16},{19,17},{4,6},{5,7... | collective-permute-start | bytes 442376 | tf_op jit(solution)/shard_map/ppermute | solution.py:578
  27.0 0.3 collective-permute-start.7
  27.3 1.5 %collective-permute-start.8 = (s16[192,384]{1,0:T(8,128)(2,1)S(1)}, s16[192,384]{1,0:T(8,128)(2,1)S(1)}, u32[]{:S(2)}, u32[]{:S(2)}) collective-permute-start(s16[192,384]{1,0:T(8,128)(2,1)S(1)} %get-tuple-element.64), channel_id=1, source_target_pairs={{0,18},{1,19},{2,16},{3,17},{16,2},{17,3},{18,0},{19,1},{4,22},{5,... | collective-permute-start | bytes 442376 | tf_op jit(solution)/shard_map/ppermute | solution.py:578
  28.9 2.3 %collective-permute-done.9.refs_3_ = s16[192,384]{1,0:T(8,128)(2,1)S(1)} collective-permute-done((s16[192,384]{1,0:T(8,128)(2,1)S(1)}, s16[192,384]{1,0:T(8,128)(2,1)S(1)}, u32[]{:S(2)}, u32[]{:S(2)}) %collective-permute-start.9) | collective-permute-done | bytes 147488 | tf_op jit(solution)/shard_map/ppermute | solution.py:578
  31.2 0.2 plane_sum.5
  31.4 0.1 collective-permute-start.13
  31.5 1.5 %collective-permute-done.6.refs_1_.refs_2_ = s16[192,384]{1,0:T(8,128)(2,1)S(1)} collective-permute-done((s16[192,384]{1,0:T(8,128)(2,1)S(1)}, s16[192,384]{1,0:T(8,128)(2,1)S(1)}, u32[]{:S(2)}, u32[]{:S(2)}) %collective-permute-start.6) | collective-permute-done | bytes 147488 | tf_op jit(solution)/shard_map/ppermute | solution.py:578
  32.9 0.3 collective-permute-done.7.refs_2_.refs_3_
  33.3 0.3 pair_sum.7
  33.6 1.4 %collective-permute-start.14 = (s16[192,384]{1,0:T(8,128)(2,1)S(1)}, s16[192,384]{1,0:T(8,128)(2,1)S(1)}, u32[]{:S(2)}, u32[]{:S(2)}) collective-permute-start(s16[192,384]{1,0:T(8,128)(2,1)S(1)} %get-tuple-element.75), channel_id=1, source_target_pairs={{0,2},{1,3},{2,0},{3,1},{16,18},{17,19},{18,16},{19,17},{4,6},{5,7... | collective-permute-start | bytes 442376 | tf_op jit(solution)/shard_map/ppermute | solution.py:578
  35.0 0.8 %collective-permute-start.15 = (s16[192,384]{1,0:T(8,128)(2,1)S(1)}, s16[192,384]{1,0:T(8,128)(2,1)S(1)}, u32[]{:S(2)}, u32[]{:S(2)}) collective-permute-start(s16[192,384]{1,0:T(8,128)(2,1)S(1)} %get-tuple-element.76), channel_id=1, source_target_pairs={{0,16},{1,17},{2,18},{3,19},{16,0},{17,1},{18,2},{19,3},{4,20},{5,... | collective-permute-start | bytes 442376 | tf_op jit(solution)/shard_map/ppermute | solution.py:578
  35.8 1.3 %collective-permute-start.16 = (s16[192,384]{1,0:T(8,128)(2,1)S(1)}, s16[192,384]{1,0:T(8,128)(2,1)S(1)}, u32[]{:S(2)}, u32[]{:S(2)}) collective-permute-start(s16[192,384]{1,0:T(8,128)(2,1)S(1)} %get-tuple-element.77), channel_id=1, source_target_pairs={{0,18},{1,19},{2,16},{3,17},{16,2},{17,3},{18,0},{19,1},{4,22},{5,... | collective-permute-start | bytes 442376 | tf_op jit(solution)/shard_map/ppermute | solution.py:578
  37.1 1.1 %collective-permute-done.13.refs_5_.refs_3_ = s16[192,384]{1,0:T(8,128)(2,1)S(1)} collective-permute-done((s16[192,384]{1,0:T(8,128)(2,1)S(1)}, s16[192,384]{1,0:T(8,128)(2,1)S(1)}, u32[]{:S(2)}, u32[]{:S(2)}) %collective-permute-start.13) | collective-permute-done | bytes 147488 | tf_op jit(solution)/shard_map/ppermute | solution.py:616
  38.2 0.2 plane_sum.6
  38.4 0.1 collective-permute-start.17
  38.5 1.3 %scale_keys.1.refs_6_ = f32[8,64,128]{2,1,0:T(8,128)} custom-call(f32[1,32]{1,0:T(1,128)S(1)} %get-tuple-element.70.refs_1_.refs_0_, f32[8,64,128]{2,1,0:T(8,128)S(1)} %copy-done.4), custom_call_target="tpu_custom_call" | custom-call | tf_op jit(solution)/shard_map/scale_keys/pallas_call | solution.py:51
  39.8 0.8 %scale_weight.1 = (f32[8,192,192]{2,1,0:T(8,128)S(1)}, f32[8,192]{1,0:T(8,128)S(1)}) custom-call(s32[1,32]{1,0:T(1,128)S(1)} %bitcast.10, f32[1,32]{1,0:T(1,128)S(1)} %get-tuple-element.70.refs_1_.refs_0_, f32[8,192,192]{2,1,0:T(8,128)S(1)} %copy-done.2), custom_call_target="tpu_custom_call" | custom-call | tf_op jit(solution)/shard_map/scale_weight/pallas_call | solution.py:51
  40.6 1.0 %early_gram.1 = (f32[2,192,384]{2,1,0:T(8,128)S(1)}, f32[2,224,128]{2,1,0:T(8,128)S(1)}, s16[2,224,128]{2,1,0:T(8,128)(2,1)S(1)}) custom-call(s32[1,32]{1,0:T(1,128)S(1)} %bitcast.11, f32[4,192,384]{2,1,0:T(8,128)S(1)} %get-tuple-element.58.refs_3_.refs_1_, s16[192,384]{1,0:T(8,128)(2,1)S(1)} %collective-permute-done.12.refs_4_.refs_2_, ...), custom_call_target="tpu_custom_call" | custom-call | tf_op jit(solution)/shard_map/early_gram/pallas_call | solution.py:51
  41.6 1.0 %collective-permute-done.15.refs_2_ = s16[192,384]{1,0:T(8,128)(2,1)S(1)} collective-permute-done((s16[192,384]{1,0:T(8,128)(2,1)S(1)}, s16[192,384]{1,0:T(8,128)(2,1)S(1)}, u32[]{:S(2)}, u32[]{:S(2)}) %collective-permute-start.15) | collective-permute-done | bytes 147488 | tf_op jit(solution)/shard_map/ppermute | solution.py:578
  42.6 1.0 %collective-permute-done.17.refs_4_.refs_6_ = s16[192,384]{1,0:T(8,128)(2,1)S(1)} collective-permute-done((s16[192,384]{1,0:T(8,128)(2,1)S(1)}, s16[192,384]{1,0:T(8,128)(2,1)S(1)}, u32[]{:S(2)}, u32[]{:S(2)}) %collective-permute-start.17) | collective-permute-done | bytes 147488 | tf_op jit(solution)/shard_map/ppermute | solution.py:616
  43.6 0.1 plane_sum.7.refs_2_
  43.8 1.1 %refresh_and_gram.1 = (f32[4,192,384]{2,1,0:T(8,128)S(1)}, f32[224,128]{1,0:T(8,128)S(1)}, s16[224,128]{1,0:T(8,128)(2,1)S(1)}, s16[224,128]{1,0:T(8,128)(2,1)S(1)}, s16[224,128]{1,0:T(8,128)(2,1)S(1)}) custom-call(s32[1,32]{1,0:T(1,128)S(1)} %bitcast.12, f32[4,192,384]{2,1,0:T(8,128)S(1)} %get-tuple-element.58.refs_3_.refs_1_, ...), custom_call_target="tpu_custom_call" | custom-call | tf_op jit(solution)/shard_map/refresh_and_gram/pallas_call | solution.py:51
  44.9 1.5 %collective-permute-start.18 = (s16[224,128]{1,0:T(8,128)(2,1)S(1)}, s16[224,128]{1,0:T(8,128)(2,1)S(1)}, u32[]{:S(2)}, u32[]{:S(2)}) collective-permute-start(s16[224,128]{1,0:T(8,128)(2,1)S(1)} %get-tuple-element.84), channel_id=1, source_target_pairs={{0,18},{1,19},{2,16},{3,17},{16,2},{17,3},{18,0},{19,1},{4,22},{5,... | collective-permute-start | bytes 172040 | tf_op jit(solution)/shard_map/ppermute | solution.py:578
  46.4 1.6 %collective-permute-start.19 = (s16[224,128]{1,0:T(8,128)(2,1)S(1)}, s16[224,128]{1,0:T(8,128)(2,1)S(1)}, u32[]{:S(2)}, u32[]{:S(2)}) collective-permute-start(s16[224,128]{1,0:T(8,128)(2,1)S(1)} %get-tuple-element.85), channel_id=1, source_target_pairs={{0,16},{1,17},{2,18},{3,19},{16,0},{17,1},{18,2},{19,3},{4,20},{5,... | collective-permute-start | bytes 172040 | tf_op jit(solution)/shard_map/ppermute | solution.py:578
  48.0 0.5 collective-permute-start.20
  48.5 1.6 %collective-permute-done.18.refs_1_ = s16[224,128]{1,0:T(8,128)(2,1)S(1)} collective-permute-done((s16[224,128]{1,0:T(8,128)(2,1)S(1)}, s16[224,128]{1,0:T(8,128)(2,1)S(1)}, u32[]{:S(2)}, u32[]{:S(2)}) %collective-permute-start.18) | collective-permute-done | bytes 57376 | tf_op jit(solution)/shard_map/ppermute | solution.py:578
  50.1 0.6 collective-permute-done.19.refs_2_
  50.7 1.5 %collective-permute-done.20.refs_3_ = s16[224,128]{1,0:T(8,128)(2,1)S(1)} collective-permute-done((s16[224,128]{1,0:T(8,128)(2,1)S(1)}, s16[224,128]{1,0:T(8,128)(2,1)S(1)}, u32[]{:S(2)}, u32[]{:S(2)}) %collective-permute-start.20) | collective-permute-done | bytes 57376 | tf_op jit(solution)/shard_map/ppermute | solution.py:578
  52.2 1.2 %newton_schulz.1.refs_1_.refs_3_ = bf16[240,128]{1,0:T(8,128)(2,1)S(1)} custom-call(f32[224,128]{1,0:T(8,128)S(1)} %get-tuple-element.83.refs_0_, s16[224,128]{1,0:T(8,128)(2,1)S(1)} %collective-permute-done.18.refs_1_, s16[224,128]{1,0:T(8,128)(2,1)S(1)} %collective-permute-done.19.refs_2_, s16[224,128]{1,0:T(8,128)(2,1)S(1)} %collective-permute-done.20.refs_3_), custom_call_target="tpu_custom_call" | custom-call | tf_op jit(solution)/shard_map/newton_schulz/pallas_call | solution.py:51
  53.3 0.7 %turn_back.1 = (f32[4,192,192]{2,1,0:T(8,128)S(1)}, f32[4,192,192]{2,1,0:T(8,128)S(1)}) custom-call(f32[4,192,384]{2,1,0:T(8,128)S(1)} %get-tuple-element.82.refs_0_, bf16[240,128]{1,0:T(8,128)(2,1)S(1)} %newton_schulz.1.refs_1_.refs_3_), custom_call_target="tpu_custom_call" | custom-call | tf_op jit(solution)/shard_map/turn_back/pallas_call | solution.py:51
  54.1 0.1 collective-permute-start.21
  54.1 1.3 %collective-permute-start.27 = (bf16[240,128]{1,0:T(8,128)(2,1)S(1)}, bf16[240,128]{1,0:T(8,128)(2,1)S(1)}, u32[]{:S(2)}, u32[]{:S(2)}) collective-permute-start(bf16[240,128]{1,0:T(8,128)(2,1)S(1)} %newton_schulz.1.refs_1_.refs_3_), channel_id=1, source_target_pairs={{0,18},{1,19},{2,16},{3,17},{16,2},{17,3},{18,0},{19,1},{4,22},{5,... | collective-permute-start | bytes 184328 | tf_op jit(solution)/shard_map/ppermute | solution.py:578
  55.5 0.7 %collective-permute-start.25 = (bf16[240,128]{1,0:T(8,128)(2,1)S(1)}, bf16[240,128]{1,0:T(8,128)(2,1)S(1)}, u32[]{:S(2)}, u32[]{:S(2)}) collective-permute-start(bf16[240,128]{1,0:T(8,128)(2,1)S(1)} %newton_schulz.1.refs_1_.refs_3_), channel_id=1, source_target_pairs={{0,16},{1,17},{2,18},{3,19},{16,0},{17,1},{18,2},{19,3},{4,20},{5,... | collective-permute-start | bytes 184328 | tf_op jit(solution)/shard_map/ppermute | solution.py:578
  56.1 1.6 %collective-permute-start.23 = (bf16[240,128]{1,0:T(8,128)(2,1)S(1)}, bf16[240,128]{1,0:T(8,128)(2,1)S(1)}, u32[]{:S(2)}, u32[]{:S(2)}) collective-permute-start(bf16[240,128]{1,0:T(8,128)(2,1)S(1)} %newton_schulz.1.refs_1_.refs_3_), channel_id=1, source_target_pairs={{0,2},{1,3},{2,0},{3,1},{16,18},{17,19},{18,16},{19,17},{4,6},{5,7... | collective-permute-start | bytes 184328 | tf_op jit(solution)/shard_map/ppermute | solution.py:578
  57.7 1.9 %collective-permute-done.27.refs_6_ = bf16[240,128]{1,0:T(8,128)(2,1)S(1)} collective-permute-done((bf16[240,128]{1,0:T(8,128)(2,1)S(1)}, bf16[240,128]{1,0:T(8,128)(2,1)S(1)}, u32[]{:S(2)}, u32[]{:S(2)}) %collective-permute-start.27) | collective-permute-done | bytes 61472 | tf_op jit(solution)/shard_map/ppermute | solution.py:578
  59.6 1.2 %collective-permute-done.25.refs_5_ = bf16[240,128]{1,0:T(8,128)(2,1)S(1)} collective-permute-done((bf16[240,128]{1,0:T(8,128)(2,1)S(1)}, bf16[240,128]{1,0:T(8,128)(2,1)S(1)}, u32[]{:S(2)}, u32[]{:S(2)}) %collective-permute-start.25) | collective-permute-done | bytes 61472 | tf_op jit(solution)/shard_map/ppermute | solution.py:578
  60.8 0.0 collective-permute-start.26
  60.8 0.5 collective-permute-start.24
  61.3 1.8 %update_weight.2 = (f32[8,192,192]{2,1,0:T(8,128)}, f32[8,192,192]{2,1,0:T(8,128)}) custom-call(f32[8,192,192]{2,1,0:T(8,128)S(1)} %get-tuple-element.71.refs_5_.refs_0_, f32[8,192]{1,0:T(8,128)S(1)} %get-tuple-element.72.refs_1_, f32[4,192,192]{2,1,0:T(8,128)S(1)} %get-tuple-element.88.refs_2_, bf16[240,128]{1,0:T(8,128)(2,1)S(1)} %newton_schulz.1.refs_1_.refs_3_, ...), custom_call_target="tpu_custom_call" | custom-call | tf_op jit(solution)/shard_map/update_weight/pallas_call | solution.py:51
  63.1 1.3 %update_weight.3 = (f32[8,192,192]{2,1,0:T(8,128)}, f32[8,192,192]{2,1,0:T(8,128)}) custom-call(f32[8,192,192]{2,1,0:T(8,128)S(1)} %get-tuple-element.71.refs_5_.refs_0_, f32[8,192]{1,0:T(8,128)S(1)} %get-tuple-element.72.refs_1_, f32[4,192,192]{2,1,0:T(8,128)S(1)} %collective-permute-done.21.refs_7_.refs_2_, ...), custom_call_target="tpu_custom_call", output_to_operand_aliasing={{0}: (7, {}), {1}: (8, {})} | custom-call | tf_op jit(solution)/shard_map/update_weight/pallas_call | solution.py:51
  (32 shorter events, 0.1 us)
Async XLA Ops:
  0.6 0.7 %copy-start.5 = (s32[32,1]{0,1:T(1,128)S(1)}, s32[32,1]{0,1:T(1,128)}, u32[]{:S(2)}) copy-start(s32[32,1]{0,1:T(1,128)} %param.7) | copy-start | bytes 388
  1.3 0.7 %copy-start.7 = (f32[1,32]{1,0:T(1,128)S(1)}, f32[1,32]{1,0:T(1,128)}, u32[]{:S(2)}) copy-start(f32[1,32]{1,0:T(1,128)} %refs_2_.4) | copy-start | bytes 388
  1.9 2.8 %copy-start = (bf16[1,1536,8,192]{1,3,2,0:T(8,128)(2,1)S(1)}, bf16[1,1536,8,192]{1,3,2,0:T(8,128)(2,1)}, u32[]{:S(2)}) copy-start(bf16[1,1536,8,192]{1,3,2,0:T(8,128)(2,1)} %param.6) | copy-start | bytes 14155780
  4.3 2.3 %collective-permute-start = (bf16[1,192,1536]{2,1,0:T(8,128)(2,1)S(1)}, bf16[1,192,1536]{2,1,0:T(8,128)(2,1)S(1)}, u32[]{:S(2)}, u32[]{:S(2)}) collective-permute-start(bf16[1,192,1536]{2,1,0:T(8,128)(2,1)S(1)} %get-tuple-element.50), channel_id=1, source_target_pairs={{0,1},{1,0},{2,3},{3,2},{16,17},{17,16},{18,19},{19,18},{4,5},{5,4... | collective-permute-start | bytes 1769480 | tf_op jit(solution)/shard_map/ppermute | solution.py:578
  6.5 5.3 %copy-start.6 = (s32[32,1]{0,1:T(1,128)S(1)}, s32[32,1]{0,1:T(1,128)}, u32[]{:S(2)}) copy-start(s32[32,1]{0,1:T(1,128)} %param.7) | copy-start | bytes 388
  6.9 8.1 %collective-permute-start.1 = (bf16[3,192,1536]{2,1,0:T(8,128)(2,1)S(1)}, bf16[3,192,1536]{2,1,0:T(8,128)(2,1)S(1)}, u32[]{:S(2)}, u32[]{:S(2)}) collective-permute-start(bf16[3,192,1536]{2,1,0:T(8,128)(2,1)S(1)} %get-tuple-element.54), channel_id=1, source_target_pairs={{0,1},{1,0},{2,3},{3,2},{16,17},{17,16},{18,19},{19,18},{4,5},{5,4... | collective-permute-start | bytes 5308424 | tf_op jit(solution)/shard_map/ppermute | solution.py:578
  7.3 6.1 %collective-permute-start.2 = (f32[4,192,256]{2,1,0:T(8,128)S(1)}, f32[4,192,256]{2,1,0:T(8,128)S(1)}, u32[]{:S(2)}, u32[]{:S(2)}) collective-permute-start(f32[4,192,256]{2,1,0:T(8,128)S(1)} %get-tuple-element.55), channel_id=1, source_target_pairs={{0,1},{1,0},{2,3},{3,2},{16,17},{17,16},{18,19},{19,18},{4,5},{5,4... | collective-permute-start | bytes 2359304 | tf_op jit(solution)/shard_map/ppermute | solution.py:578
  7.4 7.5 %collective-permute-start.3 = (s16[192,384]{1,0:T(8,128)(2,1)S(1)}, s16[192,384]{1,0:T(8,128)(2,1)S(1)}, u32[]{:S(2)}, u32[]{:S(2)}) collective-permute-start(s16[192,384]{1,0:T(8,128)(2,1)S(1)} %get-tuple-element.52.refs_2_), channel_id=1, source_target_pairs={{0,2},{1,3},{2,0},{3,1},{16,18},{17,19},{18,16},{19,17},{4,6},{5,7... | collective-permute-start | bytes 442376 | tf_op jit(solution)/shard_map/ppermute | solution.py:578
  10.3 8.6 %collective-permute-start.10 = (s16[192,384]{1,0:T(8,128)(2,1)S(1)}, s16[192,384]{1,0:T(8,128)(2,1)S(1)}, u32[]{:S(2)}, u32[]{:S(2)}) collective-permute-start(s16[192,384]{1,0:T(8,128)(2,1)S(1)} %get-tuple-element.68), channel_id=1, source_target_pairs={{0,16},{1,17},{2,18},{3,19},{16,0},{17,1},{18,2},{19,3},{4,20},{5,... | collective-permute-start | bytes 442376 | tf_op jit(solution)/shard_map/ppermute | solution.py:578
  11.8 1.6 %copy-start.1 = (f32[8,192,192]{2,1,0:T(8,128)S(1)}, f32[8,192,192]{2,1,0:T(8,128)}, u32[]{:S(2)}) copy-start(f32[8,192,192]{2,1,0:T(8,128)} %refs_0_.1) | copy-start | bytes 3538948
  11.8 1.6 %copy-start.8 = (f32[1,32]{1,0:T(1,128)S(1)}, f32[1,32]{1,0:T(1,128)}, u32[]{:S(2)}) copy-start(f32[1,32]{1,0:T(1,128)} %refs_2_.4) | copy-start | bytes 388
  11.8 7.7 %collective-permute-start.11 = (s16[192,384]{1,0:T(8,128)(2,1)S(1)}, s16[192,384]{1,0:T(8,128)(2,1)S(1)}, u32[]{:S(2)}, u32[]{:S(2)}) collective-permute-start(s16[192,384]{1,0:T(8,128)(2,1)S(1)} %get-tuple-element.69), channel_id=1, source_target_pairs={{0,18},{1,19},{2,16},{3,17},{16,2},{17,3},{18,0},{19,1},{4,22},{5,... | collective-permute-start | bytes 442376 | tf_op jit(solution)/shard_map/ppermute | solution.py:578
  15.2 9.8 %collective-permute-start.4 = (s16[192,384]{1,0:T(8,128)(2,1)S(1)}, s16[192,384]{1,0:T(8,128)(2,1)S(1)}, u32[]{:S(2)}, u32[]{:S(2)}) collective-permute-start(s16[192,384]{1,0:T(8,128)(2,1)S(1)} %get-tuple-element.59), channel_id=1, source_target_pairs={{0,2},{1,3},{2,0},{3,1},{16,18},{17,19},{18,16},{19,17},{4,6},{5,7... | collective-permute-start | bytes 442376 | tf_op jit(solution)/shard_map/ppermute | solution.py:578
  17.3 7.6 %collective-permute-start.5 = (s16[192,384]{1,0:T(8,128)(2,1)S(1)}, s16[192,384]{1,0:T(8,128)(2,1)S(1)}, u32[]{:S(2)}, u32[]{:S(2)}) collective-permute-start(s16[192,384]{1,0:T(8,128)(2,1)S(1)} %get-tuple-element.60), channel_id=1, source_target_pairs={{0,16},{1,17},{2,18},{3,19},{16,0},{17,1},{18,2},{19,3},{4,20},{5,... | collective-permute-start | bytes 442376 | tf_op jit(solution)/shard_map/ppermute | solution.py:578
  19.8 9.1 %collective-permute-start.12 = (s16[192,384]{1,0:T(8,128)(2,1)S(1)}, s16[192,384]{1,0:T(8,128)(2,1)S(1)}, u32[]{:S(2)}, u32[]{:S(2)}) collective-permute-start(s16[192,384]{1,0:T(8,128)(2,1)S(1)} %plane_sum.4), channel_id=1, source_target_pairs={{0,12},{4,8},{8,4},{12,0},{1,13},{5,9},{9,5},{13,1},{2,14},{6,10},... | collective-permute-start | bytes 442376 | tf_op jit(solution)/shard_map/ppermute | solution.py:616
  23.4 7.7 %collective-permute-start.9 = (s16[192,384]{1,0:T(8,128)(2,1)S(1)}, s16[192,384]{1,0:T(8,128)(2,1)S(1)}, u32[]{:S(2)}, u32[]{:S(2)}) collective-permute-start(s16[192,384]{1,0:T(8,128)(2,1)S(1)} %get-tuple-element.66), channel_id=1, source_target_pairs={{0,18},{1,19},{2,16},{3,17},{16,2},{17,3},{18,0},{19,1},{4,22},{5,... | collective-permute-start | bytes 442376 | tf_op jit(solution)/shard_map/ppermute | solution.py:578
  25.3 7.7 %collective-permute-start.6 = (s16[192,384]{1,0:T(8,128)(2,1)S(1)}, s16[192,384]{1,0:T(8,128)(2,1)S(1)}, u32[]{:S(2)}, u32[]{:S(2)}) collective-permute-start(s16[192,384]{1,0:T(8,128)(2,1)S(1)} %get-tuple-element.62), channel_id=1, source_target_pairs={{0,2},{1,3},{2,0},{3,1},{16,18},{17,19},{18,16},{19,17},{4,6},{5,7... | collective-permute-start | bytes 442376 | tf_op jit(solution)/shard_map/ppermute | solution.py:578
  27.0 6.3 %collective-permute-start.7 = (s16[192,384]{1,0:T(8,128)(2,1)S(1)}, s16[192,384]{1,0:T(8,128)(2,1)S(1)}, u32[]{:S(2)}, u32[]{:S(2)}) collective-permute-start(s16[192,384]{1,0:T(8,128)(2,1)S(1)} %get-tuple-element.63), channel_id=1, source_target_pairs={{0,16},{1,17},{2,18},{3,19},{16,0},{17,1},{18,2},{19,3},{4,20},{5,... | collective-permute-start | bytes 442376 | tf_op jit(solution)/shard_map/ppermute | solution.py:578
  27.3 9.8 %collective-permute-start.8 = (s16[192,384]{1,0:T(8,128)(2,1)S(1)}, s16[192,384]{1,0:T(8,128)(2,1)S(1)}, u32[]{:S(2)}, u32[]{:S(2)}) collective-permute-start(s16[192,384]{1,0:T(8,128)(2,1)S(1)} %get-tuple-element.64), channel_id=1, source_target_pairs={{0,18},{1,19},{2,16},{3,17},{16,2},{17,3},{18,0},{19,1},{4,22},{5,... | collective-permute-start | bytes 442376 | tf_op jit(solution)/shard_map/ppermute | solution.py:578
  31.4 6.8 %collective-permute-start.13 = (s16[192,384]{1,0:T(8,128)(2,1)S(1)}, s16[192,384]{1,0:T(8,128)(2,1)S(1)}, u32[]{:S(2)}, u32[]{:S(2)}) collective-permute-start(s16[192,384]{1,0:T(8,128)(2,1)S(1)} %plane_sum.5), channel_id=1, source_target_pairs={{0,8},{4,12},{8,0},{12,4},{1,9},{5,13},{9,1},{13,5},{2,10},{6,14},... | collective-permute-start | bytes 442376 | tf_op jit(solution)/shard_map/ppermute | solution.py:616
  33.3 5.2 %copy-start.4 = (f32[8,64,128]{2,1,0:T(8,128)S(1)}, f32[8,64,128]{2,1,0:T(8,128)}, u32[]{:S(2)}) copy-start(f32[8,64,128]{2,1,0:T(8,128)} %refs_1_.1) | copy-start | bytes 786436
  33.3 6.5 %copy-start.2 = (f32[8,192,192]{2,1,0:T(8,128)S(1)}, f32[8,192,192]{2,1,0:T(8,128)}, u32[]{:S(2)}) copy-start(f32[8,192,192]{2,1,0:T(8,128)} %refs_2_.5) | copy-start | bytes 3538948
  33.6 8.0 %collective-permute-start.14 = (s16[192,384]{1,0:T(8,128)(2,1)S(1)}, s16[192,384]{1,0:T(8,128)(2,1)S(1)}, u32[]{:S(2)}, u32[]{:S(2)}) collective-permute-start(s16[192,384]{1,0:T(8,128)(2,1)S(1)} %get-tuple-element.75), channel_id=1, source_target_pairs={{0,2},{1,3},{2,0},{3,1},{16,18},{17,19},{18,16},{19,17},{4,6},{5,7... | collective-permute-start | bytes 442376 | tf_op jit(solution)/shard_map/ppermute | solution.py:578
  35.0 7.7 %collective-permute-start.15 = (s16[192,384]{1,0:T(8,128)(2,1)S(1)}, s16[192,384]{1,0:T(8,128)(2,1)S(1)}, u32[]{:S(2)}, u32[]{:S(2)}) collective-permute-start(s16[192,384]{1,0:T(8,128)(2,1)S(1)} %get-tuple-element.76), channel_id=1, source_target_pairs={{0,16},{1,17},{2,18},{3,19},{16,0},{17,1},{18,2},{19,3},{4,20},{5,... | collective-permute-start | bytes 442376 | tf_op jit(solution)/shard_map/ppermute | solution.py:578
  35.8 6.8 %collective-permute-start.16 = (s16[192,384]{1,0:T(8,128)(2,1)S(1)}, s16[192,384]{1,0:T(8,128)(2,1)S(1)}, u32[]{:S(2)}, u32[]{:S(2)}) collective-permute-start(s16[192,384]{1,0:T(8,128)(2,1)S(1)} %get-tuple-element.77), channel_id=1, source_target_pairs={{0,18},{1,19},{2,16},{3,17},{16,2},{17,3},{18,0},{19,1},{4,22},{5,... | collective-permute-start | bytes 442376 | tf_op jit(solution)/shard_map/ppermute | solution.py:578
  38.4 5.2 %collective-permute-start.17 = (s16[192,384]{1,0:T(8,128)(2,1)S(1)}, s16[192,384]{1,0:T(8,128)(2,1)S(1)}, u32[]{:S(2)}, u32[]{:S(2)}) collective-permute-start(s16[192,384]{1,0:T(8,128)(2,1)S(1)} %get-tuple-element.78), channel_id=1, source_target_pairs={{0,4},{4,0},{8,12},{12,8},{1,5},{5,1},{9,13},{13,9},{2,6},{6,2},{1... | collective-permute-start | bytes 442376 | tf_op jit(solution)/shard_map/ppermute | solution.py:616
  39.8 3.8 %copy-start.3 = (f32[8,64,128]{2,1,0:T(8,128)S(1)}, f32[8,64,128]{2,1,0:T(8,128)}, u32[]{:S(2)}) copy-start(f32[8,64,128]{2,1,0:T(8,128)} %scale_keys.1.refs_6_) | copy-start | bytes 786436
  44.9 5.2 %collective-permute-start.18 = (s16[224,128]{1,0:T(8,128)(2,1)S(1)}, s16[224,128]{1,0:T(8,128)(2,1)S(1)}, u32[]{:S(2)}, u32[]{:S(2)}) collective-permute-start(s16[224,128]{1,0:T(8,128)(2,1)S(1)} %get-tuple-element.84), channel_id=1, source_target_pairs={{0,18},{1,19},{2,16},{3,17},{16,2},{17,3},{18,0},{19,1},{4,22},{5,... | collective-permute-start | bytes 172040 | tf_op jit(solution)/shard_map/ppermute | solution.py:578
  46.4 4.3 %collective-permute-start.19 = (s16[224,128]{1,0:T(8,128)(2,1)S(1)}, s16[224,128]{1,0:T(8,128)(2,1)S(1)}, u32[]{:S(2)}, u32[]{:S(2)}) collective-permute-start(s16[224,128]{1,0:T(8,128)(2,1)S(1)} %get-tuple-element.85), channel_id=1, source_target_pairs={{0,16},{1,17},{2,18},{3,19},{16,0},{17,1},{18,2},{19,3},{4,20},{5,... | collective-permute-start | bytes 172040 | tf_op jit(solution)/shard_map/ppermute | solution.py:578
  48.0 4.2 %collective-permute-start.20 = (s16[224,128]{1,0:T(8,128)(2,1)S(1)}, s16[224,128]{1,0:T(8,128)(2,1)S(1)}, u32[]{:S(2)}, u32[]{:S(2)}) collective-permute-start(s16[224,128]{1,0:T(8,128)(2,1)S(1)} %get-tuple-element.86), channel_id=1, source_target_pairs={{0,2},{1,3},{2,0},{3,1},{16,18},{17,19},{18,16},{19,17},{4,6},{5,7... | collective-permute-start | bytes 172040 | tf_op jit(solution)/shard_map/ppermute | solution.py:578
  54.1 7.2 %collective-permute-start.21 = (f32[4,192,192]{2,1,0:T(8,128)S(1)}, f32[4,192,192]{2,1,0:T(8,128)S(1)}, u32[]{:S(2)}, u32[]{:S(2)}) collective-permute-start(f32[4,192,192]{2,1,0:T(8,128)S(1)} %get-tuple-element.87), channel_id=1, source_target_pairs={{0,1},{1,0},{2,3},{3,2},{16,17},{17,16},{18,19},{19,18},{4,5},{5,4... | collective-permute-start | bytes 1769480 | tf_op jit(solution)/shard_map/ppermute | solution.py:578
  54.1 5.4 %collective-permute-start.27 = (bf16[240,128]{1,0:T(8,128)(2,1)S(1)}, bf16[240,128]{1,0:T(8,128)(2,1)S(1)}, u32[]{:S(2)}, u32[]{:S(2)}) collective-permute-start(bf16[240,128]{1,0:T(8,128)(2,1)S(1)} %newton_schulz.1.refs_1_.refs_3_), channel_id=1, source_target_pairs={{0,18},{1,19},{2,16},{3,17},{16,2},{17,3},{18,0},{19,1},{4,22},{5,... | collective-permute-start | bytes 184328 | tf_op jit(solution)/shard_map/ppermute | solution.py:578
  55.5 5.3 %collective-permute-start.25 = (bf16[240,128]{1,0:T(8,128)(2,1)S(1)}, bf16[240,128]{1,0:T(8,128)(2,1)S(1)}, u32[]{:S(2)}, u32[]{:S(2)}) collective-permute-start(bf16[240,128]{1,0:T(8,128)(2,1)S(1)} %newton_schulz.1.refs_1_.refs_3_), channel_id=1, source_target_pairs={{0,16},{1,17},{2,18},{3,19},{16,0},{17,1},{18,2},{19,3},{4,20},{5,... | collective-permute-start | bytes 184328 | tf_op jit(solution)/shard_map/ppermute | solution.py:578
  56.1 4.7 %collective-permute-start.23 = (bf16[240,128]{1,0:T(8,128)(2,1)S(1)}, bf16[240,128]{1,0:T(8,128)(2,1)S(1)}, u32[]{:S(2)}, u32[]{:S(2)}) collective-permute-start(bf16[240,128]{1,0:T(8,128)(2,1)S(1)} %newton_schulz.1.refs_1_.refs_3_), channel_id=1, source_target_pairs={{0,2},{1,3},{2,0},{3,1},{16,18},{17,19},{18,16},{19,17},{4,6},{5,7... | collective-permute-start | bytes 184328 | tf_op jit(solution)/shard_map/ppermute | solution.py:578
  57.7 5.4 %collective-permute-start.22 = (bf16[240,128]{1,0:T(8,128)(2,1)S(1)}, bf16[240,128]{1,0:T(8,128)(2,1)S(1)}, u32[]{:S(2)}, u32[]{:S(2)}) collective-permute-start(bf16[240,128]{1,0:T(8,128)(2,1)S(1)} %newton_schulz.1.refs_1_.refs_3_), channel_id=1, source_target_pairs={{0,1},{1,0},{2,3},{3,2},{16,17},{17,16},{18,19},{19,18},{4,5},{5,4... | collective-permute-start | bytes 184328 | tf_op jit(solution)/shard_map/ppermute | solution.py:578
  59.6 3.5 %collective-permute-start.28 = (bf16[240,128]{1,0:T(8,128)(2,1)S(1)}, bf16[240,128]{1,0:T(8,128)(2,1)S(1)}, u32[]{:S(2)}, u32[]{:S(2)}) collective-permute-start(bf16[240,128]{1,0:T(8,128)(2,1)S(1)} %collective-permute-done.27.refs_6_), channel_id=1, source_target_pairs={{0,1},{1,0},{2,3},{3,2},{16,17},{17,16},{18,19},{19,18},{4,5},{5,4... | collective-permute-start | bytes 184328 | tf_op jit(solution)/shard_map/ppermute | solution.py:578
  60.8 2.3 %collective-permute-start.26 = (bf16[240,128]{1,0:T(8,128)(2,1)S(1)}, bf16[240,128]{1,0:T(8,128)(2,1)S(1)}, u32[]{:S(2)}, u32[]{:S(2)}) collective-permute-start(bf16[240,128]{1,0:T(8,128)(2,1)S(1)} %collective-permute-done.25.refs_5_), channel_id=1, source_target_pairs={{0,1},{1,0},{2,3},{3,2},{16,17},{17,16},{18,19},{19,18},{4,5},{5,4... | collective-permute-start | bytes 184328 | tf_op jit(solution)/shard_map/ppermute | solution.py:578
  60.8 2.3 %collective-permute-start.24 = (bf16[240,128]{1,0:T(8,128)(2,1)S(1)}, bf16[240,128]{1,0:T(8,128)(2,1)S(1)}, u32[]{:S(2)}, u32[]{:S(2)}) collective-permute-start(bf16[240,128]{1,0:T(8,128)(2,1)S(1)} %collective-permute-done.23.refs_4_), channel_id=1, source_target_pairs={{0,1},{1,0},{2,3},{3,2},{16,17},{17,16},{18,19},{19,18},{4,5},{5,4... | collective-permute-start | bytes 184328 | tf_op jit(solution)/shard_map/ppermute | solution.py:578
